TPU v7x, 256 devices: a whole 4x4x8 slice. The times are simulated.
256 devices in a mesh: freq: 16 (over y, x), node: 16 (over z, core).
Axes of the slice: x: 4, y: 4, z: 8, core: 2. Of those that a mesh axis runs over, the one named last changes fastest.
Arguments:
- harmonics: float32 [64, 2, 3, 32768], P('freq', None, None, 'node'), may hold values from -6 to 6
- forcing: float32 [64, 2, 3, 32768], P('freq', None, None, 'node'), may hold values from -6 to 6
- depths: float32 [32768], P('node'), may hold values from 1 to 8
- damping: float32 [32768], P('node'), may hold values from 0.2 to 2
- weights: float32 [4, 32768], P(None, 'node'), may hold values from 0.1 to 1
- couple_east: float32 [4, 32768], P(None, 'node'), may hold values from -0.3 to 0.3
- couple_north: float32 [4, 32768], P(None, 'node'), may hold values from -0.3 to 0.3
- connections: int32 [256, 4], P('node'), may hold values from 0 to 255, as said below
- counts: int32 [2, 64], replicated, may hold values from 1 to 5, as said below
- harmonic_of_slot: int32 [64], replicated, may hold values from 0 to 63, each once
Outputs:
- solution: float32 [64, 2, 3, 32768], P('freq', None, None, 'node')
- residual: float32 [64, 2, 3, 32768], P('freq', None, None, 'node')
Inputs may be any that keep to these rules, and one draw needn't show every extreme that they name: `connections`: each block's neighbour blocks lie among the 16 blocks of its own node index and the one block just before and just after them; links 0 and 1 are the previous and next block (the next and previous at the ends). `counts`: in every sweep some slot takes 5 iterations.
All inputs are finite; a program needn't handle non-finite values.
Results may differ from a plain program's by a relative error of at most 0.0003.
Values sent between devices are 32-bit elements; how exact they have to be, the bound alone decides.
No kernel may reach another device: no remote copies, remote signals or barrier semaphores. Data moves between devices by JAX's collectives and lax.ppermute only.
A program may use at most 64 MiB of HBM per device.

v0:
```python
import math

import jax
import jax.numpy as jnp
from jax import lax
from jax.sharding import PartitionSpec as P

SAMPLES = 128
LMAX = 5
SWEEPS = 2


FRICTION = 2.0
CORIOLIS = 0.5
ETA_DAMP = 0.2
OMEGA_STEP = 0.05
SPEED_FLOOR = 0.01
TOP_HARMONIC = lax.Precision.HIGHEST


def extended_2(cells, sides, width):
    for axis, dim in sides:
        count = lax.axis_size(axis)
        ends = count - 1
        head = lax.slice_in_dim(cells, 0, width, axis=dim)
        tail = lax.slice_in_dim(cells, cells.shape[dim] - width, cells.shape[dim], axis=dim)
        cells = jnp.concatenate(
            [
                lax.ppermute(tail, axis, [(i, (i + 1) % count) for i in range(ends)]),
                cells,
                lax.ppermute(head, axis, [((i + 1) % count, i) for i in range(ends)]),
            ],
            axis=dim,
        )
    return cells


def harmonic_tables(harmonic_of_slot, sample_total):
    sample_moments = jnp.arange(sample_total, dtype=jnp.int32)
    pointwise_products = sample_moments[:, None] * harmonic_of_slot[None, :] % sample_total
    angles = pointwise_products.astype(jnp.float32) * (2.0 * math.pi / sample_total)
    cosine = jnp.cos(angles)
    sines = jnp.sin(angles)
    slots = harmonic_of_slot.shape[0]
    synthesis = jnp.stack([cosine, -sines], axis=2).reshape(sample_total, 2 * slots)
    weighting = jnp.where(harmonic_of_slot == 0, 1.0, 2.0).astype(jnp.float32) / sample_total
    analysis = (
        jnp.stack([cosine * weighting, -sines * weighting], axis=2)
        .reshape(sample_total, 2 * slots)
        .T
    )
    return (synthesis, analysis)


def friction_terms(fields, depth_cols, synthesis, analysis):
    slots = fields.shape[0]
    columns = fields.shape[3]
    fields_at_moments = jnp.dot(
        synthesis, fields.reshape(2 * slots, 3 * columns), precision=TOP_HARMONIC
    )
    fields_at_moments = fields_at_moments.reshape(-1, 3, columns)
    elevation = fields_at_moments[:, 0]
    eastward = fields_at_moments[:, 1]
    northward = fields_at_moments[:, 2]
    column_depth = depth_cols + 0.5 * jnp.tanh(elevation)
    magnitude = jnp.sqrt(eastward * eastward + northward * northward + SPEED_FLOOR)
    factor = FRICTION * magnitude / column_depth
    stacked = jnp.stack([factor * eastward, factor * northward], axis=1).reshape(-1, 2 * columns)
    return jnp.dot(analysis, stacked, precision=TOP_HARMONIC).reshape(slots, 2, 2, columns)


def assemble(fields, beside_of, angular, damping, weights, couple_east, couple_north):
    spread = jnp.zeros_like(fields)
    inflow = jnp.zeros_like(fields[:, :, 0])
    grad_east = jnp.zeros_like(inflow)
    northern_gradient = jnp.zeros_like(inflow)
    for link in range(weights.shape[0]):
        change = beside_of(link) - fields
        spread = spread - weights[link] * change
        inflow = inflow + couple_east[link] * change[:, :, 1] + couple_north[link] * change[:, :, 2]
        grad_east = grad_east + couple_east[link] * change[:, :, 0]
        northern_gradient = northern_gradient + couple_north[link] * change[:, :, 0]
    damping_rows = jnp.stack([ETA_DAMP * jnp.ones_like(damping), damping, damping])
    coupled = jnp.stack(
        [
            inflow,
            grad_east - CORIOLIS * fields[:, :, 2],
            northern_gradient + CORIOLIS * fields[:, :, 1],
        ],
        axis=2,
    )
    rotation = angular[:, None, None, None] * jnp.stack([-fields[:, 1], fields[:, 0]], axis=1)
    return damping_rows * fields + spread + coupled + rotation


def complex_scale(alpha_real, alpha_imag, values):
    scale_real = alpha_real[:, None, None]
    scale_imag = alpha_imag[:, None, None]
    real_part = scale_real * values[:, 0] - scale_imag * values[:, 1]
    imag_part = scale_real * values[:, 1] + scale_imag * values[:, 0]
    return jnp.stack([real_part, imag_part], axis=1)


def body(
    harmonics,
    forcing,
    depths,
    damping,
    weights,
    couple_east,
    couple_north,
    connections,
    counts,
    harmonic_of_slot,
):
    freq_here = harmonics.shape[0]
    nodes_here = harmonics.shape[3]
    blocks_here = nodes_here // 128
    total_slots = harmonic_of_slot.shape[0]
    ranks_freq = lax.axis_size("freq")
    freq_rank = lax.axis_index("freq")
    node_rank = lax.axis_index("node")
    synthesis, analysis = harmonic_tables(harmonic_of_slot, SAMPLES)
    slot_ids = lax.dynamic_slice_in_dim(harmonic_of_slot, freq_rank * freq_here, freq_here)
    angular = OMEGA_STEP * slot_ids.astype(jnp.float32)
    slot_counts = lax.dynamic_slice_in_dim(counts, freq_rank * freq_here, freq_here, axis=1)
    local_links = connections - node_rank * blocks_here + 1

    def operate(fields):
        blocked = fields.reshape(freq_here, 2, 3, blocks_here, 128)
        extended = extended_2(blocked, (("node", 3),), 1)

        def beside_of(link):
            return jnp.take(extended, local_links[:, link], axis=3).reshape(fields.shape)

        return assemble(fields, beside_of, angular, damping, weights, couple_east, couple_north)

    fields = harmonics
    residual = forcing
    for sweep_index in range(SWEEPS):
        stacked = fields.reshape(freq_here, 6, nodes_here)
        columns = nodes_here // ranks_freq
        received = lax.all_to_all(stacked, "freq", split_axis=2, concat_axis=0, tiled=True)
        mine = lax.dynamic_slice_in_dim(depths, freq_rank * columns, columns)
        terms = friction_terms(
            received.reshape(total_slots, 2, 3, columns), mine, synthesis, analysis
        )
        back = lax.all_to_all(
            terms.reshape(total_slots, 4, columns), "freq", split_axis=0, concat_axis=2, tiled=True
        )
        friction = back.reshape(freq_here, 2, 2, nodes_here)
        friction = jnp.concatenate([jnp.zeros_like(friction[:, :, :1]), friction], axis=2)
        residual = forcing - friction - operate(fields)
        for inner in range(LMAX):
            image = operate(residual)
            upper_real = jnp.sum(
                image[:, 0] * residual[:, 0] + image[:, 1] * residual[:, 1], axis=(1, 2)
            )
            upper_imag = jnp.sum(
                image[:, 0] * residual[:, 1] - image[:, 1] * residual[:, 0], axis=(1, 2)
            )
            lower_part = jnp.sum(image[:, 0] * image[:, 0] + image[:, 1] * image[:, 1], axis=(1, 2))
            upper_real, upper_imag, lower_part = lax.psum(
                (upper_real, upper_imag, lower_part), "node"
            )
            lower = lower_part + 1e-06
            active = (inner < slot_counts[sweep_index]).astype(jnp.float32)
            alpha_real = active * upper_real / lower
            alpha_imag = active * upper_imag / lower
            fields = fields + complex_scale(alpha_real, alpha_imag, residual)
            residual = residual - complex_scale(alpha_real, alpha_imag, image)
    return (fields, residual)


def solution(mesh):
    return jax.shard_map(
        body,
        mesh=mesh,
        in_specs=(
            P("freq", None, None, "node"),
            P("freq", None, None, "node"),
            P("node"),
            P("node"),
            P(None, "node"),
            P(None, "node"),
            P(None, "node"),
            P("node", None),
            P(),
            P(),
        ),
        out_specs=(P("freq", None, None, "node"), P("freq", None, None, "node")),
        check_vma=False,
    )
```

profile of v0, /device:TPU:128, one launch (start us, length us, event | category | flops | bytes accessed | tf_op | source)
XLA Modules:
  0.0 530.3 jit_solution(14213137788974810566)
XLA Ops:
  0.6 1.1 reshape.564
  1.8 1.9 collective-permute-start
  3.7 4.9 collective-permute-start.1
  19.3 1.3 bitcast_subtract_fusion.47
  20.6 3.1 copy.560
  23.7 7.2 %reshape.1217 = f32[16,1,3072]{2,1,0:T(1,128)} reshape(f32[2048,4,6]{2,1,0:T(4,128)} %bitcast.589) | data formatting | bytes 393216
  30.9 7.0 %all-to-all-start = ((f32[16,1,3072]{2,1,0:T(1,128)}), f32[16,1,3072]{2,1,0:T(1,128)S(1)}, u32[]{:S(2)}, u32[]{:S(2)}) async-start(f32[16,1,3072]{2,1,0:T(1,128)} %reshape.1217), calls=%async_computation | async-start | bytes 393216 | tf_op jit(solution)/shard_map/all_to_all | solution.py:143
  38.1 8.1 %all-to-all-done = f32[16,1,3072]{2,1,0:T(1,128)S(1)} async-done(((f32[16,1,3072]{2,1,0:T(1,128)}), f32[16,1,3072]{2,1,0:T(1,128)S(1)}, u32[]{:S(2)}, u32[]{:S(2)}) %all-to-all-start) | async-done | bytes 196640 | tf_op jit(solution)/shard_map/all_to_all | solution.py:143
  46.8 1.1 reduce.30
  48.0 6.8 %reshape.1218 = f32[2048,4,6]{2,1,0:T(4,128)} reshape(f32[16,3072]{1,0:T(8,128)S(1)} %reduce.30) | data formatting | bytes 393216
  54.8 3.6 copy.737
  60.0 3.5 all-to-all-start.1
  63.6 7.9 %all-to-all-done.1 = f32[64,4,128]{2,1,0:T(4,128)S(1)} async-done(((f32[64,4,128]{2,1,0:T(4,128)}), f32[64,4,128]{2,1,0:T(4,128)S(1)}, u32[]{:S(2)}, u32[]{:S(2)}) %all-to-all-start.1) | async-done | bytes 131104 | tf_op jit(solution)/shard_map/all_to_all | solution.py:148
  72.2 1.9 collective-permute-start.2
  74.1 4.9 collective-permute-start.3
  79.0 1.3 collective-permute-done.3
  84.4 26.5 %all-reduce.11 = (f32[4]{0:T(128)S(1)}, f32[4]{0:T(128)S(1)}, f32[4]{0:T(128)S(1)}) all-reduce(f32[4]{0:T(128)S(1)} %get-tuple-element.32, f32[4]{0:T(128)S(1)} %get-tuple-element.42, f32[4]{0:T(128)S(1)} %get-tuple-element.31), channel_id=1, replica_groups=mesh['freq'=16,'node'=16] {'node'}, use_global_device_ids=true, to_apply=%region_5.7 | all-reduce | flops 12 | bytes 96 | tf_op jit(solution)/shard_map/psum | solution.py:163
  111.2 1.9 collective-permute-start.4
  113.1 5.3 %collective-permute-start.5 = (f32[4,2,3,1,128]{4,0,3,2,1:T(4,128)S(1)}, f32[4,2,3,1,128]{4,0,3,2,1:T(4,128)S(1)}, u32[]{:S(2)}, u32[]{:S(2)}) collective-permute-start(f32[4,2,3,1,128]{4,0,3,2,1:T(4,128)S(1)} %get-tuple-element.226), channel_id=1, source_target_pairs={{1,0},{2,1},{3,2},{4,3},{5,4},{6,5},{7,6},{8,7},{9,8},{10,9},{11,1... | collective-permute-start | bytes 36872 | tf_op jit(solution)/shard_map/ppermute | solution.py:31
  123.4 26.5 %all-reduce.10 = (f32[4]{0:T(128)S(1)}, f32[4]{0:T(128)S(1)}, f32[4]{0:T(128)S(1)}) all-reduce(f32[4]{0:T(128)S(1)} %get-tuple-element.30, f32[4]{0:T(128)S(1)} %get-tuple-element.41, f32[4]{0:T(128)S(1)} %get-tuple-element.29), channel_id=1, replica_groups=mesh['freq'=16,'node'=16] {'node'}, use_global_device_ids=true, to_apply=%region_11.13 | all-reduce | flops 12 | bytes 96 | tf_op jit(solution)/shard_map/psum | solution.py:163
  150.2 1.9 collective-permute-start.6
  152.2 4.9 collective-permute-start.7
  157.1 1.3 collective-permute-done.7
  162.5 26.5 %all-reduce.9 = (f32[4]{0:T(128)S(1)}, f32[4]{0:T(128)S(1)}, f32[4]{0:T(128)S(1)}) all-reduce(f32[4]{0:T(128)S(1)} %get-tuple-element.28, f32[4]{0:T(128)S(1)} %get-tuple-element.40, f32[4]{0:T(128)S(1)} %get-tuple-element.27), channel_id=1, replica_groups=mesh['freq'=16,'node'=16] {'node'}, use_global_device_ids=true, to_apply=%region_17.19 | all-reduce | flops 12 | bytes 96 | tf_op jit(solution)/shard_map/psum | solution.py:163
  189.4 1.9 collective-permute-start.8
  191.3 4.9 collective-permute-start.9
  200.9 1.5 fusion.9
  202.7 26.5 %all-reduce.8 = (f32[4]{0:T(128)S(1)}, f32[4]{0:T(128)S(1)}, f32[4]{0:T(128)S(1)}) all-reduce(f32[4]{0:T(128)S(1)} %get-tuple-element.26, f32[4]{0:T(128)S(1)} %get-tuple-element.39, f32[4]{0:T(128)S(1)} %get-tuple-element.25), channel_id=1, replica_groups=mesh['freq'=16,'node'=16] {'node'}, use_global_device_ids=true, to_apply=%region_23.25 | all-reduce | flops 12 | bytes 96 | tf_op jit(solution)/shard_map/psum | solution.py:163
  229.7 1.9 collective-permute-start.10
  231.6 4.9 collective-permute-start.11
  241.3 1.5 fusion.10
  243.1 26.5 %all-reduce.7 = (f32[4]{0:T(128)S(1)}, f32[4]{0:T(128)S(1)}, f32[4]{0:T(128)S(1)}) all-reduce(f32[4]{0:T(128)S(1)} %get-tuple-element.24, f32[4]{0:T(128)S(1)} %get-tuple-element.38, f32[4]{0:T(128)S(1)} %get-tuple-element.23), channel_id=1, replica_groups=mesh['freq'=16,'node'=16] {'node'}, use_global_device_ids=true, to_apply=%region_29.31 | all-reduce | flops 12 | bytes 96 | tf_op jit(solution)/shard_map/psum | solution.py:163
  270.3 1.9 collective-permute-start.12
  272.2 5.0 collective-permute-start.13
  278.0 3.1 copy.650
  281.1 7.2 %reshape.1219 = f32[16,1,3072]{2,1,0:T(1,128)} reshape(f32[2048,4,6]{2,1,0:T(4,128)} %bitcast.590) | data formatting | bytes 393216
  288.3 4.2 all-to-all-start.2
  297.2 3.6 all-to-all-done.2
  300.8 2.0 reduce.31
  302.8 6.8 %reshape.1220 = f32[2048,4,6]{2,1,0:T(4,128)} reshape(f32[16,3072]{1,0:T(8,128)S(1)} %reduce.31) | data formatting | bytes 393216
  309.6 3.5 copy.784
  314.9 3.5 all-to-all-start.3
  319.4 6.9 %all-to-all-done.3 = f32[64,4,128]{2,1,0:T(4,128)S(1)} async-done(((f32[64,4,128]{2,1,0:T(4,128)}), f32[64,4,128]{2,1,0:T(4,128)S(1)}, u32[]{:S(2)}, u32[]{:S(2)}) %all-to-all-start.3) | async-done | bytes 131104 | tf_op jit(solution)/shard_map/all_to_all | solution.py:148
  326.4 1.8 fusion.12
  328.2 1.9 collective-permute-start.14
  330.2 4.9 collective-permute-start.15
  335.1 1.3 collective-permute-done.15
  340.4 26.5 %all-reduce.6 = (f32[4]{0:T(128)S(1)}, f32[4]{0:T(128)S(1)}, f32[4]{0:T(128)S(1)}) all-reduce(f32[4]{0:T(128)S(1)} %get-tuple-element.22, f32[4]{0:T(128)S(1)} %get-tuple-element.37, f32[4]{0:T(128)S(1)} %get-tuple-element.21), channel_id=1, replica_groups=mesh['freq'=16,'node'=16] {'node'}, use_global_device_ids=true, to_apply=%region_35.37 | all-reduce | flops 12 | bytes 96 | tf_op jit(solution)/shard_map/psum | solution.py:163
  367.9 1.9 collective-permute-start.16
  369.8 5.1 collective-permute-start.17
  374.9 1.1 collective-permute-done.17
  380.1 26.5 %all-reduce.5 = (f32[4]{0:T(128)S(1)}, f32[4]{0:T(128)S(1)}, f32[4]{0:T(128)S(1)}) all-reduce(f32[4]{0:T(128)S(1)} %get-tuple-element.20, f32[4]{0:T(128)S(1)} %get-tuple-element.36, f32[4]{0:T(128)S(1)} %get-tuple-element.19), channel_id=1, replica_groups=mesh['freq'=16,'node'=16] {'node'}, use_global_device_ids=true, to_apply=%region_41.43 | all-reduce | flops 12 | bytes 96 | tf_op jit(solution)/shard_map/psum | solution.py:163
  407.6 1.9 collective-permute-start.18
  409.6 4.9 collective-permute-start.19
  414.5 1.3 collective-permute-done.19
  419.9 26.5 %all-reduce.4 = (f32[4]{0:T(128)S(1)}, f32[4]{0:T(128)S(1)}, f32[4]{0:T(128)S(1)}) all-reduce(f32[4]{0:T(128)S(1)} %get-tuple-element.18, f32[4]{0:T(128)S(1)} %get-tuple-element.35, f32[4]{0:T(128)S(1)} %get-tuple-element.17), channel_id=1, replica_groups=mesh['freq'=16,'node'=16] {'node'}, use_global_device_ids=true, to_apply=%region_47.49 | all-reduce | flops 12 | bytes 96 | tf_op jit(solution)/shard_map/psum | solution.py:163
  447.5 1.9 collective-permute-start.20
  449.4 4.9 collective-permute-start.21
  454.3 1.3 collective-permute-done.21
  459.8 26.5 %all-reduce.3 = (f32[4]{0:T(128)S(1)}, f32[4]{0:T(128)S(1)}, f32[4]{0:T(128)S(1)}) all-reduce(f32[4]{0:T(128)S(1)} %get-tuple-element.16, f32[4]{0:T(128)S(1)} %get-tuple-element.34, f32[4]{0:T(128)S(1)} %get-tuple-element.15), channel_id=1, replica_groups=mesh['freq'=16,'node'=16] {'node'}, use_global_device_ids=true, to_apply=%region_53.55 | all-reduce | flops 12 | bytes 96 | tf_op jit(solution)/shard_map/psum | solution.py:163
  487.5 1.9 collective-permute-start.22
  489.4 4.9 collective-permute-start.23
  500.1 26.5 %all-reduce.2 = (f32[4]{0:T(128)S(1)}, f32[4]{0:T(128)S(1)}, f32[4]{0:T(128)S(1)}) all-reduce(f32[4]{0:T(128)S(1)} %get-tuple-element.14, f32[4]{0:T(128)S(1)} %get-tuple-element.33, f32[4]{0:T(128)S(1)} %get-tuple-element.13), channel_id=1, replica_groups=mesh['freq'=16,'node'=16] {'node'}, use_global_device_ids=true, to_apply=%region_59.61 | all-reduce | flops 12 | bytes 96 | tf_op jit(solution)/shard_map/psum | solution.py:163
  527.7 1.6 fusion.17
  (268 shorter events, 75.4 us)
Async XLA Ops:
  0.6 14.0 %copy-start = (s32[2,64]{1,0:T(2,128)S(1)}, s32[2,64]{1,0:T(2,128)}, u32[]{:S(2)}) copy-start(s32[2,64]{1,0:T(2,128)} %param.20) | copy-start | bytes 1540
  1.8 14.6 %collective-permute-start = (f32[4,2,3,1,128]{4,0,3,2,1:T(4,128)S(1)}, f32[4,2,3,1,128]{4,0,3,2,1:T(4,128)S(1)}, u32[]{:S(2)}, u32[]{:S(2)}) collective-permute-start(f32[4,2,3,1,128]{4,0,3,2,1:T(4,128)S(1)} %copy.1082), channel_id=1, source_target_pairs={{0,1},{1,2},{2,3},{3,4},{4,5},{5,6},{6,7},{7,8},{8,9},{9,10},{10,1... | collective-permute-start | bytes 36872 | tf_op jit(solution)/shard_map/ppermute | solution.py:29
  3.7 12.8 %collective-permute-start.1 = (f32[4,2,3,1,128]{4,0,3,2,1:T(4,128)S(1)}, f32[4,2,3,1,128]{4,0,3,2,1:T(4,128)S(1)}, u32[]{:S(2)}, u32[]{:S(2)}) collective-permute-start(f32[4,2,3,1,128]{4,0,3,2,1:T(4,128)S(1)} %copy.1083), channel_id=1, source_target_pairs={{1,0},{2,1},{3,2},{4,3},{5,4},{6,5},{7,6},{8,7},{9,8},{10,9},{11,1... | collective-permute-start | bytes 36872 | tf_op jit(solution)/shard_map/ppermute | solution.py:31
  15.5 43.1 %copy-start.7 = (f32[128,64,2]{0,2,1:T(2,128)}, f32[128,64,2]{0,2,1:T(2,128)S(1)}, u32[]{:S(2)}) copy-start(f32[128,64,2]{0,2,1:T(2,128)S(1)} %copy.558) | copy-start | bytes 196612
  15.5 43.5 %copy-start.5 = (f32[128,64,2]{0,2,1:T(2,128)}, f32[128,64,2]{0,2,1:T(2,128)S(1)}, u32[]{:S(2)}) copy-start(f32[128,64,2]{0,2,1:T(2,128)S(1)} %copy.557) | copy-start | bytes 196612
  30.9 15.4 %all-to-all-start = ((f32[16,1,3072]{2,1,0:T(1,128)}), f32[16,1,3072]{2,1,0:T(1,128)S(1)}, u32[]{:S(2)}, u32[]{:S(2)}) async-start(f32[16,1,3072]{2,1,0:T(1,128)} %reshape.1217), calls=%async_computation | async-start | bytes 393216 | tf_op jit(solution)/shard_map/all_to_all | solution.py:143
  54.8 16.7 %copy-start.1 = (f32[4,2,3,2048]{3,1,2,0:T(2,128)S(1)}, f32[4,2,3,2048]{3,1,2,0:T(2,128)}, u32[]{:S(2)}) copy-start(f32[4,2,3,2048]{3,1,2,0:T(2,128)} %param.12) | copy-start | bytes 589828
  54.8 16.7 %copy-start.2 = (f32[4,2,3,2048]{3,1,2,0:T(2,128)S(1)}, f32[4,2,3,2048]{3,1,2,0:T(2,128)}, u32[]{:S(2)}) copy-start(f32[4,2,3,2048]{3,1,2,0:T(2,128)} %param.13) | copy-start | bytes 589828
  60.0 11.5 %all-to-all-start.1 = ((f32[64,4,128]{2,1,0:T(4,128)}), f32[64,4,128]{2,1,0:T(4,128)S(1)}, u32[]{:S(2)}, u32[]{:S(2)}) async-start(f32[64,4,128]{2,1,0:T(4,128)} %reshape_reshape.13), calls=%async_computation.1 | async-start | bytes 262144 | tf_op jit(solution)/shard_map/all_to_all | solution.py:148
  72.2 6.8 %collective-permute-start.2 = (f32[4,2,3,1,128]{4,0,3,2,1:T(4,128)S(1)}, f32[4,2,3,1,128]{4,0,3,2,1:T(4,128)S(1)}, u32[]{:S(2)}, u32[]{:S(2)}) collective-permute-start(f32[4,2,3,1,128]{4,0,3,2,1:T(4,128)S(1)} %get-tuple-element.233), channel_id=1, source_target_pairs={{0,1},{1,2},{2,3},{3,4},{4,5},{5,6},{6,7},{7,8},{8,9},{9,10},{10,1... | collective-permute-start | bytes 36872 | tf_op jit(solution)/shard_map/ppermute | solution.py:29
  74.1 6.2 %collective-permute-start.3 = (f32[4,2,3,1,128]{4,0,3,2,1:T(4,128)S(1)}, f32[4,2,3,1,128]{4,0,3,2,1:T(4,128)S(1)}, u32[]{:S(2)}, u32[]{:S(2)}) collective-permute-start(f32[4,2,3,1,128]{4,0,3,2,1:T(4,128)S(1)} %get-tuple-element.234), channel_id=1, source_target_pairs={{1,0},{2,1},{3,2},{4,3},{5,4},{6,5},{7,6},{8,7},{9,8},{10,9},{11,1... | collective-permute-start | bytes 36872 | tf_op jit(solution)/shard_map/ppermute | solution.py:31
  111.2 7.3 %collective-permute-start.4 = (f32[4,2,3,1,128]{4,0,3,2,1:T(4,128)S(1)}, f32[4,2,3,1,128]{4,0,3,2,1:T(4,128)S(1)}, u32[]{:S(2)}, u32[]{:S(2)}) collective-permute-start(f32[4,2,3,1,128]{4,0,3,2,1:T(4,128)S(1)} %get-tuple-element.225), channel_id=1, source_target_pairs={{0,1},{1,2},{2,3},{3,4},{4,5},{5,6},{6,7},{7,8},{8,9},{9,10},{10,1... | collective-permute-start | bytes 36872 | tf_op jit(solution)/shard_map/ppermute | solution.py:29
  113.1 6.2 %collective-permute-start.5 = (f32[4,2,3,1,128]{4,0,3,2,1:T(4,128)S(1)}, f32[4,2,3,1,128]{4,0,3,2,1:T(4,128)S(1)}, u32[]{:S(2)}, u32[]{:S(2)}) collective-permute-start(f32[4,2,3,1,128]{4,0,3,2,1:T(4,128)S(1)} %get-tuple-element.226), channel_id=1, source_target_pairs={{1,0},{2,1},{3,2},{4,3},{5,4},{6,5},{7,6},{8,7},{9,8},{10,9},{11,1... | collective-permute-start | bytes 36872 | tf_op jit(solution)/shard_map/ppermute | solution.py:31
  150.2 6.8 %collective-permute-start.6 = (f32[4,2,3,1,128]{4,0,3,2,1:T(4,128)S(1)}, f32[4,2,3,1,128]{4,0,3,2,1:T(4,128)S(1)}, u32[]{:S(2)}, u32[]{:S(2)}) collective-permute-start(f32[4,2,3,1,128]{4,0,3,2,1:T(4,128)S(1)} %get-tuple-element.217), channel_id=1, source_target_pairs={{0,1},{1,2},{2,3},{3,4},{4,5},{5,6},{6,7},{7,8},{8,9},{9,10},{10,1... | collective-permute-start | bytes 36872 | tf_op jit(solution)/shard_map/ppermute | solution.py:29
  152.2 6.2 %collective-permute-start.7 = (f32[4,2,3,1,128]{4,0,3,2,1:T(4,128)S(1)}, f32[4,2,3,1,128]{4,0,3,2,1:T(4,128)S(1)}, u32[]{:S(2)}, u32[]{:S(2)}) collective-permute-start(f32[4,2,3,1,128]{4,0,3,2,1:T(4,128)S(1)} %get-tuple-element.218), channel_id=1, source_target_pairs={{1,0},{2,1},{3,2},{4,3},{5,4},{6,5},{7,6},{8,7},{9,8},{10,9},{11,1... | collective-permute-start | bytes 36872 | tf_op jit(solution)/shard_map/ppermute | solution.py:31
  189.4 7.5 %collective-permute-start.8 = (f32[4,2,3,1,128]{4,0,3,2,1:T(4,128)S(1)}, f32[4,2,3,1,128]{4,0,3,2,1:T(4,128)S(1)}, u32[]{:S(2)}, u32[]{:S(2)}) collective-permute-start(f32[4,2,3,1,128]{4,0,3,2,1:T(4,128)S(1)} %get-tuple-element.209), channel_id=1, source_target_pairs={{0,1},{1,2},{2,3},{3,4},{4,5},{5,6},{6,7},{7,8},{8,9},{9,10},{10,1... | collective-permute-start | bytes 36872 | tf_op jit(solution)/shard_map/ppermute | solution.py:29
  191.3 6.2 %collective-permute-start.9 = (f32[4,2,3,1,128]{4,0,3,2,1:T(4,128)S(1)}, f32[4,2,3,1,128]{4,0,3,2,1:T(4,128)S(1)}, u32[]{:S(2)}, u32[]{:S(2)}) collective-permute-start(f32[4,2,3,1,128]{4,0,3,2,1:T(4,128)S(1)} %get-tuple-element.210), channel_id=1, source_target_pairs={{1,0},{2,1},{3,2},{4,3},{5,4},{6,5},{7,6},{8,7},{9,8},{10,9},{11,1... | collective-permute-start | bytes 36872 | tf_op jit(solution)/shard_map/ppermute | solution.py:31
  229.7 7.5 %collective-permute-start.10 = (f32[4,2,3,1,128]{4,0,3,2,1:T(4,128)S(1)}, f32[4,2,3,1,128]{4,0,3,2,1:T(4,128)S(1)}, u32[]{:S(2)}, u32[]{:S(2)}) collective-permute-start(f32[4,2,3,1,128]{4,0,3,2,1:T(4,128)S(1)} %get-tuple-element.201), channel_id=1, source_target_pairs={{0,1},{1,2},{2,3},{3,4},{4,5},{5,6},{6,7},{7,8},{8,9},{9,10},{10,1... | collective-permute-start | bytes 36872 | tf_op jit(solution)/shard_map/ppermute | solution.py:29
  231.6 6.2 %collective-permute-start.11 = (f32[4,2,3,1,128]{4,0,3,2,1:T(4,128)S(1)}, f32[4,2,3,1,128]{4,0,3,2,1:T(4,128)S(1)}, u32[]{:S(2)}, u32[]{:S(2)}) collective-permute-start(f32[4,2,3,1,128]{4,0,3,2,1:T(4,128)S(1)} %get-tuple-element.202), channel_id=1, source_target_pairs={{1,0},{2,1},{3,2},{4,3},{5,4},{6,5},{7,6},{8,7},{9,8},{10,9},{11,1... | collective-permute-start | bytes 36872 | tf_op jit(solution)/shard_map/ppermute | solution.py:31
  270.3 22.2 %collective-permute-start.12 = (f32[4,2,3,1,128]{4,0,3,2,1:T(4,128)S(1)}, f32[4,2,3,1,128]{4,0,3,2,1:T(4,128)S(1)}, u32[]{:S(2)}, u32[]{:S(2)}) collective-permute-start(f32[4,2,3,1,128]{4,0,3,2,1:T(4,128)S(1)} %get-tuple-element.193), channel_id=1, source_target_pairs={{0,1},{1,2},{2,3},{3,4},{4,5},{5,6},{6,7},{7,8},{8,9},{9,10},{10,1... | collective-permute-start | bytes 36872 | tf_op jit(solution)/shard_map/ppermute | solution.py:29
  272.2 20.3 %collective-permute-start.13 = (f32[4,2,3,1,128]{4,0,3,2,1:T(4,128)S(1)}, f32[4,2,3,1,128]{4,0,3,2,1:T(4,128)S(1)}, u32[]{:S(2)}, u32[]{:S(2)}) collective-permute-start(f32[4,2,3,1,128]{4,0,3,2,1:T(4,128)S(1)} %get-tuple-element.194), channel_id=1, source_target_pairs={{1,0},{2,1},{3,2},{4,3},{5,4},{6,5},{7,6},{8,7},{9,8},{10,9},{11,1... | collective-permute-start | bytes 36872 | tf_op jit(solution)/shard_map/ppermute | solution.py:31
  288.3 12.5 %all-to-all-start.2 = ((f32[16,1,3072]{2,1,0:T(1,128)}), f32[16,1,3072]{2,1,0:T(1,128)}, u32[]{:S(2)}, u32[]{:S(2)}) async-start(f32[16,1,3072]{2,1,0:T(1,128)} %reshape.1219), calls=%async_computation.2 | async-start | bytes 393216 | tf_op jit(solution)/shard_map/all_to_all | solution.py:143
  295.8 0.7 copy-start.4
  295.8 13.9 %copy-start.3 = (f32[4,2,3,2048]{3,0,2,1:T(4,128)}, f32[4,2,3,2048]{3,0,2,1:T(4,128)S(1)}, u32[]{:S(2)}) copy-start(f32[4,2,3,2048]{3,0,2,1:T(4,128)S(1)} %get-tuple-element.191) | copy-start | bytes 589828
  302.8 10.6 %copy-start.8 = (f32[128,64,2]{0,2,1:T(2,128)S(1)}, f32[128,64,2]{0,2,1:T(2,128)}, u32[]{:S(2)}) copy-start(f32[128,64,2]{0,2,1:T(2,128)} %copy-done.7) | copy-start | bytes 196612
  309.6 4.2 copy-start.6
  314.9 11.5 %all-to-all-start.3 = ((f32[64,4,128]{2,1,0:T(4,128)}), f32[64,4,128]{2,1,0:T(4,128)S(1)}, u32[]{:S(2)}, u32[]{:S(2)}) async-start(f32[64,4,128]{2,1,0:T(4,128)} %reshape_reshape.15), calls=%async_computation.3 | async-start | bytes 262144 | tf_op jit(solution)/shard_map/all_to_all | solution.py:148
  328.2 6.8 %collective-permute-start.14 = (f32[4,2,3,1,128]{4,0,3,2,1:T(4,128)S(1)}, f32[4,2,3,1,128]{4,0,3,2,1:T(4,128)S(1)}, u32[]{:S(2)}, u32[]{:S(2)}) collective-permute-start(f32[4,2,3,1,128]{4,0,3,2,1:T(4,128)S(1)} %get-tuple-element.185), channel_id=1, source_target_pairs={{0,1},{1,2},{2,3},{3,4},{4,5},{5,6},{6,7},{7,8},{8,9},{9,10},{10,1... | collective-permute-start | bytes 36872 | tf_op jit(solution)/shard_map/ppermute | solution.py:29
  330.2 6.2 %collective-permute-start.15 = (f32[4,2,3,1,128]{4,0,3,2,1:T(4,128)S(1)}, f32[4,2,3,1,128]{4,0,3,2,1:T(4,128)S(1)}, u32[]{:S(2)}, u32[]{:S(2)}) collective-permute-start(f32[4,2,3,1,128]{4,0,3,2,1:T(4,128)S(1)} %get-tuple-element.186), channel_id=1, source_target_pairs={{1,0},{2,1},{3,2},{4,3},{5,4},{6,5},{7,6},{8,7},{9,8},{10,9},{11,1... | collective-permute-start | bytes 36872 | tf_op jit(solution)/shard_map/ppermute | solution.py:31
  367.9 7.0 %collective-permute-start.16 = (f32[4,2,3,1,128]{4,0,3,2,1:T(4,128)S(1)}, f32[4,2,3,1,128]{4,0,3,2,1:T(4,128)S(1)}, u32[]{:S(2)}, u32[]{:S(2)}) collective-permute-start(f32[4,2,3,1,128]{4,0,3,2,1:T(4,128)S(1)} %get-tuple-element.177), channel_id=1, source_target_pairs={{0,1},{1,2},{2,3},{3,4},{4,5},{5,6},{6,7},{7,8},{8,9},{9,10},{10,1... | collective-permute-start | bytes 36872 | tf_op jit(solution)/shard_map/ppermute | solution.py:29
  369.8 6.2 %collective-permute-start.17 = (f32[4,2,3,1,128]{4,0,3,2,1:T(4,128)S(1)}, f32[4,2,3,1,128]{4,0,3,2,1:T(4,128)S(1)}, u32[]{:S(2)}, u32[]{:S(2)}) collective-permute-start(f32[4,2,3,1,128]{4,0,3,2,1:T(4,128)S(1)} %get-tuple-element.178), channel_id=1, source_target_pairs={{1,0},{2,1},{3,2},{4,3},{5,4},{6,5},{7,6},{8,7},{9,8},{10,9},{11,1... | collective-permute-start | bytes 36872 | tf_op jit(solution)/shard_map/ppermute | solution.py:31
  407.6 6.8 %collective-permute-start.18 = (f32[4,2,3,1,128]{4,0,3,2,1:T(4,128)S(1)}, f32[4,2,3,1,128]{4,0,3,2,1:T(4,128)S(1)}, u32[]{:S(2)}, u32[]{:S(2)}) collective-permute-start(f32[4,2,3,1,128]{4,0,3,2,1:T(4,128)S(1)} %get-tuple-element.169), channel_id=1, source_target_pairs={{0,1},{1,2},{2,3},{3,4},{4,5},{5,6},{6,7},{7,8},{8,9},{9,10},{10,1... | collective-permute-start | bytes 36872 | tf_op jit(solution)/shard_map/ppermute | solution.py:29
  409.6 6.2 %collective-permute-start.19 = (f32[4,2,3,1,128]{4,0,3,2,1:T(4,128)S(1)}, f32[4,2,3,1,128]{4,0,3,2,1:T(4,128)S(1)}, u32[]{:S(2)}, u32[]{:S(2)}) collective-permute-start(f32[4,2,3,1,128]{4,0,3,2,1:T(4,128)S(1)} %get-tuple-element.170), channel_id=1, source_target_pairs={{1,0},{2,1},{3,2},{4,3},{5,4},{6,5},{7,6},{8,7},{9,8},{10,9},{11,1... | collective-permute-start | bytes 36872 | tf_op jit(solution)/shard_map/ppermute | solution.py:31
  447.5 6.8 %collective-permute-start.20 = (f32[4,2,3,1,128]{4,0,3,2,1:T(4,128)S(1)}, f32[4,2,3,1,128]{4,0,3,2,1:T(4,128)S(1)}, u32[]{:S(2)}, u32[]{:S(2)}) collective-permute-start(f32[4,2,3,1,128]{4,0,3,2,1:T(4,128)S(1)} %get-tuple-element.161), channel_id=1, source_target_pairs={{0,1},{1,2},{2,3},{3,4},{4,5},{5,6},{6,7},{7,8},{8,9},{9,10},{10,1... | collective-permute-start | bytes 36872 | tf_op jit(solution)/shard_map/ppermute | solution.py:29
  449.4 6.2 %collective-permute-start.21 = (f32[4,2,3,1,128]{4,0,3,2,1:T(4,128)S(1)}, f32[4,2,3,1,128]{4,0,3,2,1:T(4,128)S(1)}, u32[]{:S(2)}, u32[]{:S(2)}) collective-permute-start(f32[4,2,3,1,128]{4,0,3,2,1:T(4,128)S(1)} %get-tuple-element.162), channel_id=1, source_target_pairs={{1,0},{2,1},{3,2},{4,3},{5,4},{6,5},{7,6},{8,7},{9,8},{10,9},{11,1... | collective-permute-start | bytes 36872 | tf_op jit(solution)/shard_map/ppermute | solution.py:31
  487.5 7.5 %collective-permute-start.22 = (f32[4,2,3,1,128]{4,0,3,2,1:T(4,128)S(1)}, f32[4,2,3,1,128]{4,0,3,2,1:T(4,128)S(1)}, u32[]{:S(2)}, u32[]{:S(2)}) collective-permute-start(f32[4,2,3,1,128]{4,0,3,2,1:T(4,128)S(1)} %get-tuple-element.153), channel_id=1, source_target_pairs={{0,1},{1,2},{2,3},{3,4},{4,5},{5,6},{6,7},{7,8},{8,9},{9,10},{10,1... | collective-permute-start | bytes 36872 | tf_op jit(solution)/shard_map/ppermute | solution.py:29
  489.4 6.2 %collective-permute-start.23 = (f32[4,2,3,1,128]{4,0,3,2,1:T(4,128)S(1)}, f32[4,2,3,1,128]{4,0,3,2,1:T(4,128)S(1)}, u32[]{:S(2)}, u32[]{:S(2)}) collective-permute-start(f32[4,2,3,1,128]{4,0,3,2,1:T(4,128)S(1)} %get-tuple-element.154), channel_id=1, source_target_pairs={{1,0},{2,1},{3,2},{4,3},{5,4},{6,5},{7,6},{8,7},{9,8},{10,9},{11,1... | collective-permute-start | bytes 36872 | tf_op jit(solution)/shard_map/ppermute | solution.py:31
  498.5 0.9 copy-start.11
  498.5 0.9 copy-start.12
  498.8 28.9 %copy-start.9 = (f32[4,1,3,2048]{3,0,2,1:T(4,128)S(1)}, f32[4,1,3,2048]{3,0,2,1:T(4,128)}, u32[]{:S(2)}) copy-start(f32[4,1,3,2048]{3,0,2,1:T(4,128)} %get-tuple-element.290) | copy-start | bytes 294916
  498.8 28.9 %copy-start.10 = (f32[4,1,3,2048]{3,0,2,1:T(4,128)S(1)}, f32[4,1,3,2048]{3,0,2,1:T(4,128)}, u32[]{:S(2)}) copy-start(f32[4,1,3,2048]{3,0,2,1:T(4,128)} %get-tuple-element.291) | copy-start | bytes 294916
where the time goes:
time: 540 us; the launch traced here: 530 us
  blocking collectives  265 us (49%)
  starting transfers between devices  100 us (19%)
  local copies, waits for them, and re-layouts  84.4 us (16%)
  other arithmetic  40.1 us (7%)
  waiting for transfers between devices  37.3 us (7%)
    psum x10, blocking collectives, body(): lax.psum((upper_real, upper_imag, lower_part), 'node')  265 us
    ppermute x12, starting transfers between devices, extended_2(): lax.ppermute(head, axis, [((i + 1) % count, i) for i in range(ends)])  59.1 us
    gather x48, local copies, waits for them, and re-layouts, beside_of(): jnp.take(extended, local_links[:, link], axis=3).reshape(fields.shape)  33.1 us
    unnamed x36, local copies, waits for them, and re-layouts  30.6 us
    ppermute x12, starting transfers between devices, extended_2(): lax.ppermute(tail, axis, [(i, (i + 1) % count) for i in range(ends)])  23 us
    all_to_all x2, waiting for transfers between devices, body(): lax.all_to_all(terms.reshape(total_slots, 4, columns), 'freq', split_axis...  14.8 us
    all_to_all x2, waiting for transfers between devices, body(): lax.all_to_all(stacked, 'freq', split_axis=2, concat_axis=0, tiled=True)  11.8 us
    all_to_all x2, starting transfers between devices, body(): lax.all_to_all(stacked, 'freq', split_axis=2, concat_axis=0, tiled=True)  11.2 us
  transfers between devices with their start and end apart: 28, of which 14 were waited for; matrix products, arithmetic and copies ran while one was open for 5% of the time, Pallas kernels for 0%

commit v1 on v0

v1 whole, which is shorter than its diff:
```python
import functools
import math

import jax
import jax.numpy as jnp
import numpy as np
from jax import lax
from jax.experimental import pallas as pl
from jax.experimental.pallas import tpu as pltpu
from jax.sharding import PartitionSpec as P

SAMPLES = 128
LMAX = 5
SWEEPS = 2

FRICTION = 2.0
CORIOLIS = 0.5
ETA_DAMP = 0.2
OMEGA_STEP = 0.05
SPEED_FLOOR = 0.01
TOP_HARMONIC = lax.Precision.HIGHEST

RANKS = 16
LANES = 128
SHARE = 8
SHIFT = 2.5
COUNT = LMAX + 1
REAL_PAIRS = [(m, n) for m in range(COUNT) for n in range(m, COUNT)]
IMAG_PAIRS = [(m, n) for m in range(COUNT) for n in range(m + 1, COUNT)]
ROW_DAMPING, ROW_DEPTHS, ROW_LINKS = 12, 13, 14

VMEM = pl.BlockSpec(memory_space=pltpu.VMEM)
HBM = pl.BlockSpec(memory_space=pl.ANY)
SMEM = pl.BlockSpec(memory_space=pltpu.SMEM)


def iota(shape, axis):
    return lax.broadcasted_iota(jnp.int32, shape, axis)


def swap_blocks(rows):
    lane = iota((8, LANES), 1)
    rows = list(rows)
    for bit in range(4):
        step = SHARE << bit
        upper = (lane & step) != 0
        for i in range(RANKS):
            if i & (1 << bit):
                continue
            low, high = rows[i], rows[i | (1 << bit)]
            rows[i] = jnp.where(upper, pltpu.roll(high, step, 1), low)
            rows[i | (1 << bit)] = jnp.where(upper, high, pltpu.roll(low, LANES - step, 1))
    return rows


def pack_group(rows_of, out_ref, group):
    rows = [rows_of(b) for b in range(RANKS)]
    for rank, row in enumerate(swap_blocks(rows)):
        out_ref[rank, group] = row


def pack_kernel(
    fields_hbm,
    forcing_hbm,
    weights_hbm,
    east_hbm,
    north_hbm,
    damping_hbm,
    depths_hbm,
    links_ref,
    out_ref,
    fields_ref,
    forcing_ref,
    weights_ref,
    east_ref,
    north_ref,
    damping_ref,
    depths_ref,
    rows_ref,
    sems,
):
    sources = (fields_hbm, forcing_hbm, weights_hbm, east_hbm, north_hbm, damping_hbm, depths_hbm)
    targets = (fields_ref, forcing_ref, weights_ref, east_ref, north_ref, damping_ref, depths_ref)
    copies = [pltpu.make_async_copy(a, b, sems.at[i]) for i, (a, b) in enumerate(zip(sources, targets))]
    for copy in copies:
        copy.start()
    first = lax.axis_index("node") * RANKS
    for link in range(2):
        for b in range(RANKS):
            local = (links_ref[2 + link, b] - first).astype(jnp.float32)
            at = ROW_LINKS + link
            rows_ref[at, :, LANES * b : LANES * (b + 1)] = jnp.full((1, LANES), local, jnp.float32)
    for group in range(6):
        if group % 3 == 0:
            copies[group // 3].wait()
        source = (fields_ref, forcing_ref)[group // 3]

        def block(b):
            start = 32 * (group % 3) + 2 * b
            parts = [source[pl.ds(start + part, 4, stride=96), :] for part in range(2)]
            return jnp.concatenate(parts, axis=0)

        pack_group(block, out_ref, group)
    for copy in copies[2:]:
        copy.wait()
    for kind, source in enumerate((weights_ref, east_ref, north_ref)):
        for link in range(4):
            rows_ref[4 * kind + link] = source[link : link + 1, :]
    rows_ref[ROW_DAMPING] = damping_ref[...]
    rows_ref[ROW_DEPTHS] = depths_ref[...]
    mine = lax.axis_index("freq")
    pack_group(lambda b: jnp.broadcast_to(rows_ref[mine, :, LANES * b : LANES * (b + 1)], (8, LANES)), out_ref, 6)


def forward_kernel(given_ref, out_ref):
    for half in range(2):
        rows = jnp.concatenate([given_ref[8 * half + i, 6, 0:1] for i in range(8)], axis=0)
        for rank in range(RANKS):
            out_ref[rank, 3 + half] = rows
    for rank in range(RANKS):
        for comp in range(3):
            out_ref[rank, comp] = given_ref[rank, comp]


def unpack_kernel(x_ref, fields_ref, residual_ref):
    for group in range(6):
        target = fields_ref if group < 3 else residual_ref
        comp = group % 3
        rows = swap_blocks([x_ref[rank, group] for rank in range(RANKS)])
        for b, row in enumerate(rows):
            for part in range(2):
                target[pl.ds(32 * comp + 2 * b + part, 4, stride=96), :] = row[4 * part : 4 * part + 4]


def tables_kernel(harmonic_ref, cosines_ref, synthesis_ref, analysis_ref):
    samples = iota((SAMPLES, LANES), 0)
    quarter = jnp.where((iota((SAMPLES, LANES), 1) & 4) != 0, SAMPLES // 4, 0)
    harmonic = jnp.broadcast_to(harmonic_ref[...], (SAMPLES, LANES))
    turn = (samples * harmonic + quarter) & (SAMPLES - 1)
    cosines = jnp.broadcast_to(cosines_ref[...], (SAMPLES, LANES))
    synthesis = jnp.take_along_axis(cosines, turn, axis=1, mode="promise_in_bounds")
    synthesis_ref[...] = synthesis
    analysis_ref[...] = (synthesis * jnp.where(harmonic == 0, 1.0 / SAMPLES, 2.0 / SAMPLES)).T


def friction_kernel(x_ref, table_ref, synthesis_ref, analysis_ref, out_ref):
    moments = [
        jnp.dot(
            synthesis_ref[...],
            x_ref[:, comp].reshape(LANES, LANES),
            precision=TOP_HARMONIC,
            preferred_element_type=jnp.float32,
        )
        for comp in range(3)
    ]
    elevation, eastward, northward = moments
    group = lax.axis_index("freq")
    depths = table_ref[ROW_DEPTHS, 3 + group // 8]
    depth = jnp.sum(jnp.where(iota((8, LANES), 0) == group % 8, depths, 0.0), axis=0, keepdims=True)
    column_depth = depth + 0.5 * jnp.tanh(elevation)
    magnitude = jnp.sqrt(eastward * eastward + northward * northward + SPEED_FLOOR)
    factor = FRICTION * magnitude / column_depth
    for comp, moving in enumerate((eastward, northward)):
        terms = jnp.dot(
            analysis_ref[...], factor * moving, precision=TOP_HARMONIC, preferred_element_type=jnp.float32
        )
        out_ref[:, comp] = terms.reshape(RANKS, 8, LANES)


def prepare_links(table_ref, links_ref, index_ref):
    share = iota((8, LANES), 1) & (SHARE - 1)
    for half in range(2):
        rows = [table_ref[at, 3 + half] for at in range(RANKS)]
        spread = rows[0] + rows[1] + rows[2] + rows[3]
        values = rows[:12] + [
            spread + (ETA_DAMP - SHIFT),
            spread + (rows[ROW_DAMPING] - SHIFT),
            rows[4] + rows[5] + rows[6] + rows[7],
            rows[8] + rows[9] + rows[10] + rows[11],
        ]
        for i in range(8):
            for at, value in enumerate(values):
                links_ref[8 * half + i, at] = jnp.broadcast_to(value[i : i + 1], (8, LANES))
        for link in range(2):
            at = rows[ROW_LINKS + link].astype(jnp.int32)
            outside = jnp.logical_or(at < 0, at > RANKS - 1)
            lane = (at & (RANKS - 1)) * SHARE + share
            index = jnp.where(outside, lane + LANES, lane)
            for i in range(8):
                index_ref[8 * half + i, link] = jnp.broadcast_to(index[i : i + 1], (8, LANES))


def apply_operator(vectors, links_ref, index_ref):
    lane = iota((8, LANES), 1)
    first = lane < SHARE
    last = lane >= LANES - SHARE
    result = []
    for g in range(RANKS):
        here = vectors[g]
        before = vectors[g - 1] if g > 0 else [pltpu.roll(x, LANES - 2 * SHARE, 1) for x in here]
        after = vectors[g + 1] if g < RANKS - 1 else [pltpu.roll(x, 2 * SHARE, 1) for x in here]
        beside = []
        beside.append([pltpu.roll(jnp.where(last, p, x), SHARE, 1) for p, x in zip(before, here)])
        beside.append([pltpu.roll(jnp.where(first, n, x), LANES - SHARE, 1) for n, x in zip(after, here)])
        edges = [jnp.where(last, p, n) for p, n in zip(before, after)]
        for link in range(2):
            index = index_ref[g, link]
            outside = index >= LANES
            index = index & (LANES - 1)
            beside.append(
                [
                    jnp.where(
                        outside,
                        jnp.take_along_axis(e, index, axis=1, mode="promise_in_bounds"),
                        jnp.take_along_axis(x, index, axis=1, mode="promise_in_bounds"),
                    )
                    for e, x in zip(edges, here)
                ]
            )
        x_ele, x_east, x_north = here
        eta_sum, flow_sum, east_sum, north_sum = [links_ref[g, 12 + at] for at in range(4)]
        ele = eta_sum * x_ele - east_sum * x_east - north_sum * x_north
        east = flow_sum * x_east - east_sum * x_ele - CORIOLIS * x_north
        north = flow_sum * x_north - north_sum * x_ele + CORIOLIS * x_east
        for link in range(4):
            y_ele, y_east, y_north = beside[link]
            weight, to_east, to_north = [links_ref[g, at + link] for at in (0, 4, 8)]
            ele = ele - weight * y_ele + to_east * y_east + to_north * y_north
            east = east - weight * y_east + to_east * y_ele
            north = north - weight * y_north + to_north * y_ele
        result.append([ele, east, north])
    return result


def slot_rows(ref, pick):
    first = lax.axis_index("freq") * 4
    slot = iota((8, LANES), 0) & 3
    values = [pick(ref, first + s) for s in range(4)]
    return jnp.where(slot == 0, values[0], jnp.where(slot == 1, values[1], jnp.where(slot == 2, values[2], values[3])))


def angular_rows(harmonic_ref):
    return OMEGA_STEP * slot_rows(harmonic_ref, lambda ref, i: ref[i]).astype(jnp.float32)


def start_kernel(given_ref, table_ref, harmonic_ref, base_ref, links_ref, index_ref):
    prepare_links(table_ref, links_ref, index_ref)
    turn = angular_rows(harmonic_ref) * jnp.where(iota((8, LANES), 0) < 4, -1.0, 1.0)
    vectors = [[given_ref[g, comp] for comp in range(3)] for g in range(RANKS)]
    images = apply_operator(vectors, links_ref, index_ref)
    for g in range(RANKS):
        for comp in range(3):
            rest = SHIFT * vectors[g][comp] + turn * pltpu.roll(vectors[g][comp], 4, 0)
            base_ref[g, comp] = given_ref[g, 3 + comp] - images[g][comp] - rest


def basis_kernel(base_ref, friction_ref, links_ref, index_ref, basis_ref, gram_ref):
    for g in range(RANKS):
        basis_ref[0, g, 0] = base_ref[g, 0]
        basis_ref[0, g, 1] = base_ref[g, 1] - friction_ref[g, 0]
        basis_ref[0, g, 2] = base_ref[g, 2] - friction_ref[g, 1]

    def power(m, _):
        vectors = [[basis_ref[m, g, comp] for comp in range(3)] for g in range(RANKS)]
        images = apply_operator(vectors, links_ref, index_ref)
        for g in range(RANKS):
            for comp in range(3):
                basis_ref[m + 1, g, comp] = images[g][comp]
        return 0

    lax.fori_loop(0, LMAX, power, 0)

    def products(g, sums):
        for comp in range(3):
            vectors = [basis_ref[m, g, comp] for m in range(COUNT)]
            turned = [None] + [pltpu.roll(v, 4, 0) for v in vectors[1:]]
            terms = [vectors[m] * vectors[n] for m, n in REAL_PAIRS]
            terms += [vectors[m] * turned[n] for m, n in IMAG_PAIRS]
            sums = tuple(a + b for a, b in zip(sums, terms))
        return sums

    entries = len(REAL_PAIRS) + len(IMAG_PAIRS)
    sums = lax.fori_loop(0, RANKS, products, tuple(jnp.zeros((8, LANES), jnp.float32) for _ in range(entries)))
    lane = iota((8, LANES), 1)
    gram = jnp.zeros((8, LANES), jnp.float32)
    for entry, value in enumerate(sums):
        gram = jnp.where(lane == entry, jnp.sum(value, axis=1, keepdims=True), gram)
    turned = pltpu.roll(gram, 4, 0)
    gram = jnp.where(lane < len(REAL_PAIRS), gram + turned, gram - turned)
    packed = jnp.where(lane < LANES // 2, gram, pltpu.roll(pltpu.roll(gram, LANES // 2, 1), 6, 0))[:2]
    for rank in range(RANKS):
        gram_ref[rank] = packed


def step_sizes(gram_ref, harmonic_ref, counts_ref, sweep):
    gram = gram_ref[0]
    for rank in range(1, RANKS):
        gram = gram + gram_ref[rank]
    swapped = pltpu.roll(gram, LANES // 2, 1)
    gram = jnp.concatenate([gram, swapped, gram, swapped], axis=0)

    def entry(values, at):
        return jnp.broadcast_to(values[:, at : at + 1], (8, LANES))

    inner = {}
    for at, (m, n) in enumerate(REAL_PAIRS):
        inner[m, n] = (entry(gram, at), None)
    for at, (m, n) in enumerate(IMAG_PAIRS):
        inner[m, n] = (inner[m, n][0], entry(gram, len(REAL_PAIRS) + at))

    def mul(a, b):
        return (a[0] * b[0] - a[1] * b[1], a[0] * b[1] + a[1] * b[0])

    def add(a, b):
        return (a[0] + b[0], a[1] + b[1])

    def conj_mul(a, b):
        return (a[0] * b[0] + a[1] * b[1], a[0] * b[1] - a[1] * b[0])

    def gram_times(m, n, b):
        if m == n:
            g = inner[m, n][0]
            return (g * b[0], g * b[1])
        if m < n:
            return mul(inner[m, n], b)
        return conj_mul(inner[n, m], b)

    angular = angular_rows(harmonic_ref)
    counts = slot_rows(counts_ref, lambda ref, i: ref[sweep, i])
    zero = jnp.zeros((8, LANES), jnp.float32)
    residual = [(jnp.ones((8, LANES), jnp.float32), zero)]
    correction = [(zero, zero) for _ in range(LMAX)]
    for step in range(LMAX):
        image = []
        for m in range(step + 2):
            value = (zero, zero)
            if m <= step:
                r = residual[m]
                value = (SHIFT * r[0] - angular * r[1], SHIFT * r[1] + angular * r[0])
            if m > 0:
                value = add(value, residual[m - 1])
            image.append(value)
        upper = (zero, zero)
        lower = zero
        for m in range(step + 2):
            with_residual = (zero, zero)
            for n in range(step + 1):
                with_residual = add(with_residual, gram_times(m, n, residual[n]))
            upper = add(upper, conj_mul(image[m], with_residual))
            with_image = (zero, zero)
            for n in range(step + 2):
                with_image = add(with_image, gram_times(m, n, image[n]))
            lower = lower + image[m][0] * with_image[0] + image[m][1] * with_image[1]
        lower = lower + 1e-06
        active = jnp.where(step < counts, 1.0, 0.0)
        alpha = (active * upper[0] / lower, active * upper[1] / lower)
        for m in range(step + 1):
            correction[m] = add(correction[m], mul(alpha, residual[m]))
        residual = residual + [(zero, zero)]
        for m in range(step + 2):
            change = mul(alpha, image[m])
            residual[m] = (residual[m][0] - change[0], residual[m][1] - change[1])
    return correction, residual


def combine(coefs, vectors, sign):
    straight = coefs[0][0] * vectors[0]
    turned = coefs[0][1] * vectors[0]
    for (real, imag), vector in zip(coefs[1:], vectors[1:]):
        straight = straight + real * vector
        turned = turned + imag * vector
    return straight + sign * pltpu.roll(turned, 4, 0)


def update_kernel(sweep, gram_ref, fields_ref, basis_ref, friction_ref, harmonic_ref, counts_ref, *outs):
    correction, residual = step_sizes(gram_ref, harmonic_ref, counts_ref, sweep)
    sign = jnp.where(iota((8, LANES), 0) < 4, -1.0, 1.0)

    def update(g, _):
        for comp in range(3):
            vectors = [basis_ref[m, g, comp] for m in range(COUNT)]
            fields = fields_ref[g, comp] + combine(correction, vectors[:LMAX], sign)
            left = combine(residual, vectors, sign)
            if sweep == SWEEPS - 1:
                outs[0][g, comp] = fields
                outs[0][g, 3 + comp] = left
            else:
                outs[0][g, comp] = fields
                outs[1][g, comp] = left if comp == 0 else left + friction_ref[g, comp - 1]
        return 0

    lax.fori_loop(0, RANKS, update, 0)


def struct(*shape):
    return jax.ShapeDtypeStruct(shape, jnp.float32)


def call(kernel, out, specs, scratch=(), mebibytes=16):
    outs = out if isinstance(out, list) else [out]
    result = pl.pallas_call(
        kernel,
        out_shape=outs,
        in_specs=specs,
        out_specs=[VMEM] * len(outs),
        scratch_shapes=list(scratch),
        compiler_params=pltpu.CompilerParams(vmem_limit_bytes=mebibytes * 1024 * 1024),
    )
    return (lambda *args: result(*args)) if isinstance(out, list) else (lambda *args: result(*args)[0])


def exchange(values, axis):
    return lax.all_to_all(values, axis, split_axis=0, concat_axis=0, tiled=True)


def rows_of(x):
    return x.transpose(0, 2, 1, 3).reshape(4, 3, 2, RANKS, LANES).transpose(0, 1, 3, 2, 4).reshape(-1, LANES)


def fields_of(rows):
    return rows.reshape(4, 3, RANKS, 2, LANES).transpose(0, 3, 1, 2, 4).reshape(4, 2, 3, RANKS * LANES)


def body(
    harmonics, forcing, depths, damping, weights, couple_east, couple_north, connections, counts, harmonic_of_slot
):
    whole = pltpu.VMEM((384, LANES), jnp.float32)
    four = pltpu.VMEM((4, 2048), jnp.float32)
    line = pltpu.VMEM((1, 2048), jnp.float32)
    packed = call(
        pack_kernel,
        struct(RANKS, 7, 8, LANES),
        [HBM] * 7 + [SMEM],
        (
            whole,
            whole,
            four,
            four,
            four,
            line,
            line,
            pltpu.VMEM((RANKS, 1, 2048), jnp.float32),
            pltpu.SemaphoreType.DMA((7,)),
        ),
        58,
    )(
        rows_of(harmonics),
        rows_of(forcing),
        weights,
        couple_east,
        couple_north,
        damping.reshape(1, -1),
        depths.reshape(1, -1),
        connections.T,
    )
    given = exchange(packed, "node")
    table = exchange(call(forward_kernel, struct(RANKS, 5, 8, LANES), [VMEM])(given), "freq")

    slots = jnp.broadcast_to(harmonic_of_slot.reshape(RANKS, 1, 4), (RANKS, 2, 4)).reshape(1, LANES)
    cosines = np.cos(np.arange(SAMPLES) * (2.0 * math.pi / SAMPLES)).astype(np.float32).reshape(1, SAMPLES)

    synthesis, analysis = call(tables_kernel, [struct(SAMPLES, LANES), struct(LANES, SAMPLES)], [VMEM] * 2)(
        slots, cosines
    )

    def friction_of(received):
        terms = call(friction_kernel, struct(RANKS, 2, 8, LANES), [VMEM] * 4)(received, table, synthesis, analysis)
        return exchange(terms, "freq")

    base, links, index = call(
        start_kernel,
        [
            struct(RANKS, 3, 8, LANES),
            struct(RANKS, 16, 8, LANES),
            jax.ShapeDtypeStruct((RANKS, 2, 8, LANES), jnp.int32),
        ],
        [VMEM, VMEM, SMEM],
    )(given, table, harmonic_of_slot)
    fields = given
    friction = friction_of(table)
    for sweep in range(SWEEPS):
        basis, gram = call(
            basis_kernel, [struct(COUNT, RANKS, 3, 8, LANES), struct(RANKS, 2, LANES)], [VMEM] * 4
        )(base, friction, links, index)
        gram = exchange(gram, "node")
        if sweep < SWEEPS - 1:
            outs = [struct(RANKS, 3, 8, LANES), struct(RANKS, 3, 8, LANES)]
        else:
            outs = [struct(RANKS, 6, 8, LANES)]
        results = call(functools.partial(update_kernel, sweep), outs, [VMEM] * 4 + [SMEM] * 2)(
            gram, fields, basis, friction, harmonic_of_slot, counts
        )
        if sweep < SWEEPS - 1:
            fields, base = results
            friction = friction_of(exchange(fields, "freq"))
    out = [struct(384, LANES)] * 2
    fields, residual = call(unpack_kernel, out, [VMEM])(exchange(results[0], "node"))
    return (fields_of(fields), fields_of(residual))


def solution(mesh):
    return jax.shard_map(
        body,
        mesh=mesh,
        in_specs=(
            P("freq", None, None, "node"),
            P("freq", None, None, "node"),
            P("node"),
            P("node"),
            P(None, "node"),
            P(None, "node"),
            P(None, "node"),
            P("node", None),
            P(),
            P(),
        ),
        out_specs=(P("freq", None, None, "node"), P("freq", None, None, "node")),
        check_vma=False,
    )
```

time: 540 us -> 134 us (0.25)
  the two profiles are of different devices: /device:TPU:128 before, /device:TPU:1 now
where the time goes in v1:
time: 134 us; the launch traced here: 133 us
  blocking collectives  87.6 us (65%)
  Pallas kernels  19.5 us (15%)
  waiting for transfers between devices  14.6 us (11%)
  starting transfers between devices  10.3 us (8%)
    all_to_all x6, blocking collectives, exchange(): return lax.all_to_all(values, axis, split_axis=0, concat_axis=0, tiled=True)  87.6 us
    all_to_all x2, waiting for transfers between devices, exchange(): return lax.all_to_all(values, axis, split_axis=0, concat_axis=0, tiled=True)  14.6 us
    pallas_call x7, Pallas kernels, call(): result(*args)  13.3 us
    all_to_all x2, starting transfers between devices, exchange(): return lax.all_to_all(values, axis, split_axis=0, concat_axis=0, tiled=True)  10.3 us
    pallas_call x4, Pallas kernels, call(): result(*args)[0]  6.2 us
  transfers between devices with their start and end apart: 2, of which 2 were waited for; matrix products, arithmetic and copies ran while one was open for 0% of the time, Pallas kernels for 1%

profile of v1, /device:TPU:1, one launch (start us, length us, event | category | flops | bytes accessed | tf_op | source)
XLA Modules:
  0.0 132.9 jit_solution(3232451752465075603)
XLA Ops:
  0.6 3.6 %shard_map.122 = f32[16,7,8,128]{3,2,1,0:T(8,128)} custom-call(f32[384,128]{1,0:T(8,128)} %bitcast.27, f32[384,128]{1,0:T(8,128)} %bitcast.28, f32[4,2048]{1,0:T(4,128)} %weights_hbm.1, f32[4,2048]{1,0:T(4,128)} %east_hbm.1, f32[4,2048]{1,0:T(4,128)} %north_hbm.1, f32[1,2048]{1,0:T(1,128)} %bitcast.29, f32[1,2048]{1,0:T(1,128)} %bitcast.30, s32[4,16]{1,0:T(4,128)} %bitcast.31), custom_call_target="tpu_custom_call" | custom-call | tf_op jit(solution)/shard_map/pallas_call | solution.py:409
  4.2 0.0 copy-start
  4.2 0.0 copy-start.2
  4.3 26.0 %all_to_all.40.given_ref.fields_ref = f32[16,7,8,128]{3,2,1,0:T(8,128)S(1)} all-to-all(f32[16,7,8,128]{3,2,1,0:T(8,128)} %shard_map.122), channel_id=1, replica_groups=mesh['freq'=16,'node'=16] {'node'}, dimensions={0} | all-to-all | bytes 917504 | tf_op jit(solution)/shard_map/all_to_all | solution.py:413
  30.2 0.7 shard_map.123
  31.0 6.8 %all-to-all-start.1 = ((f32[16,5,8,128]{3,2,1,0:T(8,128)}), f32[16,5,8,128]{3,2,1,0:T(8,128)S(1)}, u32[]{:S(2)}, u32[]{:S(2)}) async-start(f32[16,5,8,128]{3,2,1,0:T(8,128)} %shard_map.123), calls=%async_computation.1 | async-start | bytes 655360 | tf_op jit(solution)/shard_map/all_to_all | solution.py:413
  37.7 0.0 copy-done
  37.7 0.1 broadcast_in_dim.7
  37.8 0.1 reshape.45.harmonic_ref
  38.0 0.0 copy-done.2
  38.0 0.2 shard_map.125
  38.1 9.0 %all-to-all-done.1.table_ref.x_ref = f32[16,5,8,128]{3,2,1,0:T(8,128)S(1)} async-done(((f32[16,5,8,128]{3,2,1,0:T(8,128)}), f32[16,5,8,128]{3,2,1,0:T(8,128)S(1)}, u32[]{:S(2)}, u32[]{:S(2)}) %all-to-all-start.1) | async-done | bytes 327712 | tf_op jit(solution)/shard_map/all_to_all | solution.py:413
  47.1 1.3 shard_map.126
  48.4 3.5 %all-to-all-start.2 = ((f32[16,2,8,128]{3,2,1,0:T(8,128)}), f32[16,2,8,128]{3,2,1,0:T(8,128)S(1)}, u32[]{:S(2)}, u32[]{:S(2)}) async-start(f32[16,2,8,128]{3,2,1,0:T(8,128)} %shard_map.126), calls=%async_computation.2 | async-start | bytes 262144 | tf_op jit(solution)/shard_map/all_to_all | solution.py:413
  51.9 0.0 copy-start.1
  51.9 1.1 shard_map.124
  53.0 5.7 %all-to-all-done.2.friction_ref = f32[16,2,8,128]{3,2,1,0:T(8,128)S(1)} async-done(((f32[16,2,8,128]{3,2,1,0:T(8,128)}), f32[16,2,8,128]{3,2,1,0:T(8,128)S(1)}, u32[]{:S(2)}, u32[]{:S(2)}) %all-to-all-start.2) | async-done | bytes 131104 | tf_op jit(solution)/shard_map/all_to_all | solution.py:413
  58.7 3.8 %shard_map.127 = (f32[6,16,3,8,128]{4,3,2,1,0:T(8,128)S(1)}, f32[16,2,128]{2,1,0:T(2,128)S(1)}) custom-call(f32[16,3,8,128]{3,2,1,0:T(8,128)S(1)} %get-tuple-element.15.base_ref, f32[16,2,8,128]{3,2,1,0:T(8,128)S(1)} %all-to-all-done.2.friction_ref, f32[16,16,8,128]{3,2,1,0:T(8,128)S(1)} %get-tuple-element.18.links_ref, ...), custom_call_target="tpu_custom_call" | custom-call | tf_op jit(solution)/shard_map/pallas_call | solution.py:409
  62.5 11.7 %all_to_all.41.gram_ref = f32[16,2,128]{2,1,0:T(2,128)S(1)} all-to-all(f32[16,2,128]{2,1,0:T(2,128)S(1)} %get-tuple-element.20), channel_id=1, replica_groups=mesh['freq'=16,'node'=16] {'node'}, dimensions={0} | all-to-all | bytes 32768 | tf_op jit(solution)/shard_map/all_to_all | solution.py:413
  74.2 0.0 copy-done.1
  74.2 1.4 %shard_map.128 = (f32[16,3,8,128]{3,2,1,0:T(8,128)S(1)}, f32[16,3,8,128]{3,2,1,0:T(8,128)S(1)}) custom-call(f32[16,2,128]{2,1,0:T(2,128)S(1)} %all_to_all.41.gram_ref, f32[16,7,8,128]{3,2,1,0:T(8,128)S(1)} %all_to_all.40.given_ref.fields_ref, f32[6,16,3,8,128]{4,3,2,1,0:T(8,128)S(1)} %get-tuple-element.21.basis_ref, ...), custom_call_target="tpu_custom_call" | custom-call | tf_op jit(solution)/shard_map/pallas_call | solution.py:409
  75.6 10.0 %all_to_all.42.x_ref = f32[16,3,8,128]{3,2,1,0:T(8,128)S(1)} all-to-all(f32[16,3,8,128]{3,2,1,0:T(8,128)S(1)} %get-tuple-element.23.fields_ref), channel_id=1, replica_groups=mesh['freq'=16,'node'=16] {'freq'}, dimensions={0} | all-to-all | bytes 393216 | tf_op jit(solution)/shard_map/all_to_all | solution.py:413
  85.6 0.6 shard_map.129
  86.2 9.8 %all_to_all.43.friction_ref = f32[16,2,8,128]{3,2,1,0:T(8,128)S(1)} all-to-all(f32[16,2,8,128]{3,2,1,0:T(8,128)S(1)} %shard_map.129), channel_id=1, replica_groups=mesh['freq'=16,'node'=16] {'freq'}, dimensions={0} | all-to-all | bytes 262144 | tf_op jit(solution)/shard_map/all_to_all | solution.py:413
  96.0 3.8 %shard_map.130 = (f32[6,16,3,8,128]{4,3,2,1,0:T(8,128)S(1)}, f32[16,2,128]{2,1,0:T(2,128)S(1)}) custom-call(f32[16,3,8,128]{3,2,1,0:T(8,128)S(1)} %get-tuple-element.22.base_ref, f32[16,2,8,128]{3,2,1,0:T(8,128)S(1)} %all_to_all.43.friction_ref, f32[16,16,8,128]{3,2,1,0:T(8,128)S(1)} %get-tuple-element.18.links_ref, ...), custom_call_target="tpu_custom_call" | custom-call | tf_op jit(solution)/shard_map/pallas_call | solution.py:409
  99.8 12.8 %all_to_all.44.gram_ref = f32[16,2,128]{2,1,0:T(2,128)S(1)} all-to-all(f32[16,2,128]{2,1,0:T(2,128)S(1)} %get-tuple-element.24), channel_id=1, replica_groups=mesh['freq'=16,'node'=16] {'node'}, dimensions={0} | all-to-all | bytes 32768 | tf_op jit(solution)/shard_map/all_to_all | solution.py:413
  112.6 1.4 %shard_map.131 = f32[16,6,8,128]{3,2,1,0:T(8,128)S(1)} custom-call(f32[16,2,128]{2,1,0:T(2,128)S(1)} %all_to_all.44.gram_ref, f32[16,3,8,128]{3,2,1,0:T(8,128)S(1)} %get-tuple-element.23.fields_ref, f32[6,16,3,8,128]{4,3,2,1,0:T(8,128)S(1)} %get-tuple-element.25.basis_ref, f32[16,2,8,128]{3,2,1,0:T(8,128)S(1)} %all_to_all.43.friction_ref, s32[64]{0:T(128)S(1)} %copy-done, ...), custom_call_target="tpu_custom_call" | custom-call | tf_op jit(solution)/shard_map/pallas_call | solution.py:409
  114.0 17.4 %all_to_all.45.x_ref = f32[16,6,8,128]{3,2,1,0:T(8,128)S(1)} all-to-all(f32[16,6,8,128]{3,2,1,0:T(8,128)S(1)} %shard_map.131), channel_id=1, replica_groups=mesh['freq'=16,'node'=16] {'node'}, dimensions={0} | all-to-all | bytes 786432 | tf_op jit(solution)/shard_map/all_to_all | solution.py:413
  131.3 1.6 %shard_map.132 = (f32[384,128]{1,0:T(8,128)}, f32[384,128]{1,0:T(8,128)}) custom-call(f32[16,6,8,128]{3,2,1,0:T(8,128)S(1)} %all_to_all.45.x_ref), custom_call_target="tpu_custom_call" | custom-call | tf_op jit(solution)/shard_map/pallas_call | solution.py:409
  (1 shorter events, 0.0 us)
Async XLA Ops:
  4.2 33.5 %copy-start = (s32[64]{0:T(128)S(1)}, s32[64]{0:T(128)}, u32[]{:S(2)}) copy-start(s32[64]{0:T(128)} %harmonic_ref.5) | copy-start | bytes 772
  4.2 33.7 %copy-start.2 = (f32[1,128]{1,0:T(1,128)S(1)}, f32[1,128]{1,0:T(1,128)}, u32[]{:S(2)}) copy-start(f32[1,128]{1,0:T(1,128)} %constant.2.clone.cosines_ref) | copy-start | bytes 1540
  31.0 16.1 %all-to-all-start.1 = ((f32[16,5,8,128]{3,2,1,0:T(8,128)}), f32[16,5,8,128]{3,2,1,0:T(8,128)S(1)}, u32[]{:S(2)}, u32[]{:S(2)}) async-start(f32[16,5,8,128]{3,2,1,0:T(8,128)} %shard_map.123), calls=%async_computation.1 | async-start | bytes 655360 | tf_op jit(solution)/shard_map/all_to_all | solution.py:413
  48.4 10.3 %all-to-all-start.2 = ((f32[16,2,8,128]{3,2,1,0:T(8,128)}), f32[16,2,8,128]{3,2,1,0:T(8,128)S(1)}, u32[]{:S(2)}, u32[]{:S(2)}) async-start(f32[16,2,8,128]{3,2,1,0:T(8,128)} %shard_map.126), calls=%async_computation.2 | async-start | bytes 262144 | tf_op jit(solution)/shard_map/all_to_all | solution.py:413
  51.9 22.3 %copy-start.1 = (s32[2,64]{1,0:T(2,128)S(1)}, s32[2,64]{1,0:T(2,128)}, u32[]{:S(2)}) copy-start(s32[2,64]{1,0:T(2,128)} %counts_ref.3) | copy-start | bytes 1540

commit v2 on v1

--- a/solution.py
+++ b/solution.py
@@ -28,6 +28,8 @@
 REAL_PAIRS = [(m, n) for m in range(COUNT) for n in range(m, COUNT)]
 IMAG_PAIRS = [(m, n) for m in range(COUNT) for n in range(m + 1, COUNT)]
 ROW_DAMPING, ROW_DEPTHS, ROW_LINKS = 12, 13, 14
+
+FIELDS_AT, COEFS_AT, FRICTION_AT = 3, 6, 8
 
 VMEM = pl.BlockSpec(memory_space=pltpu.VMEM)
 HBM = pl.BlockSpec(memory_space=pl.ANY)
@@ -53,10 +55,18 @@
     return rows
 
 
-def pack_group(rows_of, out_ref, group):
-    rows = [rows_of(b) for b in range(RANKS)]
-    for rank, row in enumerate(swap_blocks(rows)):
-        out_ref[rank, group] = row
+def read_rows(ref, comp, block):
+    start = 32 * comp + 2 * block
+    return jnp.concatenate([ref[pl.ds(start + part, 4, stride=96), :] for part in range(2)], axis=0)
+
+
+def first_kernel(fields_hbm, out_ref, fields_ref, sem):
+    copy = pltpu.make_async_copy(fields_hbm, fields_ref, sem)
+    copy.start()
+    copy.wait()
+    for block in range(RANKS):
+        for comp in range(3):
+            out_ref[block, comp] = read_rows(fields_ref, comp, block)
 
 
 def pack_kernel(
@@ -68,7 +78,9 @@
     damping_hbm,
     depths_hbm,
     links_ref,
+    _,
     out_ref,
+    depth_ref,
     fields_ref,
     forcing_ref,
     weights_ref,
@@ -84,42 +96,41 @@
     copies = [pltpu.make_async_copy(a, b, sems.at[i]) for i, (a, b) in enumerate(zip(sources, targets))]
     for copy in copies:
         copy.start()
-    first = lax.axis_index("node") * RANKS
+    node = lax.axis_index("node")
     for link in range(2):
         for b in range(RANKS):
-            local = (links_ref[2 + link, b] - first).astype(jnp.float32)
+            local = (links_ref[2 + link, b] - node * RANKS).astype(jnp.float32)
             at = ROW_LINKS + link
-            rows_ref[at, :, LANES * b : LANES * (b + 1)] = jnp.full((1, LANES), local, jnp.float32)
-    for group in range(6):
-        if group % 3 == 0:
-            copies[group // 3].wait()
-        source = (fields_ref, forcing_ref)[group // 3]
-
-        def block(b):
-            start = 32 * (group % 3) + 2 * b
-            parts = [source[pl.ds(start + part, 4, stride=96), :] for part in range(2)]
-            return jnp.concatenate(parts, axis=0)
-
-        pack_group(block, out_ref, group)
-    for copy in copies[2:]:
+            rows_ref[at : at + 1, LANES * b : LANES * (b + 1)] = jnp.full((1, LANES), local, jnp.float32)
+    for copy in copies:
         copy.wait()
-    for kind, source in enumerate((weights_ref, east_ref, north_ref)):
-        for link in range(4):
-            rows_ref[4 * kind + link] = source[link : link + 1, :]
-    rows_ref[ROW_DAMPING] = damping_ref[...]
-    rows_ref[ROW_DEPTHS] = depths_ref[...]
+    rows_ref[0:4, :] = weights_ref[...]
+    rows_ref[4:8, :] = east_ref[...]
+    rows_ref[8:12, :] = north_ref[...]
+    rows_ref[ROW_DAMPING : ROW_DAMPING + 1, :] = damping_ref[...]
+    rows_ref[ROW_DEPTHS : ROW_DEPTHS + 1, :] = depths_ref[...]
     mine = lax.axis_index("freq")
-    pack_group(lambda b: jnp.broadcast_to(rows_ref[mine, :, LANES * b : LANES * (b + 1)], (8, LANES)), out_ref, 6)
-
-
-def forward_kernel(given_ref, out_ref):
-    for half in range(2):
-        rows = jnp.concatenate([given_ref[8 * half + i, 6, 0:1] for i in range(8)], axis=0)
-        for rank in range(RANKS):
-            out_ref[rank, 3 + half] = rows
+    depth_ref[...] = depths_ref[:, pl.ds(pl.multiple_of(mine * LANES, LANES), LANES)]
+    for group in range(8):
+        if group < 6:
+            rows = [read_rows((forcing_ref, fields_ref)[group // 3], group % 3, b) for b in range(RANKS)]
+        else:
+            at = 8 * (group - 6)
+            rows = [rows_ref[at : at + 8, LANES * b : LANES * (b + 1)] for b in range(RANKS)]
+        for rank, row in enumerate(swap_blocks(rows)):
+            out_ref[rank, group] = row
+
+
+def turn_kernel(friction_ref, packed_ref, out_ref):
     for rank in range(RANKS):
-        for comp in range(3):
-            out_ref[rank, comp] = given_ref[rank, comp]
+        out_ref[rank, 0] = packed_ref[rank, 0]
+        for group in range(3, 8):
+            out_ref[rank, group] = packed_ref[rank, group]
+    for comp in range(2):
+        rows = swap_blocks([friction_ref[b, comp] for b in range(RANKS)])
+        for rank, row in enumerate(rows):
+            out_ref[rank, 1 + comp] = packed_ref[rank, 1 + comp] - row
+            out_ref[rank, FRICTION_AT + comp] = row
 
 
 def unpack_kernel(x_ref, fields_ref, residual_ref):
@@ -143,7 +154,7 @@
     analysis_ref[...] = (synthesis * jnp.where(harmonic == 0, 1.0 / SAMPLES, 2.0 / SAMPLES)).T
 
 
-def friction_kernel(x_ref, table_ref, synthesis_ref, analysis_ref, out_ref):
+def friction_kernel(x_ref, depth_ref, synthesis_ref, analysis_ref, out_ref):
     moments = [
         jnp.dot(
             synthesis_ref[...],
@@ -154,10 +165,7 @@
         for comp in range(3)
     ]
     elevation, eastward, northward = moments
-    group = lax.axis_index("freq")
-    depths = table_ref[ROW_DEPTHS, 3 + group // 8]
-    depth = jnp.sum(jnp.where(iota((8, LANES), 0) == group % 8, depths, 0.0), axis=0, keepdims=True)
-    column_depth = depth + 0.5 * jnp.tanh(elevation)
+    column_depth = depth_ref[...] + 0.5 * jnp.tanh(elevation)
     magnitude = jnp.sqrt(eastward * eastward + northward * northward + SPEED_FLOOR)
     factor = FRICTION * magnitude / column_depth
     for comp, moving in enumerate((eastward, northward)):
@@ -167,10 +175,11 @@
         out_ref[:, comp] = terms.reshape(RANKS, 8, LANES)
 
 
-def prepare_links(table_ref, links_ref, index_ref):
+def prepare_links(given_ref, links_ref, index_ref):
     share = iota((8, LANES), 1) & (SHARE - 1)
-    for half in range(2):
-        rows = [table_ref[at, 3 + half] for at in range(RANKS)]
+
+    def prepare(g, _):
+        rows = [jnp.broadcast_to(given_ref[g, COEFS_AT + at // 8, at % 8 : at % 8 + 1], (8, LANES)) for at in range(RANKS)]
         spread = rows[0] + rows[1] + rows[2] + rows[3]
         values = rows[:12] + [
             spread + (ETA_DAMP - SHIFT),
@@ -178,16 +187,16 @@
             rows[4] + rows[5] + rows[6] + rows[7],
             rows[8] + rows[9] + rows[10] + rows[11],
         ]
-        for i in range(8):
-            for at, value in enumerate(values):
-                links_ref[8 * half + i, at] = jnp.broadcast_to(value[i : i + 1], (8, LANES))
+        for at, value in enumerate(values):
+            links_ref[g, at] = value
         for link in range(2):
             at = rows[ROW_LINKS + link].astype(jnp.int32)
             outside = jnp.logical_or(at < 0, at > RANKS - 1)
             lane = (at & (RANKS - 1)) * SHARE + share
-            index = jnp.where(outside, lane + LANES, lane)
-            for i in range(8):
-                index_ref[8 * half + i, link] = jnp.broadcast_to(index[i : i + 1], (8, LANES))
+            index_ref[g, link] = jnp.where(outside, lane + LANES, lane)
+        return 0
+
+    lax.fori_loop(0, RANKS, prepare, 0)
 
 
 def apply_operator(vectors, links_ref, index_ref):
@@ -243,15 +252,17 @@
     return OMEGA_STEP * slot_rows(harmonic_ref, lambda ref, i: ref[i]).astype(jnp.float32)
 
 
-def start_kernel(given_ref, table_ref, harmonic_ref, base_ref, links_ref, index_ref):
-    prepare_links(table_ref, links_ref, index_ref)
+def first_basis_kernel(given_ref, harmonic_ref, basis_ref, gram_ref, links_ref, index_ref, depth_ref):
+    prepare_links(given_ref, links_ref, index_ref)
+    depth_ref[...] = given_ref[lax.axis_index("freq"), COEFS_AT + 1, ROW_DEPTHS - 8 : ROW_DEPTHS - 7]
     turn = angular_rows(harmonic_ref) * jnp.where(iota((8, LANES), 0) < 4, -1.0, 1.0)
-    vectors = [[given_ref[g, comp] for comp in range(3)] for g in range(RANKS)]
+    vectors = [[given_ref[g, FIELDS_AT + comp] for comp in range(3)] for g in range(RANKS)]
     images = apply_operator(vectors, links_ref, index_ref)
     for g in range(RANKS):
         for comp in range(3):
             rest = SHIFT * vectors[g][comp] + turn * pltpu.roll(vectors[g][comp], 4, 0)
-            base_ref[g, comp] = given_ref[g, 3 + comp] - images[g][comp] - rest
+            basis_ref[0, g, comp] = given_ref[g, comp] - images[g][comp] - rest
+    extend_basis(links_ref, index_ref, basis_ref, gram_ref)
 
 
 def basis_kernel(base_ref, friction_ref, links_ref, index_ref, basis_ref, gram_ref):
@@ -259,7 +270,10 @@
         basis_ref[0, g, 0] = base_ref[g, 0]
         basis_ref[0, g, 1] = base_ref[g, 1] - friction_ref[g, 0]
         basis_ref[0, g, 2] = base_ref[g, 2] - friction_ref[g, 1]
-
+    extend_basis(links_ref, index_ref, basis_ref, gram_ref)
+
+
+def extend_basis(links_ref, index_ref, basis_ref, gram_ref):
     def power(m, _):
         vectors = [[basis_ref[m, g, comp] for comp in range(3)] for g in range(RANKS)]
         images = apply_operator(vectors, links_ref, index_ref)
@@ -375,18 +389,19 @@
 def update_kernel(sweep, gram_ref, fields_ref, basis_ref, friction_ref, harmonic_ref, counts_ref, *outs):
     correction, residual = step_sizes(gram_ref, harmonic_ref, counts_ref, sweep)
     sign = jnp.where(iota((8, LANES), 0) < 4, -1.0, 1.0)
+    fields_at = FIELDS_AT if sweep == 0 else 0
 
     def update(g, _):
         for comp in range(3):
             vectors = [basis_ref[m, g, comp] for m in range(COUNT)]
-            fields = fields_ref[g, comp] + combine(correction, vectors[:LMAX], sign)
+            fields = fields_ref[g, fields_at + comp] + combine(correction, vectors[:LMAX], sign)
             left = combine(residual, vectors, sign)
             if sweep == SWEEPS - 1:
                 outs[0][g, comp] = fields
                 outs[0][g, 3 + comp] = left
             else:
                 outs[0][g, comp] = fields
-                outs[1][g, comp] = left if comp == 0 else left + friction_ref[g, comp - 1]
+                outs[1][g, comp] = left if comp == 0 else left + friction_ref[g, FRICTION_AT + comp - 1]
         return 0
 
     lax.fori_loop(0, RANKS, update, 0)
@@ -396,13 +411,13 @@
     return jax.ShapeDtypeStruct(shape, jnp.float32)
 
 
-def call(kernel, out, specs, scratch=(), mebibytes=16):
+def call(kernel, out, specs, scratch=(), mebibytes=16, out_specs=None):
     outs = out if isinstance(out, list) else [out]
     result = pl.pallas_call(
         kernel,
         out_shape=outs,
         in_specs=specs,
-        out_specs=[VMEM] * len(outs),
+        out_specs=out_specs or [VMEM] * len(outs),
         scratch_shapes=list(scratch),
         compiler_params=pltpu.CompilerParams(vmem_limit_bytes=mebibytes * 1024 * 1024),
     )
@@ -427,10 +442,25 @@
     whole = pltpu.VMEM((384, LANES), jnp.float32)
     four = pltpu.VMEM((4, 2048), jnp.float32)
     line = pltpu.VMEM((1, 2048), jnp.float32)
-    packed = call(
+    fields_rows = rows_of(harmonics)
+    first = call(
+        first_kernel, struct(RANKS, 3, 8, LANES), [HBM], (whole, pltpu.SemaphoreType.DMA(())), 58
+    )(fields_rows)
+    received = exchange(first, "freq")
+
+    slots = jnp.broadcast_to(harmonic_of_slot.reshape(RANKS, 1, 4), (RANKS, 2, 4)).reshape(1, LANES)
+    cosines = np.cos(np.arange(SAMPLES) * (2.0 * math.pi / SAMPLES)).astype(np.float32).reshape(1, SAMPLES)
+    synthesis, analysis = call(tables_kernel, [struct(SAMPLES, LANES), struct(LANES, SAMPLES)], [VMEM] * 2)(
+        slots, cosines
+    )
+
+    def friction_of(received, depth):
+        return call(friction_kernel, struct(RANKS, 2, 8, LANES), [VMEM] * 4)(received, depth, synthesis, analysis)
+
+    packed, depth = call(
         pack_kernel,
-        struct(RANKS, 7, 8, LANES),
-        [HBM] * 7 + [SMEM],
+        [struct(RANKS, 8, 8, LANES), struct(1, LANES)],
+        [HBM] * 7 + [SMEM, HBM],
         (
             whole,
             whole,
@@ -439,12 +469,12 @@
             four,
             line,
             line,
-            pltpu.VMEM((RANKS, 1, 2048), jnp.float32),
+            pltpu.VMEM((RANKS, 2048), jnp.float32),
             pltpu.SemaphoreType.DMA((7,)),
         ),
         58,
     )(
-        rows_of(harmonics),
+        fields_rows,
         rows_of(forcing),
         weights,
         couple_east,
@@ -452,47 +482,27 @@
         damping.reshape(1, -1),
         depths.reshape(1, -1),
         connections.T,
+        first,
     )
+    friction = exchange(friction_of(received, depth), "freq")
+    packed = call(turn_kernel, struct(RANKS, 10, 8, LANES), [VMEM] * 2)(friction, packed)
     given = exchange(packed, "node")
-    table = exchange(call(forward_kernel, struct(RANKS, 5, 8, LANES), [VMEM])(given), "freq")
-
-    slots = jnp.broadcast_to(harmonic_of_slot.reshape(RANKS, 1, 4), (RANKS, 2, 4)).reshape(1, LANES)
-    cosines = np.cos(np.arange(SAMPLES) * (2.0 * math.pi / SAMPLES)).astype(np.float32).reshape(1, SAMPLES)
-
-    synthesis, analysis = call(tables_kernel, [struct(SAMPLES, LANES), struct(LANES, SAMPLES)], [VMEM] * 2)(
-        slots, cosines
+
+    basis_out = [struct(COUNT, RANKS, 3, 8, LANES), struct(RANKS, 2, LANES)]
+    links_out = [struct(RANKS, 16, 8, LANES), jax.ShapeDtypeStruct((RANKS, 2, 8, LANES), jnp.int32), struct(1, LANES)]
+    basis, gram, links, index, depth = call(first_basis_kernel, basis_out + links_out, [VMEM, SMEM])(
+        given, harmonic_of_slot
     )
 
-    def friction_of(received):
-        terms = call(friction_kernel, struct(RANKS, 2, 8, LANES), [VMEM] * 4)(received, table, synthesis, analysis)
-        return exchange(terms, "freq")
-
-    base, links, index = call(
-        start_kernel,
-        [
-            struct(RANKS, 3, 8, LANES),
-            struct(RANKS, 16, 8, LANES),
-            jax.ShapeDtypeStruct((RANKS, 2, 8, LANES), jnp.int32),
-        ],
-        [VMEM, VMEM, SMEM],
-    )(given, table, harmonic_of_slot)
-    fields = given
-    friction = friction_of(table)
-    for sweep in range(SWEEPS):
-        basis, gram = call(
-            basis_kernel, [struct(COUNT, RANKS, 3, 8, LANES), struct(RANKS, 2, LANES)], [VMEM] * 4
-        )(base, friction, links, index)
-        gram = exchange(gram, "node")
-        if sweep < SWEEPS - 1:
-            outs = [struct(RANKS, 3, 8, LANES), struct(RANKS, 3, 8, LANES)]
-        else:
-            outs = [struct(RANKS, 6, 8, LANES)]
-        results = call(functools.partial(update_kernel, sweep), outs, [VMEM] * 4 + [SMEM] * 2)(
-            gram, fields, basis, friction, harmonic_of_slot, counts
+    def update(sweep, outs, gram, fields, basis):
+        return call(functools.partial(update_kernel, sweep), outs, [VMEM] * 4 + [SMEM] * 2)(
+            exchange(gram, "node"), fields, basis, given, harmonic_of_slot, counts
         )
-        if sweep < SWEEPS - 1:
-            fields, base = results
-            friction = friction_of(exchange(fields, "freq"))
+
+    fields, base = update(0, [struct(RANKS, 3, 8, LANES)] * 2, gram, given, basis)
+    friction = exchange(friction_of(exchange(fields, "freq"), depth), "freq")
+    basis, gram = call(basis_kernel, basis_out, [VMEM] * 4)(base, friction, links, index)
+    results = update(1, [struct(RANKS, 6, 8, LANES)], gram, fields, basis)
     out = [struct(384, LANES)] * 2
     fields, residual = call(unpack_kernel, out, [VMEM])(exchange(results[0], "node"))
     return (fields_of(fields), fields_of(residual))

time: 134 us -> 137 us (1.022)
  blocking collectives: 87.6 us -> 103 us
  waiting for transfers between devices: 14.6 us -> 1.5 us
  local copies, waits for them, and re-layouts: 0.22 us -> 3.22 us
  starting transfers between devices: 10.3 us -> 7.6 us
    all_to_all x6 -> x7, blocking collectives: 87.6 us -> 103 us  [exchange(): return lax.all_to_all(values, axis, split_axis=0, concat_axis=0, tiled=True)]
    all_to_all x2 -> x1, waiting for transfers between devices: 14.6 us -> 1.5 us  [exchange(): return lax.all_to_all(values, axis, split_axis=0, concat_axis=0, tiled=True)]
    pallas_call x7, Pallas kernels: 13.3 us -> 17.4 us  [call(): result(*args)]
    pallas_call x4, Pallas kernels: 6.2 us -> 3.26 us  [call(): result(*args)[0]]
    all_to_all x2 -> x1, starting transfers between devices: 10.3 us -> 7.6 us  [exchange(): return lax.all_to_all(values, axis, split_axis=0, concat_axis=0, tiled=True)]
    unnamed x6 -> x10, local copies, waits for them, and re-layouts: 0.02 us -> 2.36 us
  transfers between devices with their start and end apart: 2 -> 1, of which waited for: 2 -> 1; matrix products, arithmetic and copies ran while one was open for 0% -> 1% of each run, Pallas kernels for 1% -> 3%
where the time goes in v2:
time: 137 us
  blocking collectives  103 us (75%)
  Pallas kernels  20.7 us (15%)
  starting transfers between devices  7.6 us (6%)
  local copies, waits for them, and re-layouts  3.22 us (2%)
  waiting for transfers between devices  1.5 us (1%)
    all_to_all x7, blocking collectives, exchange(): return lax.all_to_all(values, axis, split_axis=0, concat_axis=0, tiled=True)  103 us
    pallas_call x7, Pallas kernels, call(): result(*args)  17.4 us
    all_to_all x1, starting transfers between devices, exchange(): return lax.all_to_all(values, axis, split_axis=0, concat_axis=0, tiled=True)  7.6 us
    pallas_call x4, Pallas kernels, call(): result(*args)[0]  3.26 us
  transfers between devices with their start and end apart: 1, of which 1 were waited for; matrix products, arithmetic and copies ran while one was open for 1% of the time, Pallas kernels for 3%

profile of v2, /device:TPU:1, one launch (start us, length us, event | category | flops | bytes accessed | tf_op | source)
XLA Modules:
  0.0 136.6 jit_solution(15572866828113146390)
XLA Ops:
  0.6 1.7 %shard_map.122._ = f32[16,3,8,128]{3,2,1,0:T(8,128)} custom-call(f32[384,128]{1,0:T(8,128)} %bitcast.27), custom_call_target="tpu_custom_call" | custom-call | tf_op jit(solution)/shard_map/pallas_call | solution.py:424
  2.4 7.6 %all-to-all-start = ((f32[16,3,8,128]{3,2,1,0:T(8,128)}), f32[16,3,8,128]{3,2,1,0:T(8,128)S(1)}, u32[]{:S(2)}, u32[]{:S(2)}) async-start(f32[16,3,8,128]{3,2,1,0:T(8,128)} %shard_map.122._), calls=%async_computation | async-start | bytes 393216 | tf_op jit(solution)/shard_map/all_to_all | solution.py:428
  10.0 0.7 broadcast_in_dim.7
  10.7 0.1 reshape.45.harmonic_ref
  10.9 0.0 copy-start.4
  10.9 0.6 copy-done.4
  11.5 0.2 shard_map.124
  11.7 4.0 %shard_map.123 = (f32[16,8,8,128]{3,2,1,0:T(8,128)}, f32[1,128]{1,0:T(1,128)}) custom-call(f32[384,128]{1,0:T(8,128)} %bitcast.28, f32[384,128]{1,0:T(8,128)} %bitcast.29, f32[4,2048]{1,0:T(4,128)} %weights_hbm.1, f32[4,2048]{1,0:T(4,128)} %east_hbm.1, f32[4,2048]{1,0:T(4,128)} %north_hbm.1, f32[1,2048]{1,0:T(1,128)} %bitcast.30, f32[1,2048]{1,0:T(1,128)} %bitcast.31, ...), custom_call_target="tpu_custom_call" | custom-call | tf_op jit(solution)/shard_map/pallas_call | solution.py:424
  15.7 1.5 %all-to-all-done.x_ref = f32[16,3,8,128]{3,2,1,0:T(8,128)S(1)} async-done(((f32[16,3,8,128]{3,2,1,0:T(8,128)}), f32[16,3,8,128]{3,2,1,0:T(8,128)S(1)}, u32[]{:S(2)}, u32[]{:S(2)}) %all-to-all-start) | async-done | bytes 196640 | tf_op jit(solution)/shard_map/all_to_all | solution.py:428
  17.2 0.0 copy-start.3
  17.2 0.7 copy-done.3
  17.8 0.6 shard_map.125
  18.4 11.8 %all_to_all.40.friction_ref = f32[16,2,8,128]{3,2,1,0:T(8,128)S(1)} all-to-all(f32[16,2,8,128]{3,2,1,0:T(8,128)S(1)} %shard_map.125), channel_id=1, replica_groups=mesh['freq'=16,'node'=16] {'freq'}, dimensions={0} | all-to-all | bytes 262144 | tf_op jit(solution)/shard_map/all_to_all | solution.py:428
  30.3 0.0 copy-start
  30.3 1.0 copy-done
  31.3 0.0 copy-start.1
  31.3 0.3 shard_map.126
  31.6 0.0 copy-start.2
  31.6 31.2 %all_to_all.41.given_ref.fields_ref.friction_ref = f32[16,10,8,128]{3,2,1,0:T(8,128)S(1)} all-to-all(f32[16,10,8,128]{3,2,1,0:T(8,128)S(1)} %shard_map.126), channel_id=1, replica_groups=mesh['freq'=16,'node'=16] {'node'}, dimensions={0} | all-to-all | bytes 1310720 | tf_op jit(solution)/shard_map/all_to_all | solution.py:428
  62.8 0.0 copy-done.1
  62.8 5.1 %shard_map.127 = (f32[6,16,3,8,128]{4,3,2,1,0:T(8,128)S(1)}, f32[16,2,128]{2,1,0:T(2,128)S(1)}, f32[16,16,8,128]{3,2,1,0:T(8,128)S(1)}, s32[16,2,8,128]{3,2,1,0:T(8,128)S(1)}, f32[1,128]{1,0:T(1,128)S(1)}) custom-call(f32[16,10,8,128]{3,2,1,0:T(8,128)S(1)} %all_to_all.41.given_ref.fields_ref.friction_ref, s32[64]{0:T(128)S(1)} %copy-done.1), custom_call_target="tpu_custom_call" | custom-call | tf_op jit(solution)/shard_map/pallas_call | solution.py:424
  67.9 9.9 %all_to_all.42.gram_ref = f32[16,2,128]{2,1,0:T(2,128)S(1)} all-to-all(f32[16,2,128]{2,1,0:T(2,128)S(1)} %get-tuple-element.21), channel_id=1, replica_groups=mesh['freq'=16,'node'=16] {'node'}, dimensions={0} | all-to-all | bytes 32768 | tf_op jit(solution)/shard_map/all_to_all | solution.py:428
  77.8 0.0 copy-done.2
  77.8 1.4 %shard_map.128 = (f32[16,3,8,128]{3,2,1,0:T(8,128)S(1)}, f32[16,3,8,128]{3,2,1,0:T(8,128)S(1)}) custom-call(f32[16,2,128]{2,1,0:T(2,128)S(1)} %all_to_all.42.gram_ref, f32[16,10,8,128]{3,2,1,0:T(8,128)S(1)} %all_to_all.41.given_ref.fields_ref.friction_ref, f32[6,16,3,8,128]{4,3,2,1,0:T(8,128)S(1)} %get-tuple-element.22.basis_ref, ...), custom_call_target="tpu_custom_call" | custom-call | tf_op jit(solution)/shard_map/pallas_call | solution.py:424
  79.2 10.0 %all_to_all.43.x_ref = f32[16,3,8,128]{3,2,1,0:T(8,128)S(1)} all-to-all(f32[16,3,8,128]{3,2,1,0:T(8,128)S(1)} %get-tuple-element.24.fields_ref), channel_id=1, replica_groups=mesh['freq'=16,'node'=16] {'freq'}, dimensions={0} | all-to-all | bytes 393216 | tf_op jit(solution)/shard_map/all_to_all | solution.py:428
  89.2 0.6 shard_map.129
  89.8 9.8 %all_to_all.44.friction_ref = f32[16,2,8,128]{3,2,1,0:T(8,128)S(1)} all-to-all(f32[16,2,8,128]{3,2,1,0:T(8,128)S(1)} %shard_map.129), channel_id=1, replica_groups=mesh['freq'=16,'node'=16] {'freq'}, dimensions={0} | all-to-all | bytes 262144 | tf_op jit(solution)/shard_map/all_to_all | solution.py:428
  99.7 3.8 %shard_map.130 = (f32[6,16,3,8,128]{4,3,2,1,0:T(8,128)S(1)}, f32[16,2,128]{2,1,0:T(2,128)S(1)}) custom-call(f32[16,3,8,128]{3,2,1,0:T(8,128)S(1)} %get-tuple-element.23.base_ref, f32[16,2,8,128]{3,2,1,0:T(8,128)S(1)} %all_to_all.44.friction_ref, f32[16,16,8,128]{3,2,1,0:T(8,128)S(1)} %get-tuple-element.26.links_ref, ...), custom_call_target="tpu_custom_call" | custom-call | tf_op jit(solution)/shard_map/pallas_call | solution.py:424
  103.4 12.8 %all_to_all.45.gram_ref = f32[16,2,128]{2,1,0:T(2,128)S(1)} all-to-all(f32[16,2,128]{2,1,0:T(2,128)S(1)} %get-tuple-element.28), channel_id=1, replica_groups=mesh['freq'=16,'node'=16] {'node'}, dimensions={0} | all-to-all | bytes 32768 | tf_op jit(solution)/shard_map/all_to_all | solution.py:428
  116.2 1.4 %shard_map.131 = f32[16,6,8,128]{3,2,1,0:T(8,128)S(1)} custom-call(f32[16,2,128]{2,1,0:T(2,128)S(1)} %all_to_all.45.gram_ref, f32[16,3,8,128]{3,2,1,0:T(8,128)S(1)} %get-tuple-element.24.fields_ref, f32[6,16,3,8,128]{4,3,2,1,0:T(8,128)S(1)} %get-tuple-element.29.basis_ref, f32[16,10,8,128]{3,2,1,0:T(8,128)S(1)} %all_to_all.41.given_ref.fields_ref.friction_ref, ...), custom_call_target="tpu_custom_call" | custom-call | tf_op jit(solution)/shard_map/pallas_call | solution.py:424
  117.6 17.4 %all_to_all.46.x_ref = f32[16,6,8,128]{3,2,1,0:T(8,128)S(1)} all-to-all(f32[16,6,8,128]{3,2,1,0:T(8,128)S(1)} %shard_map.131), channel_id=1, replica_groups=mesh['freq'=16,'node'=16] {'node'}, dimensions={0} | all-to-all | bytes 786432 | tf_op jit(solution)/shard_map/all_to_all | solution.py:428
  135.0 1.6 %shard_map.132 = (f32[384,128]{1,0:T(8,128)}, f32[384,128]{1,0:T(8,128)}) custom-call(f32[16,6,8,128]{3,2,1,0:T(8,128)S(1)} %all_to_all.46.x_ref), custom_call_target="tpu_custom_call" | custom-call | tf_op jit(solution)/shard_map/pallas_call | solution.py:424
  (1 shorter events, 0.0 us)
Async XLA Ops:
  2.4 14.8 %all-to-all-start = ((f32[16,3,8,128]{3,2,1,0:T(8,128)}), f32[16,3,8,128]{3,2,1,0:T(8,128)S(1)}, u32[]{:S(2)}, u32[]{:S(2)}) async-start(f32[16,3,8,128]{3,2,1,0:T(8,128)} %shard_map.122._), calls=%async_computation | async-start | bytes 393216 | tf_op jit(solution)/shard_map/all_to_all | solution.py:428
  10.9 0.7 copy-start.4
  17.2 0.7 copy-start.3
  30.3 1.0 copy-start
  31.3 31.5 %copy-start.1 = (s32[64]{0:T(128)S(1)}, s32[64]{0:T(128)}, u32[]{:S(2)}) copy-start(s32[64]{0:T(128)} %harmonic_ref.5) | copy-start | bytes 772
  31.6 46.2 %copy-start.2 = (s32[2,64]{1,0:T(2,128)S(1)}, s32[2,64]{1,0:T(2,128)}, u32[]{:S(2)}) copy-start(s32[2,64]{1,0:T(2,128)} %counts_ref.3) | copy-start | bytes 1540

commit v3 on v1

--- a/solution.py
+++ b/solution.py
@@ -23,7 +23,6 @@
 RANKS = 16
 LANES = 128
 SHARE = 8
-SHIFT = 2.5
 COUNT = LMAX + 1
 REAL_PAIRS = [(m, n) for m in range(COUNT) for n in range(m, COUNT)]
 IMAG_PAIRS = [(m, n) for m in range(COUNT) for n in range(m + 1, COUNT)]
@@ -68,7 +67,7 @@
     damping_hbm,
     depths_hbm,
     links_ref,
-    out_ref,
+    out_hbm,
     fields_ref,
     forcing_ref,
     weights_ref,
@@ -77,7 +76,9 @@
     damping_ref,
     depths_ref,
     rows_ref,
+    out_ref,
     sems,
+    out_sems,
 ):
     sources = (fields_hbm, forcing_hbm, weights_hbm, east_hbm, north_hbm, damping_hbm, depths_hbm)
     targets = (fields_ref, forcing_ref, weights_ref, east_ref, north_ref, damping_ref, depths_ref)
@@ -90,6 +91,14 @@
             local = (links_ref[2 + link, b] - first).astype(jnp.float32)
             at = ROW_LINKS + link
             rows_ref[at, :, LANES * b : LANES * (b + 1)] = jnp.full((1, LANES), local, jnp.float32)
+    sent = []
+
+    def send(index, group, count):
+        part = pl.ds(group, count)
+        copy = pltpu.make_async_copy(out_ref.at[:, part], out_hbm.at[:, part], out_sems.at[index])
+        copy.start()
+        sent.append(copy)
+
     for group in range(6):
         if group % 3 == 0:
             copies[group // 3].wait()
@@ -101,6 +110,8 @@
             return jnp.concatenate(parts, axis=0)
 
         pack_group(block, out_ref, group)
+        if group % 3 == 2:
+            send(group // 3, group - 2, 3)
     for copy in copies[2:]:
         copy.wait()
     for kind, source in enumerate((weights_ref, east_ref, north_ref)):
@@ -109,7 +120,15 @@
     rows_ref[ROW_DAMPING] = damping_ref[...]
     rows_ref[ROW_DEPTHS] = depths_ref[...]
     mine = lax.axis_index("freq")
-    pack_group(lambda b: jnp.broadcast_to(rows_ref[mine, :, LANES * b : LANES * (b + 1)], (8, LANES)), out_ref, 6)
+    rows = [jnp.broadcast_to(rows_ref[mine, :, LANES * b : LANES * (b + 1)], (8, LANES)) for b in range(RANKS)]
+    diagonal = jnp.sum(weights_ref[...], axis=0, keepdims=True) + (2.0 / 3.0) * damping_ref[...] + ETA_DAMP / 3.0
+    mean = jnp.sum(diagonal, axis=1, keepdims=True) * (1.0 / diagonal.shape[1])
+    top = iota((8, LANES), 0) == 0
+    for rank, row in enumerate(swap_blocks(rows)):
+        out_ref[rank, 6] = jnp.where(top, row, mean)
+    send(2, 6, 1)
+    for copy in sent:
+        copy.wait()
 
 
 def forward_kernel(given_ref, out_ref):
@@ -122,14 +141,18 @@
             out_ref[rank, comp] = given_ref[rank, comp]
 
 
-def unpack_kernel(x_ref, fields_ref, residual_ref):
-    for group in range(6):
-        target = fields_ref if group < 3 else residual_ref
-        comp = group % 3
-        rows = swap_blocks([x_ref[rank, group] for rank in range(RANKS)])
-        for b, row in enumerate(rows):
-            for part in range(2):
-                target[pl.ds(32 * comp + 2 * b + part, 4, stride=96), :] = row[4 * part : 4 * part + 4]
+def unpack_kernel(x_ref, fields_hbm, residual_hbm, fields_ref, residual_ref, sems):
+    copies = []
+    for i, (target, out) in enumerate(((fields_ref, fields_hbm), (residual_ref, residual_hbm))):
+        for comp in range(3):
+            rows = swap_blocks([x_ref[rank, 3 * i + comp] for rank in range(RANKS)])
+            for b, row in enumerate(rows):
+                for part in range(2):
+                    target[pl.ds(32 * comp + 2 * b + part, 4, stride=96), :] = row[4 * part : 4 * part + 4]
+        copies.append(pltpu.make_async_copy(target, out, sems.at[i]))
+        copies[-1].start()
+    for copy in copies:
+        copy.wait()
 
 
 def tables_kernel(harmonic_ref, cosines_ref, synthesis_ref, analysis_ref):
@@ -167,14 +190,14 @@
         out_ref[:, comp] = terms.reshape(RANKS, 8, LANES)
 
 
-def prepare_links(table_ref, links_ref, index_ref):
+def prepare_links(table_ref, shift, links_ref, index_ref):
     share = iota((8, LANES), 1) & (SHARE - 1)
     for half in range(2):
         rows = [table_ref[at, 3 + half] for at in range(RANKS)]
         spread = rows[0] + rows[1] + rows[2] + rows[3]
         values = rows[:12] + [
-            spread + (ETA_DAMP - SHIFT),
-            spread + (rows[ROW_DAMPING] - SHIFT),
+            spread + (ETA_DAMP - shift),
+            spread + (rows[ROW_DAMPING] - shift),
             rows[4] + rows[5] + rows[6] + rows[7],
             rows[8] + rows[9] + rows[10] + rows[11],
         ]
@@ -243,14 +266,19 @@
     return OMEGA_STEP * slot_rows(harmonic_ref, lambda ref, i: ref[i]).astype(jnp.float32)
 
 
-def start_kernel(given_ref, table_ref, harmonic_ref, base_ref, links_ref, index_ref):
-    prepare_links(table_ref, links_ref, index_ref)
+def start_kernel(given_ref, table_ref, harmonic_ref, base_ref, links_ref, index_ref, shift_ref):
+    shift = given_ref[0, 6, 1:2]
+    for g in range(1, RANKS):
+        shift = shift + given_ref[g, 6, 1:2]
+    shift = jnp.broadcast_to(shift * (1.0 / RANKS), (8, LANES))
+    shift_ref[...] = shift
+    prepare_links(table_ref, shift, links_ref, index_ref)
     turn = angular_rows(harmonic_ref) * jnp.where(iota((8, LANES), 0) < 4, -1.0, 1.0)
     vectors = [[given_ref[g, comp] for comp in range(3)] for g in range(RANKS)]
     images = apply_operator(vectors, links_ref, index_ref)
     for g in range(RANKS):
         for comp in range(3):
-            rest = SHIFT * vectors[g][comp] + turn * pltpu.roll(vectors[g][comp], 4, 0)
+            rest = shift * vectors[g][comp] + turn * pltpu.roll(vectors[g][comp], 4, 0)
             base_ref[g, comp] = given_ref[g, 3 + comp] - images[g][comp] - rest
 
 
@@ -292,7 +320,7 @@
         gram_ref[rank] = packed
 
 
-def step_sizes(gram_ref, harmonic_ref, counts_ref, sweep):
+def step_sizes(gram_ref, shift, harmonic_ref, counts_ref, sweep):
     gram = gram_ref[0]
     for rank in range(1, RANKS):
         gram = gram + gram_ref[rank]
@@ -336,7 +364,7 @@
             value = (zero, zero)
             if m <= step:
                 r = residual[m]
-                value = (SHIFT * r[0] - angular * r[1], SHIFT * r[1] + angular * r[0])
+                value = (shift * r[0] - angular * r[1], shift * r[1] + angular * r[0])
             if m > 0:
                 value = add(value, residual[m - 1])
             image.append(value)
@@ -372,8 +400,8 @@
     return straight + sign * pltpu.roll(turned, 4, 0)
 
 
-def update_kernel(sweep, gram_ref, fields_ref, basis_ref, friction_ref, harmonic_ref, counts_ref, *outs):
-    correction, residual = step_sizes(gram_ref, harmonic_ref, counts_ref, sweep)
+def update_kernel(sweep, gram_ref, fields_ref, basis_ref, friction_ref, shift_ref, harmonic_ref, counts_ref, *outs):
+    correction, residual = step_sizes(gram_ref, shift_ref[...], harmonic_ref, counts_ref, sweep)
     sign = jnp.where(iota((8, LANES), 0) < 4, -1.0, 1.0)
 
     def update(g, _):
@@ -396,13 +424,13 @@
     return jax.ShapeDtypeStruct(shape, jnp.float32)
 
 
-def call(kernel, out, specs, scratch=(), mebibytes=16):
+def call(kernel, out, specs, scratch=(), mebibytes=16, out_specs=None):
     outs = out if isinstance(out, list) else [out]
     result = pl.pallas_call(
         kernel,
         out_shape=outs,
         in_specs=specs,
-        out_specs=[VMEM] * len(outs),
+        out_specs=out_specs or [VMEM] * len(outs),
         scratch_shapes=list(scratch),
         compiler_params=pltpu.CompilerParams(vmem_limit_bytes=mebibytes * 1024 * 1024),
     )
@@ -440,9 +468,12 @@
             line,
             line,
             pltpu.VMEM((RANKS, 1, 2048), jnp.float32),
+            pltpu.VMEM((RANKS, 7, 8, LANES), jnp.float32),
             pltpu.SemaphoreType.DMA((7,)),
+            pltpu.SemaphoreType.DMA((3,)),
         ),
         58,
+        [HBM],
     )(
         rows_of(harmonics),
         rows_of(forcing),
@@ -467,12 +498,13 @@
         terms = call(friction_kernel, struct(RANKS, 2, 8, LANES), [VMEM] * 4)(received, table, synthesis, analysis)
         return exchange(terms, "freq")
 
-    base, links, index = call(
+    base, links, index, shift = call(
         start_kernel,
         [
             struct(RANKS, 3, 8, LANES),
             struct(RANKS, 16, 8, LANES),
             jax.ShapeDtypeStruct((RANKS, 2, 8, LANES), jnp.int32),
+            struct(8, LANES),
         ],
         [VMEM, VMEM, SMEM],
     )(given, table, harmonic_of_slot)
@@ -487,14 +519,16 @@
             outs = [struct(RANKS, 3, 8, LANES), struct(RANKS, 3, 8, LANES)]
         else:
             outs = [struct(RANKS, 6, 8, LANES)]
-        results = call(functools.partial(update_kernel, sweep), outs, [VMEM] * 4 + [SMEM] * 2)(
-            gram, fields, basis, friction, harmonic_of_slot, counts
+        results = call(functools.partial(update_kernel, sweep), outs, [VMEM] * 5 + [SMEM] * 2)(
+            gram, fields, basis, friction, shift, harmonic_of_slot, counts
         )
         if sweep < SWEEPS - 1:
             fields, base = results
             friction = friction_of(exchange(fields, "freq"))
     out = [struct(384, LANES)] * 2
-    fields, residual = call(unpack_kernel, out, [VMEM])(exchange(results[0], "node"))
+    fields, residual = call(
+        unpack_kernel, out, [VMEM], (whole, whole, pltpu.SemaphoreType.DMA((2,))), 16, [HBM] * 2
+    )(exchange(results[0], "node"))
     return (fields_of(fields), fields_of(residual))
 
 

time: 134 us -> 133 us (level)
  no operation moved by 1% of the time
where the time goes in v3:
time: 133 us
  blocking collectives  87.6 us (66%)
  Pallas kernels  19.4 us (15%)
  waiting for transfers between devices  14.6 us (11%)
  starting transfers between devices  10.3 us (8%)
    all_to_all x6, blocking collectives, exchange(): return lax.all_to_all(values, axis, split_axis=0, concat_axis=0, tiled=True)  87.6 us
    all_to_all x2, waiting for transfers between devices, exchange(): return lax.all_to_all(values, axis, split_axis=0, concat_axis=0, tiled=True)  14.6 us
    pallas_call x7, Pallas kernels, call(): result(*args)  13.3 us
    all_to_all x2, starting transfers between devices, exchange(): return lax.all_to_all(values, axis, split_axis=0, concat_axis=0, tiled=True)  10.3 us
    pallas_call x4, Pallas kernels, call(): result(*args)[0]  6.09 us
  transfers between devices with their start and end apart: 2, of which 2 were waited for; matrix products, arithmetic and copies ran while one was open for 0% of the time, Pallas kernels for 1%

profile of v3, /device:TPU:1, one launch (start us, length us, event | category | flops | bytes accessed | tf_op | source)
XLA Modules:
  0.0 132.9 jit_solution(6851257832654444681)
XLA Ops:
  0.6 3.5 %shard_map.122 = f32[16,7,8,128]{3,2,1,0:T(8,128)} custom-call(f32[384,128]{1,0:T(8,128)} %bitcast.27, f32[384,128]{1,0:T(8,128)} %bitcast.28, f32[4,2048]{1,0:T(4,128)} %weights_hbm.1, f32[4,2048]{1,0:T(4,128)} %east_hbm.1, f32[4,2048]{1,0:T(4,128)} %north_hbm.1, f32[1,2048]{1,0:T(1,128)} %bitcast.29, f32[1,2048]{1,0:T(1,128)} %bitcast.30, s32[4,16]{1,0:T(4,128)} %bitcast.31), custom_call_target="tpu_custom_call" | custom-call | tf_op jit(solution)/shard_map/pallas_call | solution.py:437
  4.1 0.0 copy-start
  4.1 0.0 copy-start.2
  4.1 26.0 %all_to_all.40.given_ref.fields_ref = f32[16,7,8,128]{3,2,1,0:T(8,128)S(1)} all-to-all(f32[16,7,8,128]{3,2,1,0:T(8,128)} %shard_map.122), channel_id=1, replica_groups=mesh['freq'=16,'node'=16] {'node'}, dimensions={0} | all-to-all | bytes 917504 | tf_op jit(solution)/shard_map/all_to_all | solution.py:441
  30.1 0.7 shard_map.123
  30.9 6.8 %all-to-all-start.1 = ((f32[16,5,8,128]{3,2,1,0:T(8,128)}), f32[16,5,8,128]{3,2,1,0:T(8,128)S(1)}, u32[]{:S(2)}, u32[]{:S(2)}) async-start(f32[16,5,8,128]{3,2,1,0:T(8,128)} %shard_map.123), calls=%async_computation.1 | async-start | bytes 655360 | tf_op jit(solution)/shard_map/all_to_all | solution.py:441
  37.6 0.0 copy-done
  37.6 0.1 broadcast_in_dim.7
  37.7 0.1 reshape.45.harmonic_ref
  37.8 0.0 copy-done.2
  37.9 0.2 shard_map.125
  38.0 9.0 %all-to-all-done.1.table_ref.x_ref = f32[16,5,8,128]{3,2,1,0:T(8,128)S(1)} async-done(((f32[16,5,8,128]{3,2,1,0:T(8,128)}), f32[16,5,8,128]{3,2,1,0:T(8,128)S(1)}, u32[]{:S(2)}, u32[]{:S(2)}) %all-to-all-start.1) | async-done | bytes 327712 | tf_op jit(solution)/shard_map/all_to_all | solution.py:441
  47.0 1.3 shard_map.126
  48.2 3.5 %all-to-all-start.2 = ((f32[16,2,8,128]{3,2,1,0:T(8,128)}), f32[16,2,8,128]{3,2,1,0:T(8,128)S(1)}, u32[]{:S(2)}, u32[]{:S(2)}) async-start(f32[16,2,8,128]{3,2,1,0:T(8,128)} %shard_map.126), calls=%async_computation.2 | async-start | bytes 262144 | tf_op jit(solution)/shard_map/all_to_all | solution.py:441
  51.8 0.0 copy-start.1
  51.8 1.1 shard_map.124
  52.9 5.7 %all-to-all-done.2.friction_ref = f32[16,2,8,128]{3,2,1,0:T(8,128)S(1)} async-done(((f32[16,2,8,128]{3,2,1,0:T(8,128)}), f32[16,2,8,128]{3,2,1,0:T(8,128)S(1)}, u32[]{:S(2)}, u32[]{:S(2)}) %all-to-all-start.2) | async-done | bytes 131104 | tf_op jit(solution)/shard_map/all_to_all | solution.py:441
  58.6 3.8 %shard_map.127 = (f32[6,16,3,8,128]{4,3,2,1,0:T(8,128)S(1)}, f32[16,2,128]{2,1,0:T(2,128)S(1)}) custom-call(f32[16,3,8,128]{3,2,1,0:T(8,128)S(1)} %get-tuple-element.16.base_ref, f32[16,2,8,128]{3,2,1,0:T(8,128)S(1)} %all-to-all-done.2.friction_ref, f32[16,16,8,128]{3,2,1,0:T(8,128)S(1)} %get-tuple-element.19.links_ref, ...), custom_call_target="tpu_custom_call" | custom-call | tf_op jit(solution)/shard_map/pallas_call | solution.py:437
  62.4 11.7 %all_to_all.41.gram_ref = f32[16,2,128]{2,1,0:T(2,128)S(1)} all-to-all(f32[16,2,128]{2,1,0:T(2,128)S(1)} %get-tuple-element.21), channel_id=1, replica_groups=mesh['freq'=16,'node'=16] {'node'}, dimensions={0} | all-to-all | bytes 32768 | tf_op jit(solution)/shard_map/all_to_all | solution.py:441
  74.1 0.0 copy-done.1
  74.1 1.4 %shard_map.128 = (f32[16,3,8,128]{3,2,1,0:T(8,128)S(1)}, f32[16,3,8,128]{3,2,1,0:T(8,128)S(1)}) custom-call(f32[16,2,128]{2,1,0:T(2,128)S(1)} %all_to_all.41.gram_ref, f32[16,7,8,128]{3,2,1,0:T(8,128)S(1)} %all_to_all.40.given_ref.fields_ref, f32[6,16,3,8,128]{4,3,2,1,0:T(8,128)S(1)} %get-tuple-element.22.basis_ref, ...), custom_call_target="tpu_custom_call" | custom-call | tf_op jit(solution)/shard_map/pallas_call | solution.py:437
  75.5 10.0 %all_to_all.42.x_ref = f32[16,3,8,128]{3,2,1,0:T(8,128)S(1)} all-to-all(f32[16,3,8,128]{3,2,1,0:T(8,128)S(1)} %get-tuple-element.25.fields_ref), channel_id=1, replica_groups=mesh['freq'=16,'node'=16] {'freq'}, dimensions={0} | all-to-all | bytes 393216 | tf_op jit(solution)/shard_map/all_to_all | solution.py:441
  85.5 0.6 shard_map.129
  86.1 9.8 %all_to_all.43.friction_ref = f32[16,2,8,128]{3,2,1,0:T(8,128)S(1)} all-to-all(f32[16,2,8,128]{3,2,1,0:T(8,128)S(1)} %shard_map.129), channel_id=1, replica_groups=mesh['freq'=16,'node'=16] {'freq'}, dimensions={0} | all-to-all | bytes 262144 | tf_op jit(solution)/shard_map/all_to_all | solution.py:441
  95.9 3.8 %shard_map.130 = (f32[6,16,3,8,128]{4,3,2,1,0:T(8,128)S(1)}, f32[16,2,128]{2,1,0:T(2,128)S(1)}) custom-call(f32[16,3,8,128]{3,2,1,0:T(8,128)S(1)} %get-tuple-element.24.base_ref, f32[16,2,8,128]{3,2,1,0:T(8,128)S(1)} %all_to_all.43.friction_ref, f32[16,16,8,128]{3,2,1,0:T(8,128)S(1)} %get-tuple-element.19.links_ref, ...), custom_call_target="tpu_custom_call" | custom-call | tf_op jit(solution)/shard_map/pallas_call | solution.py:437
  99.7 12.8 %all_to_all.44.gram_ref = f32[16,2,128]{2,1,0:T(2,128)S(1)} all-to-all(f32[16,2,128]{2,1,0:T(2,128)S(1)} %get-tuple-element.26), channel_id=1, replica_groups=mesh['freq'=16,'node'=16] {'node'}, dimensions={0} | all-to-all | bytes 32768 | tf_op jit(solution)/shard_map/all_to_all | solution.py:441
  112.5 1.4 %shard_map.131 = f32[16,6,8,128]{3,2,1,0:T(8,128)S(1)} custom-call(f32[16,2,128]{2,1,0:T(2,128)S(1)} %all_to_all.44.gram_ref, f32[16,3,8,128]{3,2,1,0:T(8,128)S(1)} %get-tuple-element.25.fields_ref, f32[6,16,3,8,128]{4,3,2,1,0:T(8,128)S(1)} %get-tuple-element.27.basis_ref, f32[16,2,8,128]{3,2,1,0:T(8,128)S(1)} %all_to_all.43.friction_ref, ...), custom_call_target="tpu_custom_call" | custom-call | tf_op jit(solution)/shard_map/pallas_call | solution.py:437
  113.8 17.4 %all_to_all.45.x_ref = f32[16,6,8,128]{3,2,1,0:T(8,128)S(1)} all-to-all(f32[16,6,8,128]{3,2,1,0:T(8,128)S(1)} %shard_map.131), channel_id=1, replica_groups=mesh['freq'=16,'node'=16] {'node'}, dimensions={0} | all-to-all | bytes 786432 | tf_op jit(solution)/shard_map/all_to_all | solution.py:441
  131.2 1.6 %shard_map.132 = (f32[384,128]{1,0:T(8,128)}, f32[384,128]{1,0:T(8,128)}) custom-call(f32[16,6,8,128]{3,2,1,0:T(8,128)S(1)} %all_to_all.45.x_ref), custom_call_target="tpu_custom_call" | custom-call | tf_op jit(solution)/shard_map/pallas_call | solution.py:437
  (1 shorter events, 0.0 us)
Async XLA Ops:
  4.1 33.5 %copy-start = (s32[64]{0:T(128)S(1)}, s32[64]{0:T(128)}, u32[]{:S(2)}) copy-start(s32[64]{0:T(128)} %harmonic_ref.5) | copy-start | bytes 772
  4.1 33.7 %copy-start.2 = (f32[1,128]{1,0:T(1,128)S(1)}, f32[1,128]{1,0:T(1,128)}, u32[]{:S(2)}) copy-start(f32[1,128]{1,0:T(1,128)} %constant.2.clone.cosines_ref) | copy-start | bytes 1540
  30.9 16.1 %all-to-all-start.1 = ((f32[16,5,8,128]{3,2,1,0:T(8,128)}), f32[16,5,8,128]{3,2,1,0:T(8,128)S(1)}, u32[]{:S(2)}, u32[]{:S(2)}) async-start(f32[16,5,8,128]{3,2,1,0:T(8,128)} %shard_map.123), calls=%async_computation.1 | async-start | bytes 655360 | tf_op jit(solution)/shard_map/all_to_all | solution.py:441
  48.2 10.3 %all-to-all-start.2 = ((f32[16,2,8,128]{3,2,1,0:T(8,128)}), f32[16,2,8,128]{3,2,1,0:T(8,128)S(1)}, u32[]{:S(2)}, u32[]{:S(2)}) async-start(f32[16,2,8,128]{3,2,1,0:T(8,128)} %shard_map.126), calls=%async_computation.2 | async-start | bytes 262144 | tf_op jit(solution)/shard_map/all_to_all | solution.py:441
  51.8 22.3 %copy-start.1 = (s32[2,64]{1,0:T(2,128)S(1)}, s32[2,64]{1,0:T(2,128)}, u32[]{:S(2)}) copy-start(s32[2,64]{1,0:T(2,128)} %counts_ref.3) | copy-start | bytes 1540

commit v4 on v3

--- a/solution.py
+++ b/solution.py
@@ -131,7 +131,7 @@
         copy.wait()
 
 
-def forward_kernel(given_ref, out_ref):
+def forward_kernel(given_ref, _, out_ref):
     for half in range(2):
         rows = jnp.concatenate([given_ref[8 * half + i, 6, 0:1] for i in range(8)], axis=0)
         for rank in range(RANKS):
@@ -282,7 +282,7 @@
             base_ref[g, comp] = given_ref[g, 3 + comp] - images[g][comp] - rest
 
 
-def basis_kernel(base_ref, friction_ref, links_ref, index_ref, basis_ref, gram_ref):
+def basis_kernel(base_ref, friction_ref, links_ref, index_ref, basis_ref, gram_ref, swap_ref):
     for g in range(RANKS):
         basis_ref[0, g, 0] = base_ref[g, 0]
         basis_ref[0, g, 1] = base_ref[g, 1] - friction_ref[g, 0]
@@ -294,6 +294,8 @@
         for g in range(RANKS):
             for comp in range(3):
                 basis_ref[m + 1, g, comp] = images[g][comp]
+                swap_ref[m, g, comp, pl.ds(0, 8, stride=2), :] = images[g][comp]
+                swap_ref[m, g, comp, pl.ds(16, 8, stride=2), :] = images[g][comp]
         return 0
 
     lax.fori_loop(0, LMAX, power, 0)
@@ -301,7 +303,7 @@
     def products(g, sums):
         for comp in range(3):
             vectors = [basis_ref[m, g, comp] for m in range(COUNT)]
-            turned = [None] + [pltpu.roll(v, 4, 0) for v in vectors[1:]]
+            turned = [None] + [swap_ref[m, g, comp, pl.ds(8, 8, stride=2), :] for m in range(LMAX)]
             terms = [vectors[m] * vectors[n] for m, n in REAL_PAIRS]
             terms += [vectors[m] * turned[n] for m, n in IMAG_PAIRS]
             sums = tuple(a + b for a, b in zip(sums, terms))
@@ -485,14 +487,13 @@
         connections.T,
     )
     given = exchange(packed, "node")
-    table = exchange(call(forward_kernel, struct(RANKS, 5, 8, LANES), [VMEM])(given), "freq")
-
     slots = jnp.broadcast_to(harmonic_of_slot.reshape(RANKS, 1, 4), (RANKS, 2, 4)).reshape(1, LANES)
     cosines = np.cos(np.arange(SAMPLES) * (2.0 * math.pi / SAMPLES)).astype(np.float32).reshape(1, SAMPLES)
 
     synthesis, analysis = call(tables_kernel, [struct(SAMPLES, LANES), struct(LANES, SAMPLES)], [VMEM] * 2)(
         slots, cosines
     )
+    table = exchange(call(forward_kernel, struct(RANKS, 5, 8, LANES), [VMEM, HBM])(given, analysis), "freq")
 
     def friction_of(received):
         terms = call(friction_kernel, struct(RANKS, 2, 8, LANES), [VMEM] * 4)(received, table, synthesis, analysis)
@@ -512,7 +513,10 @@
     friction = friction_of(table)
     for sweep in range(SWEEPS):
         basis, gram = call(
-            basis_kernel, [struct(COUNT, RANKS, 3, 8, LANES), struct(RANKS, 2, LANES)], [VMEM] * 4
+            basis_kernel,
+            [struct(COUNT, RANKS, 3, 8, LANES), struct(RANKS, 2, LANES)],
+            [VMEM] * 4,
+            (pltpu.VMEM((LMAX, RANKS, 3, 32, LANES), jnp.float32),),
         )(base, friction, links, index)
         gram = exchange(gram, "node")
         if sweep < SWEEPS - 1:

time: 133 us -> 133 us (level)
  blocking collectives: 87.6 us -> 77.6 us
  waiting for transfers between devices: 14.6 us -> 21.2 us
  starting transfers between devices: 10.3 us -> 13.5 us
    all_to_all x6, blocking collectives: 87.6 us -> 77.6 us  [exchange(): return lax.all_to_all(values, axis, split_axis=0, concat_axis=0, tiled=True)]
    all_to_all x2, waiting for transfers between devices: 14.6 us -> 21.2 us  [exchange(): return lax.all_to_all(values, axis, split_axis=0, concat_axis=0, tiled=True)]
    all_to_all x2, starting transfers between devices: 10.3 us -> 13.5 us  [exchange(): return lax.all_to_all(values, axis, split_axis=0, concat_axis=0, tiled=True)]
where the time goes in v4:
time: 133 us; the launch traced here: 132 us
  blocking collectives  77.6 us (58%)
  waiting for transfers between devices  21.2 us (16%)
  Pallas kernels  18.9 us (14%)
  starting transfers between devices  13.5 us (10%)
    all_to_all x6, blocking collectives, exchange(): return lax.all_to_all(values, axis, split_axis=0, concat_axis=0, tiled=True)  77.6 us
    all_to_all x2, waiting for transfers between devices, exchange(): return lax.all_to_all(values, axis, split_axis=0, concat_axis=0, tiled=True)  21.2 us
    all_to_all x2, starting transfers between devices, exchange(): return lax.all_to_all(values, axis, split_axis=0, concat_axis=0, tiled=True)  13.5 us
    pallas_call x7, Pallas kernels, call(): result(*args)  13.4 us
    pallas_call x4, Pallas kernels, call(): result(*args)[0]  5.51 us
  transfers between devices with their start and end apart: 2, of which 2 were waited for; matrix products, arithmetic and copies ran while one was open for 0% of the time, Pallas kernels for 1%

profile of v4, /device:TPU:1, one launch (start us, length us, event | category | flops | bytes accessed | tf_op | source)
XLA Modules:
  0.0 132.1 jit_solution(18136913518545827950)
XLA Ops:
  0.6 0.0 copy-start.2
  0.6 0.0 copy-start
  0.7 3.6 %shard_map.122 = f32[16,7,8,128]{3,2,1,0:T(8,128)} custom-call(f32[384,128]{1,0:T(8,128)} %bitcast.27, f32[384,128]{1,0:T(8,128)} %bitcast.28, f32[4,2048]{1,0:T(4,128)} %weights_hbm.1, f32[4,2048]{1,0:T(4,128)} %east_hbm.1, f32[4,2048]{1,0:T(4,128)} %north_hbm.1, f32[1,2048]{1,0:T(1,128)} %bitcast.29, f32[1,2048]{1,0:T(1,128)} %bitcast.30, s32[4,16]{1,0:T(4,128)} %bitcast.31), custom_call_target="tpu_custom_call" | custom-call | tf_op jit(solution)/shard_map/pallas_call | solution.py:439
  4.3 10.0 %all-to-all-start = ((f32[16,7,8,128]{3,2,1,0:T(8,128)}), f32[16,7,8,128]{3,2,1,0:T(8,128)S(1)}, u32[]{:S(2)}, u32[]{:S(2)}) async-start(f32[16,7,8,128]{3,2,1,0:T(8,128)} %shard_map.122), calls=%async_computation | async-start | bytes 917504 | tf_op jit(solution)/shard_map/all_to_all | solution.py:443
  14.3 0.0 copy-done
  14.3 0.1 broadcast_in_dim.7
  14.4 0.1 reshape.45.harmonic_ref
  14.5 0.0 copy-done.2
  14.5 0.2 shard_map.123
  14.7 15.6 %all-to-all-done.given_ref.fields_ref = f32[16,7,8,128]{3,2,1,0:T(8,128)S(1)} async-done(((f32[16,7,8,128]{3,2,1,0:T(8,128)}), f32[16,7,8,128]{3,2,1,0:T(8,128)S(1)}, u32[]{:S(2)}, u32[]{:S(2)}) %all-to-all-start) | async-done | bytes 458784 | tf_op jit(solution)/shard_map/all_to_all | solution.py:443
  30.3 15.9 %all_to_all.40.table_ref.x_ref = f32[16,5,8,128]{3,2,1,0:T(8,128)S(1)} all-to-all(f32[16,5,8,128]{3,2,1,0:T(8,128)S(1)} %shard_map.124), channel_id=1, replica_groups=mesh['freq'=16,'node'=16] {'freq'}, dimensions={0} | all-to-all | bytes 655360 | tf_op jit(solution)/shard_map/all_to_all | solution.py:443
  46.2 1.3 shard_map.126
  47.5 3.5 %all-to-all-start.2 = ((f32[16,2,8,128]{3,2,1,0:T(8,128)}), f32[16,2,8,128]{3,2,1,0:T(8,128)S(1)}, u32[]{:S(2)}, u32[]{:S(2)}) async-start(f32[16,2,8,128]{3,2,1,0:T(8,128)} %shard_map.126), calls=%async_computation.2 | async-start | bytes 262144 | tf_op jit(solution)/shard_map/all_to_all | solution.py:443
  51.0 0.0 copy-start.1
  51.0 1.1 shard_map.125
  52.1 5.7 %all-to-all-done.2.friction_ref = f32[16,2,8,128]{3,2,1,0:T(8,128)S(1)} async-done(((f32[16,2,8,128]{3,2,1,0:T(8,128)}), f32[16,2,8,128]{3,2,1,0:T(8,128)S(1)}, u32[]{:S(2)}, u32[]{:S(2)}) %all-to-all-start.2) | async-done | bytes 131104 | tf_op jit(solution)/shard_map/all_to_all | solution.py:443
  57.8 3.8 %shard_map.127 = (f32[6,16,3,8,128]{4,3,2,1,0:T(8,128)S(1)}, f32[16,2,128]{2,1,0:T(2,128)S(1)}) custom-call(f32[16,3,8,128]{3,2,1,0:T(8,128)S(1)} %get-tuple-element.17.base_ref, f32[16,2,8,128]{3,2,1,0:T(8,128)S(1)} %all-to-all-done.2.friction_ref, f32[16,16,8,128]{3,2,1,0:T(8,128)S(1)} %get-tuple-element.19.links_ref, ...), custom_call_target="tpu_custom_call" | custom-call | tf_op jit(solution)/shard_map/pallas_call | solution.py:439
  61.6 11.7 %all_to_all.41.gram_ref = f32[16,2,128]{2,1,0:T(2,128)S(1)} all-to-all(f32[16,2,128]{2,1,0:T(2,128)S(1)} %get-tuple-element.21), channel_id=1, replica_groups=mesh['freq'=16,'node'=16] {'node'}, dimensions={0} | all-to-all | bytes 32768 | tf_op jit(solution)/shard_map/all_to_all | solution.py:443
  73.3 0.0 copy-done.1
  73.3 1.4 %shard_map.128 = (f32[16,3,8,128]{3,2,1,0:T(8,128)S(1)}, f32[16,3,8,128]{3,2,1,0:T(8,128)S(1)}) custom-call(f32[16,2,128]{2,1,0:T(2,128)S(1)} %all_to_all.41.gram_ref, f32[16,7,8,128]{3,2,1,0:T(8,128)S(1)} %all-to-all-done.given_ref.fields_ref, f32[6,16,3,8,128]{4,3,2,1,0:T(8,128)S(1)} %get-tuple-element.22.basis_ref, ...), custom_call_target="tpu_custom_call" | custom-call | tf_op jit(solution)/shard_map/pallas_call | solution.py:439
  74.7 10.0 %all_to_all.42.x_ref = f32[16,3,8,128]{3,2,1,0:T(8,128)S(1)} all-to-all(f32[16,3,8,128]{3,2,1,0:T(8,128)S(1)} %get-tuple-element.25.fields_ref), channel_id=1, replica_groups=mesh['freq'=16,'node'=16] {'freq'}, dimensions={0} | all-to-all | bytes 393216 | tf_op jit(solution)/shard_map/all_to_all | solution.py:443
  84.7 0.6 shard_map.129
  85.3 9.8 %all_to_all.43.friction_ref = f32[16,2,8,128]{3,2,1,0:T(8,128)S(1)} all-to-all(f32[16,2,8,128]{3,2,1,0:T(8,128)S(1)} %shard_map.129), channel_id=1, replica_groups=mesh['freq'=16,'node'=16] {'freq'}, dimensions={0} | all-to-all | bytes 262144 | tf_op jit(solution)/shard_map/all_to_all | solution.py:443
  95.2 3.8 %shard_map.130 = (f32[6,16,3,8,128]{4,3,2,1,0:T(8,128)S(1)}, f32[16,2,128]{2,1,0:T(2,128)S(1)}) custom-call(f32[16,3,8,128]{3,2,1,0:T(8,128)S(1)} %get-tuple-element.24.base_ref, f32[16,2,8,128]{3,2,1,0:T(8,128)S(1)} %all_to_all.43.friction_ref, f32[16,16,8,128]{3,2,1,0:T(8,128)S(1)} %get-tuple-element.19.links_ref, ...), custom_call_target="tpu_custom_call" | custom-call | tf_op jit(solution)/shard_map/pallas_call | solution.py:439
  99.0 12.8 %all_to_all.44.gram_ref = f32[16,2,128]{2,1,0:T(2,128)S(1)} all-to-all(f32[16,2,128]{2,1,0:T(2,128)S(1)} %get-tuple-element.26), channel_id=1, replica_groups=mesh['freq'=16,'node'=16] {'node'}, dimensions={0} | all-to-all | bytes 32768 | tf_op jit(solution)/shard_map/all_to_all | solution.py:443
  111.7 1.4 %shard_map.131 = f32[16,6,8,128]{3,2,1,0:T(8,128)S(1)} custom-call(f32[16,2,128]{2,1,0:T(2,128)S(1)} %all_to_all.44.gram_ref, f32[16,3,8,128]{3,2,1,0:T(8,128)S(1)} %get-tuple-element.25.fields_ref, f32[6,16,3,8,128]{4,3,2,1,0:T(8,128)S(1)} %get-tuple-element.27.basis_ref, f32[16,2,8,128]{3,2,1,0:T(8,128)S(1)} %all_to_all.43.friction_ref, ...), custom_call_target="tpu_custom_call" | custom-call | tf_op jit(solution)/shard_map/pallas_call | solution.py:439
  113.1 17.4 %all_to_all.45.x_ref = f32[16,6,8,128]{3,2,1,0:T(8,128)S(1)} all-to-all(f32[16,6,8,128]{3,2,1,0:T(8,128)S(1)} %shard_map.131), channel_id=1, replica_groups=mesh['freq'=16,'node'=16] {'node'}, dimensions={0} | all-to-all | bytes 786432 | tf_op jit(solution)/shard_map/all_to_all | solution.py:443
  130.5 1.6 %shard_map.132 = (f32[384,128]{1,0:T(8,128)}, f32[384,128]{1,0:T(8,128)}) custom-call(f32[16,6,8,128]{3,2,1,0:T(8,128)S(1)} %all_to_all.45.x_ref), custom_call_target="tpu_custom_call" | custom-call | tf_op jit(solution)/shard_map/pallas_call | solution.py:439
  (2 shorter events, 0.0 us)
Async XLA Ops:
  0.6 13.9 %copy-start.2 = (f32[1,128]{1,0:T(1,128)S(1)}, f32[1,128]{1,0:T(1,128)}, u32[]{:S(2)}) copy-start(f32[1,128]{1,0:T(1,128)} %constant.2.clone.cosines_ref) | copy-start | bytes 1540
  0.6 13.6 %copy-start = (s32[64]{0:T(128)S(1)}, s32[64]{0:T(128)}, u32[]{:S(2)}) copy-start(s32[64]{0:T(128)} %harmonic_ref.5) | copy-start | bytes 772
  4.3 26.0 %all-to-all-start = ((f32[16,7,8,128]{3,2,1,0:T(8,128)}), f32[16,7,8,128]{3,2,1,0:T(8,128)S(1)}, u32[]{:S(2)}, u32[]{:S(2)}) async-start(f32[16,7,8,128]{3,2,1,0:T(8,128)} %shard_map.122), calls=%async_computation | async-start | bytes 917504 | tf_op jit(solution)/shard_map/all_to_all | solution.py:443
  47.5 10.3 %all-to-all-start.2 = ((f32[16,2,8,128]{3,2,1,0:T(8,128)}), f32[16,2,8,128]{3,2,1,0:T(8,128)S(1)}, u32[]{:S(2)}, u32[]{:S(2)}) async-start(f32[16,2,8,128]{3,2,1,0:T(8,128)} %shard_map.126), calls=%async_computation.2 | async-start | bytes 262144 | tf_op jit(solution)/shard_map/all_to_all | solution.py:443
  51.0 22.3 %copy-start.1 = (s32[2,64]{1,0:T(2,128)S(1)}, s32[2,64]{1,0:T(2,128)}, u32[]{:S(2)}) copy-start(s32[2,64]{1,0:T(2,128)} %counts_ref.3) | copy-start | bytes 1540

commit v5 on v4

--- a/solution.py
+++ b/solution.py
@@ -206,38 +206,52 @@
                 links_ref[8 * half + i, at] = jnp.broadcast_to(value[i : i + 1], (8, LANES))
         for link in range(2):
             at = rows[ROW_LINKS + link].astype(jnp.int32)
-            outside = jnp.logical_or(at < 0, at > RANKS - 1)
             lane = (at & (RANKS - 1)) * SHARE + share
-            index = jnp.where(outside, lane + LANES, lane)
+            index = jnp.where(at < 0, lane + LANES, jnp.where(at > RANKS - 1, lane + 2 * LANES, lane))
             for i in range(8):
                 index_ref[8 * half + i, link] = jnp.broadcast_to(index[i : i + 1], (8, LANES))
 
 
-def apply_operator(vectors, links_ref, index_ref):
+def make_moves(moves_ref):
+    source, lane = iota((LANES, LANES), 0), iota((LANES, LANES), 1)
+    share = lane & (SHARE - 1)
+    for i, wanted in enumerate((share + (LANES - SHARE), share, lane - SHARE, lane + SHARE)):
+        moves_ref[i] = jnp.where(source == wanted, 1.0, 0.0)
+
+
+def move(vectors, moves_ref, moved_ref):
+    rows = vectors.reshape(RANKS * 3 * 8, LANES)
+    for i in range(4):
+        result = jnp.dot(rows, moves_ref[i], precision=TOP_HARMONIC, preferred_element_type=jnp.float32)
+        moved_ref[i] = result.reshape(RANKS, 3, 8, LANES)
+
+
+def apply_operator(vectors, moved_ref, links_ref, index_ref):
     lane = iota((8, LANES), 1)
     first = lane < SHARE
     last = lane >= LANES - SHARE
     result = []
     for g in range(RANKS):
         here = vectors[g]
-        before = vectors[g - 1] if g > 0 else [pltpu.roll(x, LANES - 2 * SHARE, 1) for x in here]
-        after = vectors[g + 1] if g < RANKS - 1 else [pltpu.roll(x, 2 * SHARE, 1) for x in here]
+        on = [moved_ref[2, g, comp] for comp in range(3)]
+        back = [moved_ref[3, g, comp] for comp in range(3)]
+        before = [moved_ref[0, g - 1, comp] for comp in range(3)] if g > 0 else back
+        after = [moved_ref[1, g + 1, comp] for comp in range(3)] if g < RANKS - 1 else on
         beside = []
-        beside.append([pltpu.roll(jnp.where(last, p, x), SHARE, 1) for p, x in zip(before, here)])
-        beside.append([pltpu.roll(jnp.where(first, n, x), LANES - SHARE, 1) for n, x in zip(after, here)])
-        edges = [jnp.where(last, p, n) for p, n in zip(before, after)]
+        beside.append([jnp.where(first, p, x) for p, x in zip(before, on)])
+        beside.append([jnp.where(last, n, x) for n, x in zip(after, back)])
         for link in range(2):
             index = index_ref[g, link]
-            outside = index >= LANES
+            outside, following = index >= LANES, index >= 2 * LANES
             index = index & (LANES - 1)
             beside.append(
                 [
                     jnp.where(
                         outside,
-                        jnp.take_along_axis(e, index, axis=1, mode="promise_in_bounds"),
+                        jnp.where(following, n, p),
                         jnp.take_along_axis(x, index, axis=1, mode="promise_in_bounds"),
                     )
-                    for e, x in zip(edges, here)
+                    for p, n, x in zip(before, after, here)
                 ]
             )
         x_ele, x_east, x_north = here
@@ -266,7 +280,7 @@
     return OMEGA_STEP * slot_rows(harmonic_ref, lambda ref, i: ref[i]).astype(jnp.float32)
 
 
-def start_kernel(given_ref, table_ref, harmonic_ref, base_ref, links_ref, index_ref, shift_ref):
+def start_kernel(given_ref, table_ref, harmonic_ref, base_ref, links_ref, index_ref, shift_ref, moves_ref, moved_ref):
     shift = given_ref[0, 6, 1:2]
     for g in range(1, RANKS):
         shift = shift + given_ref[g, 6, 1:2]
@@ -275,14 +289,17 @@
     prepare_links(table_ref, shift, links_ref, index_ref)
     turn = angular_rows(harmonic_ref) * jnp.where(iota((8, LANES), 0) < 4, -1.0, 1.0)
     vectors = [[given_ref[g, comp] for comp in range(3)] for g in range(RANKS)]
-    images = apply_operator(vectors, links_ref, index_ref)
+    make_moves(moves_ref)
+    move(given_ref[:, :3], moves_ref, moved_ref)
+    images = apply_operator(vectors, moved_ref, links_ref, index_ref)
     for g in range(RANKS):
         for comp in range(3):
             rest = shift * vectors[g][comp] + turn * pltpu.roll(vectors[g][comp], 4, 0)
             base_ref[g, comp] = given_ref[g, 3 + comp] - images[g][comp] - rest
 
 
-def basis_kernel(base_ref, friction_ref, links_ref, index_ref, basis_ref, gram_ref, swap_ref):
+def basis_kernel(base_ref, friction_ref, links_ref, index_ref, basis_ref, gram_ref, swap_ref, moves_ref, moved_ref):
+    make_moves(moves_ref)
     for g in range(RANKS):
         basis_ref[0, g, 0] = base_ref[g, 0]
         basis_ref[0, g, 1] = base_ref[g, 1] - friction_ref[g, 0]
@@ -290,7 +307,8 @@
 
     def power(m, _):
         vectors = [[basis_ref[m, g, comp] for comp in range(3)] for g in range(RANKS)]
-        images = apply_operator(vectors, links_ref, index_ref)
+        move(basis_ref[m], moves_ref, moved_ref)
+        images = apply_operator(vectors, moved_ref, links_ref, index_ref)
         for g in range(RANKS):
             for comp in range(3):
                 basis_ref[m + 1, g, comp] = images[g][comp]
@@ -457,6 +475,7 @@
     whole = pltpu.VMEM((384, LANES), jnp.float32)
     four = pltpu.VMEM((4, 2048), jnp.float32)
     line = pltpu.VMEM((1, 2048), jnp.float32)
+    moving = (pltpu.VMEM((4, LANES, LANES), jnp.float32), pltpu.VMEM((4, RANKS, 3, 8, LANES), jnp.float32))
     packed = call(
         pack_kernel,
         struct(RANKS, 7, 8, LANES),
@@ -508,6 +527,7 @@
             struct(8, LANES),
         ],
         [VMEM, VMEM, SMEM],
+        moving,
     )(given, table, harmonic_of_slot)
     fields = given
     friction = friction_of(table)
@@ -516,7 +536,7 @@
             basis_kernel,
             [struct(COUNT, RANKS, 3, 8, LANES), struct(RANKS, 2, LANES)],
             [VMEM] * 4,
-            (pltpu.VMEM((LMAX, RANKS, 3, 32, LANES), jnp.float32),),
+            (pltpu.VMEM((LMAX, RANKS, 3, 32, LANES), jnp.float32), *moving),
         )(base, friction, links, index)
         gram = exchange(gram, "node")
         if sweep < SWEEPS - 1:

time: 133 us -> 136 us (1.023)
  Pallas kernels: 18.9 us -> 22.7 us
    pallas_call x7, Pallas kernels: 13.4 us -> 17.2 us  [call(): result(*args)]
where the time goes in v5:
time: 136 us
  blocking collectives  77.6 us (57%)
  Pallas kernels  22.7 us (17%)
  waiting for transfers between devices  20.8 us (15%)
  starting transfers between devices  13.5 us (10%)
    all_to_all x6, blocking collectives, exchange(): return lax.all_to_all(values, axis, split_axis=0, concat_axis=0, tiled=True)  77.6 us
    all_to_all x2, waiting for transfers between devices, exchange(): return lax.all_to_all(values, axis, split_axis=0, concat_axis=0, tiled=True)  20.8 us
    pallas_call x7, Pallas kernels, call(): result(*args)  17.2 us
    all_to_all x2, starting transfers between devices, exchange(): return lax.all_to_all(values, axis, split_axis=0, concat_axis=0, tiled=True)  13.5 us
    pallas_call x4, Pallas kernels, call(): result(*args)[0]  5.51 us
  transfers between devices with their start and end apart: 2, of which 2 were waited for; matrix products, arithmetic and copies ran while one was open for 0% of the time, Pallas kernels for 1%

profile of v5, /device:TPU:1, one launch (start us, length us, event | category | flops | bytes accessed | tf_op | source)
XLA Modules:
  0.0 135.6 jit_solution(11998862605296892897)
XLA Ops:
  0.6 0.0 copy-start.2
  0.6 0.0 copy-start
  0.7 3.6 %shard_map.122 = f32[16,7,8,128]{3,2,1,0:T(8,128)} custom-call(f32[384,128]{1,0:T(8,128)} %bitcast.27, f32[384,128]{1,0:T(8,128)} %bitcast.28, f32[4,2048]{1,0:T(4,128)} %weights_hbm.1, f32[4,2048]{1,0:T(4,128)} %east_hbm.1, f32[4,2048]{1,0:T(4,128)} %north_hbm.1, f32[1,2048]{1,0:T(1,128)} %bitcast.29, f32[1,2048]{1,0:T(1,128)} %bitcast.30, s32[4,16]{1,0:T(4,128)} %bitcast.31), custom_call_target="tpu_custom_call" | custom-call | tf_op jit(solution)/shard_map/pallas_call | solution.py:457
  4.3 10.0 %all-to-all-start = ((f32[16,7,8,128]{3,2,1,0:T(8,128)}), f32[16,7,8,128]{3,2,1,0:T(8,128)S(1)}, u32[]{:S(2)}, u32[]{:S(2)}) async-start(f32[16,7,8,128]{3,2,1,0:T(8,128)} %shard_map.122), calls=%async_computation | async-start | bytes 917504 | tf_op jit(solution)/shard_map/all_to_all | solution.py:461
  14.3 0.0 copy-done
  14.3 0.1 broadcast_in_dim.7
  14.4 0.1 reshape.45.harmonic_ref
  14.5 0.0 copy-done.2
  14.5 0.2 shard_map.123
  14.7 15.6 %all-to-all-done.given_ref.fields_ref = f32[16,7,8,128]{3,2,1,0:T(8,128)S(1)} async-done(((f32[16,7,8,128]{3,2,1,0:T(8,128)}), f32[16,7,8,128]{3,2,1,0:T(8,128)S(1)}, u32[]{:S(2)}, u32[]{:S(2)}) %all-to-all-start) | async-done | bytes 458784 | tf_op jit(solution)/shard_map/all_to_all | solution.py:461
  30.3 15.9 %all_to_all.40.table_ref.x_ref = f32[16,5,8,128]{3,2,1,0:T(8,128)S(1)} all-to-all(f32[16,5,8,128]{3,2,1,0:T(8,128)S(1)} %shard_map.124), channel_id=1, replica_groups=mesh['freq'=16,'node'=16] {'freq'}, dimensions={0} | all-to-all | bytes 655360 | tf_op jit(solution)/shard_map/all_to_all | solution.py:461
  46.2 1.3 shard_map.126
  47.5 3.5 %all-to-all-start.2 = ((f32[16,2,8,128]{3,2,1,0:T(8,128)}), f32[16,2,8,128]{3,2,1,0:T(8,128)S(1)}, u32[]{:S(2)}, u32[]{:S(2)}) async-start(f32[16,2,8,128]{3,2,1,0:T(8,128)} %shard_map.126), calls=%async_computation.2 | async-start | bytes 262144 | tf_op jit(solution)/shard_map/all_to_all | solution.py:461
  51.0 0.0 copy-start.1
  51.0 1.5 %shard_map.125 = (f32[16,3,8,128]{3,2,1,0:T(8,128)S(1)}, f32[16,16,8,128]{3,2,1,0:T(8,128)S(1)}, s32[16,2,8,128]{3,2,1,0:T(8,128)S(1)}, f32[8,128]{1,0:T(8,128)S(1)}) custom-call(f32[16,7,8,128]{3,2,1,0:T(8,128)S(1)} %all-to-all-done.given_ref.fields_ref, f32[16,5,8,128]{3,2,1,0:T(8,128)S(1)} %all_to_all.40.table_ref.x_ref, s32[64]{0:T(128)S(1)} %copy-done), custom_call_target="tpu_custom_call" | custom-call | tf_op jit(solution)/shard_map/pallas_call | solution.py:457
  52.5 5.3 %all-to-all-done.2.friction_ref = f32[16,2,8,128]{3,2,1,0:T(8,128)S(1)} async-done(((f32[16,2,8,128]{3,2,1,0:T(8,128)}), f32[16,2,8,128]{3,2,1,0:T(8,128)S(1)}, u32[]{:S(2)}, u32[]{:S(2)}) %all-to-all-start.2) | async-done | bytes 131104 | tf_op jit(solution)/shard_map/all_to_all | solution.py:461
  57.8 5.5 %shard_map.127 = (f32[6,16,3,8,128]{4,3,2,1,0:T(8,128)S(1)}, f32[16,2,128]{2,1,0:T(2,128)S(1)}) custom-call(f32[16,3,8,128]{3,2,1,0:T(8,128)S(1)} %get-tuple-element.17.base_ref, f32[16,2,8,128]{3,2,1,0:T(8,128)S(1)} %all-to-all-done.2.friction_ref, f32[16,16,8,128]{3,2,1,0:T(8,128)S(1)} %get-tuple-element.19.links_ref, ...), custom_call_target="tpu_custom_call" | custom-call | tf_op jit(solution)/shard_map/pallas_call | solution.py:457
  63.3 11.7 %all_to_all.41.gram_ref = f32[16,2,128]{2,1,0:T(2,128)S(1)} all-to-all(f32[16,2,128]{2,1,0:T(2,128)S(1)} %get-tuple-element.21), channel_id=1, replica_groups=mesh['freq'=16,'node'=16] {'node'}, dimensions={0} | all-to-all | bytes 32768 | tf_op jit(solution)/shard_map/all_to_all | solution.py:461
  75.0 0.0 copy-done.1
  75.0 1.4 %shard_map.128 = (f32[16,3,8,128]{3,2,1,0:T(8,128)S(1)}, f32[16,3,8,128]{3,2,1,0:T(8,128)S(1)}) custom-call(f32[16,2,128]{2,1,0:T(2,128)S(1)} %all_to_all.41.gram_ref, f32[16,7,8,128]{3,2,1,0:T(8,128)S(1)} %all-to-all-done.given_ref.fields_ref, f32[6,16,3,8,128]{4,3,2,1,0:T(8,128)S(1)} %get-tuple-element.22.basis_ref, ...), custom_call_target="tpu_custom_call" | custom-call | tf_op jit(solution)/shard_map/pallas_call | solution.py:457
  76.4 10.0 %all_to_all.42.x_ref = f32[16,3,8,128]{3,2,1,0:T(8,128)S(1)} all-to-all(f32[16,3,8,128]{3,2,1,0:T(8,128)S(1)} %get-tuple-element.25.fields_ref), channel_id=1, replica_groups=mesh['freq'=16,'node'=16] {'freq'}, dimensions={0} | all-to-all | bytes 393216 | tf_op jit(solution)/shard_map/all_to_all | solution.py:461
  86.4 0.6 shard_map.129
  87.0 9.8 %all_to_all.43.friction_ref = f32[16,2,8,128]{3,2,1,0:T(8,128)S(1)} all-to-all(f32[16,2,8,128]{3,2,1,0:T(8,128)S(1)} %shard_map.129), channel_id=1, replica_groups=mesh['freq'=16,'node'=16] {'freq'}, dimensions={0} | all-to-all | bytes 262144 | tf_op jit(solution)/shard_map/all_to_all | solution.py:461
  96.9 5.5 %shard_map.130 = (f32[6,16,3,8,128]{4,3,2,1,0:T(8,128)S(1)}, f32[16,2,128]{2,1,0:T(2,128)S(1)}) custom-call(f32[16,3,8,128]{3,2,1,0:T(8,128)S(1)} %get-tuple-element.24.base_ref, f32[16,2,8,128]{3,2,1,0:T(8,128)S(1)} %all_to_all.43.friction_ref, f32[16,16,8,128]{3,2,1,0:T(8,128)S(1)} %get-tuple-element.19.links_ref, ...), custom_call_target="tpu_custom_call" | custom-call | tf_op jit(solution)/shard_map/pallas_call | solution.py:457
  102.4 12.7 %all_to_all.44.gram_ref = f32[16,2,128]{2,1,0:T(2,128)S(1)} all-to-all(f32[16,2,128]{2,1,0:T(2,128)S(1)} %get-tuple-element.26), channel_id=1, replica_groups=mesh['freq'=16,'node'=16] {'node'}, dimensions={0} | all-to-all | bytes 32768 | tf_op jit(solution)/shard_map/all_to_all | solution.py:461
  115.2 1.4 %shard_map.131 = f32[16,6,8,128]{3,2,1,0:T(8,128)S(1)} custom-call(f32[16,2,128]{2,1,0:T(2,128)S(1)} %all_to_all.44.gram_ref, f32[16,3,8,128]{3,2,1,0:T(8,128)S(1)} %get-tuple-element.25.fields_ref, f32[6,16,3,8,128]{4,3,2,1,0:T(8,128)S(1)} %get-tuple-element.27.basis_ref, f32[16,2,8,128]{3,2,1,0:T(8,128)S(1)} %all_to_all.43.friction_ref, ...), custom_call_target="tpu_custom_call" | custom-call | tf_op jit(solution)/shard_map/pallas_call | solution.py:457
  116.5 17.4 %all_to_all.45.x_ref = f32[16,6,8,128]{3,2,1,0:T(8,128)S(1)} all-to-all(f32[16,6,8,128]{3,2,1,0:T(8,128)S(1)} %shard_map.131), channel_id=1, replica_groups=mesh['freq'=16,'node'=16] {'node'}, dimensions={0} | all-to-all | bytes 786432 | tf_op jit(solution)/shard_map/all_to_all | solution.py:461
  133.9 1.6 %shard_map.132 = (f32[384,128]{1,0:T(8,128)}, f32[384,128]{1,0:T(8,128)}) custom-call(f32[16,6,8,128]{3,2,1,0:T(8,128)S(1)} %all_to_all.45.x_ref), custom_call_target="tpu_custom_call" | custom-call | tf_op jit(solution)/shard_map/pallas_call | solution.py:457
  (2 shorter events, 0.0 us)
Async XLA Ops:
  0.6 13.9 %copy-start.2 = (f32[1,128]{1,0:T(1,128)S(1)}, f32[1,128]{1,0:T(1,128)}, u32[]{:S(2)}) copy-start(f32[1,128]{1,0:T(1,128)} %constant.2.clone.cosines_ref) | copy-start | bytes 1540
  0.6 13.6 %copy-start = (s32[64]{0:T(128)S(1)}, s32[64]{0:T(128)}, u32[]{:S(2)}) copy-start(s32[64]{0:T(128)} %harmonic_ref.5) | copy-start | bytes 772
  4.3 26.0 %all-to-all-start = ((f32[16,7,8,128]{3,2,1,0:T(8,128)}), f32[16,7,8,128]{3,2,1,0:T(8,128)S(1)}, u32[]{:S(2)}, u32[]{:S(2)}) async-start(f32[16,7,8,128]{3,2,1,0:T(8,128)} %shard_map.122), calls=%async_computation | async-start | bytes 917504 | tf_op jit(solution)/shard_map/all_to_all | solution.py:461
  47.5 10.3 %all-to-all-start.2 = ((f32[16,2,8,128]{3,2,1,0:T(8,128)}), f32[16,2,8,128]{3,2,1,0:T(8,128)S(1)}, u32[]{:S(2)}, u32[]{:S(2)}) async-start(f32[16,2,8,128]{3,2,1,0:T(8,128)} %shard_map.126), calls=%async_computation.2 | async-start | bytes 262144 | tf_op jit(solution)/shard_map/all_to_all | solution.py:461
  51.0 24.0 %copy-start.1 = (s32[2,64]{1,0:T(2,128)S(1)}, s32[2,64]{1,0:T(2,128)}, u32[]{:S(2)}) copy-start(s32[2,64]{1,0:T(2,128)} %counts_ref.3) | copy-start | bytes 1540

commit v6 on v4

--- a/solution.py
+++ b/solution.py
@@ -47,8 +47,10 @@
             if i & (1 << bit):
                 continue
             low, high = rows[i], rows[i | (1 << bit)]
-            rows[i] = jnp.where(upper, pltpu.roll(high, step, 1), low)
-            rows[i | (1 << bit)] = jnp.where(upper, high, pltpu.roll(low, LANES - step, 1))
+            crossing = jnp.where(upper, low, high)
+            crossed = jnp.take_along_axis(crossing, lane ^ step, axis=1, mode="promise_in_bounds")
+            rows[i] = jnp.where(upper, crossed, low)
+            rows[i | (1 << bit)] = jnp.where(upper, high, crossed)
     return rows
 
 

time: 133 us -> 132 us (level)
  no operation moved by 1% of the time
where the time goes in v6:
time: 132 us
  blocking collectives  77.6 us (59%)
  waiting for transfers between devices  21.2 us (16%)
  Pallas kernels  18.5 us (14%)
  starting transfers between devices  13.5 us (10%)
    all_to_all x6, blocking collectives, exchange(): return lax.all_to_all(values, axis, split_axis=0, concat_axis=0, tiled=True)  77.6 us
    all_to_all x2, waiting for transfers between devices, exchange(): return lax.all_to_all(values, axis, split_axis=0, concat_axis=0, tiled=True)  21.2 us
    all_to_all x2, starting transfers between devices, exchange(): return lax.all_to_all(values, axis, split_axis=0, concat_axis=0, tiled=True)  13.5 us
    pallas_call x7, Pallas kernels, call(): result(*args)  13 us
    pallas_call x4, Pallas kernels, call(): result(*args)[0]  5.48 us
  transfers between devices with their start and end apart: 2, of which 2 were waited for; matrix products, arithmetic and copies ran while one was open for 0% of the time, Pallas kernels for 1%

profile of v6, /device:TPU:1, one launch (start us, length us, event | category | flops | bytes accessed | tf_op | source)
XLA Modules:
  0.0 131.7 jit_solution(17485771078769039841)
XLA Ops:
  0.6 0.0 copy-start.2
  0.6 0.0 copy-start
  0.7 3.6 %shard_map.122 = f32[16,7,8,128]{3,2,1,0:T(8,128)} custom-call(f32[384,128]{1,0:T(8,128)} %bitcast.27, f32[384,128]{1,0:T(8,128)} %bitcast.28, f32[4,2048]{1,0:T(4,128)} %weights_hbm.1, f32[4,2048]{1,0:T(4,128)} %east_hbm.1, f32[4,2048]{1,0:T(4,128)} %north_hbm.1, f32[1,2048]{1,0:T(1,128)} %bitcast.29, f32[1,2048]{1,0:T(1,128)} %bitcast.30, s32[4,16]{1,0:T(4,128)} %bitcast.31), custom_call_target="tpu_custom_call" | custom-call | tf_op jit(solution)/shard_map/pallas_call | solution.py:441
  4.3 10.0 %all-to-all-start = ((f32[16,7,8,128]{3,2,1,0:T(8,128)}), f32[16,7,8,128]{3,2,1,0:T(8,128)S(1)}, u32[]{:S(2)}, u32[]{:S(2)}) async-start(f32[16,7,8,128]{3,2,1,0:T(8,128)} %shard_map.122), calls=%async_computation | async-start | bytes 917504 | tf_op jit(solution)/shard_map/all_to_all | solution.py:445
  14.2 0.0 copy-done
  14.3 0.1 broadcast_in_dim.7
  14.3 0.1 reshape.45.harmonic_ref
  14.5 0.0 copy-done.2
  14.5 0.2 shard_map.123
  14.7 15.6 %all-to-all-done.given_ref.fields_ref = f32[16,7,8,128]{3,2,1,0:T(8,128)S(1)} async-done(((f32[16,7,8,128]{3,2,1,0:T(8,128)}), f32[16,7,8,128]{3,2,1,0:T(8,128)S(1)}, u32[]{:S(2)}, u32[]{:S(2)}) %all-to-all-start) | async-done | bytes 458784 | tf_op jit(solution)/shard_map/all_to_all | solution.py:445
  30.2 15.9 %all_to_all.40.table_ref.x_ref = f32[16,5,8,128]{3,2,1,0:T(8,128)S(1)} all-to-all(f32[16,5,8,128]{3,2,1,0:T(8,128)S(1)} %shard_map.124), channel_id=1, replica_groups=mesh['freq'=16,'node'=16] {'freq'}, dimensions={0} | all-to-all | bytes 655360 | tf_op jit(solution)/shard_map/all_to_all | solution.py:445
  46.2 1.3 shard_map.126
  47.4 3.5 %all-to-all-start.2 = ((f32[16,2,8,128]{3,2,1,0:T(8,128)}), f32[16,2,8,128]{3,2,1,0:T(8,128)S(1)}, u32[]{:S(2)}, u32[]{:S(2)}) async-start(f32[16,2,8,128]{3,2,1,0:T(8,128)} %shard_map.126), calls=%async_computation.2 | async-start | bytes 262144 | tf_op jit(solution)/shard_map/all_to_all | solution.py:445
  51.0 0.0 copy-start.1
  51.0 1.1 shard_map.125
  52.1 5.7 %all-to-all-done.2.friction_ref = f32[16,2,8,128]{3,2,1,0:T(8,128)S(1)} async-done(((f32[16,2,8,128]{3,2,1,0:T(8,128)}), f32[16,2,8,128]{3,2,1,0:T(8,128)S(1)}, u32[]{:S(2)}, u32[]{:S(2)}) %all-to-all-start.2) | async-done | bytes 131104 | tf_op jit(solution)/shard_map/all_to_all | solution.py:445
  57.8 3.8 %shard_map.127 = (f32[6,16,3,8,128]{4,3,2,1,0:T(8,128)S(1)}, f32[16,2,128]{2,1,0:T(2,128)S(1)}) custom-call(f32[16,3,8,128]{3,2,1,0:T(8,128)S(1)} %get-tuple-element.17.base_ref, f32[16,2,8,128]{3,2,1,0:T(8,128)S(1)} %all-to-all-done.2.friction_ref, f32[16,16,8,128]{3,2,1,0:T(8,128)S(1)} %get-tuple-element.19.links_ref, ...), custom_call_target="tpu_custom_call" | custom-call | tf_op jit(solution)/shard_map/pallas_call | solution.py:441
  61.6 11.7 %all_to_all.41.gram_ref = f32[16,2,128]{2,1,0:T(2,128)S(1)} all-to-all(f32[16,2,128]{2,1,0:T(2,128)S(1)} %get-tuple-element.21), channel_id=1, replica_groups=mesh['freq'=16,'node'=16] {'node'}, dimensions={0} | all-to-all | bytes 32768 | tf_op jit(solution)/shard_map/all_to_all | solution.py:445
  73.3 0.0 copy-done.1
  73.3 1.4 %shard_map.128 = (f32[16,3,8,128]{3,2,1,0:T(8,128)S(1)}, f32[16,3,8,128]{3,2,1,0:T(8,128)S(1)}) custom-call(f32[16,2,128]{2,1,0:T(2,128)S(1)} %all_to_all.41.gram_ref, f32[16,7,8,128]{3,2,1,0:T(8,128)S(1)} %all-to-all-done.given_ref.fields_ref, f32[6,16,3,8,128]{4,3,2,1,0:T(8,128)S(1)} %get-tuple-element.22.basis_ref, ...), custom_call_target="tpu_custom_call" | custom-call | tf_op jit(solution)/shard_map/pallas_call | solution.py:441
  74.7 10.0 %all_to_all.42.x_ref = f32[16,3,8,128]{3,2,1,0:T(8,128)S(1)} all-to-all(f32[16,3,8,128]{3,2,1,0:T(8,128)S(1)} %get-tuple-element.25.fields_ref), channel_id=1, replica_groups=mesh['freq'=16,'node'=16] {'freq'}, dimensions={0} | all-to-all | bytes 393216 | tf_op jit(solution)/shard_map/all_to_all | solution.py:445
  84.7 0.6 shard_map.129
  85.3 9.8 %all_to_all.43.friction_ref = f32[16,2,8,128]{3,2,1,0:T(8,128)S(1)} all-to-all(f32[16,2,8,128]{3,2,1,0:T(8,128)S(1)} %shard_map.129), channel_id=1, replica_groups=mesh['freq'=16,'node'=16] {'freq'}, dimensions={0} | all-to-all | bytes 262144 | tf_op jit(solution)/shard_map/all_to_all | solution.py:445
  95.1 3.8 %shard_map.130 = (f32[6,16,3,8,128]{4,3,2,1,0:T(8,128)S(1)}, f32[16,2,128]{2,1,0:T(2,128)S(1)}) custom-call(f32[16,3,8,128]{3,2,1,0:T(8,128)S(1)} %get-tuple-element.24.base_ref, f32[16,2,8,128]{3,2,1,0:T(8,128)S(1)} %all_to_all.43.friction_ref, f32[16,16,8,128]{3,2,1,0:T(8,128)S(1)} %get-tuple-element.19.links_ref, ...), custom_call_target="tpu_custom_call" | custom-call | tf_op jit(solution)/shard_map/pallas_call | solution.py:441
  99.0 12.8 %all_to_all.44.gram_ref = f32[16,2,128]{2,1,0:T(2,128)S(1)} all-to-all(f32[16,2,128]{2,1,0:T(2,128)S(1)} %get-tuple-element.26), channel_id=1, replica_groups=mesh['freq'=16,'node'=16] {'node'}, dimensions={0} | all-to-all | bytes 32768 | tf_op jit(solution)/shard_map/all_to_all | solution.py:445
  111.7 1.4 %shard_map.131 = f32[16,6,8,128]{3,2,1,0:T(8,128)S(1)} custom-call(f32[16,2,128]{2,1,0:T(2,128)S(1)} %all_to_all.44.gram_ref, f32[16,3,8,128]{3,2,1,0:T(8,128)S(1)} %get-tuple-element.25.fields_ref, f32[6,16,3,8,128]{4,3,2,1,0:T(8,128)S(1)} %get-tuple-element.27.basis_ref, f32[16,2,8,128]{3,2,1,0:T(8,128)S(1)} %all_to_all.43.friction_ref, ...), custom_call_target="tpu_custom_call" | custom-call | tf_op jit(solution)/shard_map/pallas_call | solution.py:441
  113.1 17.4 %all_to_all.45.x_ref = f32[16,6,8,128]{3,2,1,0:T(8,128)S(1)} all-to-all(f32[16,6,8,128]{3,2,1,0:T(8,128)S(1)} %shard_map.131), channel_id=1, replica_groups=mesh['freq'=16,'node'=16] {'node'}, dimensions={0} | all-to-all | bytes 786432 | tf_op jit(solution)/shard_map/all_to_all | solution.py:445
  130.5 1.3 shard_map.132
  (2 shorter events, 0.0 us)
Async XLA Ops:
  0.6 13.8 %copy-start.2 = (f32[1,128]{1,0:T(1,128)S(1)}, f32[1,128]{1,0:T(1,128)}, u32[]{:S(2)}) copy-start(f32[1,128]{1,0:T(1,128)} %constant.2.clone.cosines_ref) | copy-start | bytes 1540
  0.6 13.6 %copy-start = (s32[64]{0:T(128)S(1)}, s32[64]{0:T(128)}, u32[]{:S(2)}) copy-start(s32[64]{0:T(128)} %harmonic_ref.5) | copy-start | bytes 772
  4.3 26.0 %all-to-all-start = ((f32[16,7,8,128]{3,2,1,0:T(8,128)}), f32[16,7,8,128]{3,2,1,0:T(8,128)S(1)}, u32[]{:S(2)}, u32[]{:S(2)}) async-start(f32[16,7,8,128]{3,2,1,0:T(8,128)} %shard_map.122), calls=%async_computation | async-start | bytes 917504 | tf_op jit(solution)/shard_map/all_to_all | solution.py:445
  47.4 10.3 %all-to-all-start.2 = ((f32[16,2,8,128]{3,2,1,0:T(8,128)}), f32[16,2,8,128]{3,2,1,0:T(8,128)S(1)}, u32[]{:S(2)}, u32[]{:S(2)}) async-start(f32[16,2,8,128]{3,2,1,0:T(8,128)} %shard_map.126), calls=%async_computation.2 | async-start | bytes 262144 | tf_op jit(solution)/shard_map/all_to_all | solution.py:445
  51.0 22.3 %copy-start.1 = (s32[2,64]{1,0:T(2,128)S(1)}, s32[2,64]{1,0:T(2,128)}, u32[]{:S(2)}) copy-start(s32[2,64]{1,0:T(2,128)} %counts_ref.3) | copy-start | bytes 1540

commit v7 on v6

--- a/solution.py
+++ b/solution.py
@@ -68,7 +68,7 @@
     north_hbm,
     damping_hbm,
     depths_hbm,
-    links_ref,
+    links_hbm,
     out_hbm,
     fields_ref,
     forcing_ref,
@@ -77,22 +77,17 @@
     north_ref,
     damping_ref,
     depths_ref,
+    links_ref,
     rows_ref,
     out_ref,
     sems,
     out_sems,
 ):
-    sources = (fields_hbm, forcing_hbm, weights_hbm, east_hbm, north_hbm, damping_hbm, depths_hbm)
-    targets = (fields_ref, forcing_ref, weights_ref, east_ref, north_ref, damping_ref, depths_ref)
+    sources = (fields_hbm, forcing_hbm, weights_hbm, east_hbm, north_hbm, damping_hbm, depths_hbm, links_hbm)
+    targets = (fields_ref, forcing_ref, weights_ref, east_ref, north_ref, damping_ref, depths_ref, links_ref)
     copies = [pltpu.make_async_copy(a, b, sems.at[i]) for i, (a, b) in enumerate(zip(sources, targets))]
     for copy in copies:
         copy.start()
-    first = lax.axis_index("node") * RANKS
-    for link in range(2):
-        for b in range(RANKS):
-            local = (links_ref[2 + link, b] - first).astype(jnp.float32)
-            at = ROW_LINKS + link
-            rows_ref[at, :, LANES * b : LANES * (b + 1)] = jnp.full((1, LANES), local, jnp.float32)
     sent = []
 
     def send(index, group, count):
@@ -121,6 +116,11 @@
             rows_ref[4 * kind + link] = source[link : link + 1, :]
     rows_ref[ROW_DAMPING] = damping_ref[...]
     rows_ref[ROW_DEPTHS] = depths_ref[...]
+    local = (links_ref[...] - lax.axis_index("node") * RANKS).astype(jnp.float32)
+    for link in range(2):
+        for b in range(RANKS):
+            row = jnp.broadcast_to(local[2 + link : 3 + link, b : b + 1], (1, LANES))
+            rows_ref[ROW_LINKS + link, :, LANES * b : LANES * (b + 1)] = row
     mine = lax.axis_index("freq")
     rows = [jnp.broadcast_to(rows_ref[mine, :, LANES * b : LANES * (b + 1)], (8, LANES)) for b in range(RANKS)]
     diagonal = jnp.sum(weights_ref[...], axis=0, keepdims=True) + (2.0 / 3.0) * damping_ref[...] + ETA_DAMP / 3.0
@@ -268,14 +268,18 @@
     return OMEGA_STEP * slot_rows(harmonic_ref, lambda ref, i: ref[i]).astype(jnp.float32)
 
 
-def start_kernel(given_ref, table_ref, harmonic_ref, base_ref, links_ref, index_ref, shift_ref):
+def start_kernel(given_ref, table_ref, harmonic_ref, counts_ref, base_ref, links_ref, index_ref, slots_ref):
     shift = given_ref[0, 6, 1:2]
     for g in range(1, RANKS):
         shift = shift + given_ref[g, 6, 1:2]
     shift = jnp.broadcast_to(shift * (1.0 / RANKS), (8, LANES))
-    shift_ref[...] = shift
+    angular = angular_rows(harmonic_ref)
+    slots_ref[0] = shift
+    slots_ref[1] = angular
+    for sweep in range(SWEEPS):
+        slots_ref[2 + sweep] = slot_rows(counts_ref, lambda ref, i: ref[sweep, i]).astype(jnp.float32)
     prepare_links(table_ref, shift, links_ref, index_ref)
-    turn = angular_rows(harmonic_ref) * jnp.where(iota((8, LANES), 0) < 4, -1.0, 1.0)
+    turn = angular * jnp.where(iota((8, LANES), 0) < 4, -1.0, 1.0)
     vectors = [[given_ref[g, comp] for comp in range(3)] for g in range(RANKS)]
     images = apply_operator(vectors, links_ref, index_ref)
     for g in range(RANKS):
@@ -324,7 +328,7 @@
         gram_ref[rank] = packed
 
 
-def step_sizes(gram_ref, shift, harmonic_ref, counts_ref, sweep):
+def step_sizes(gram_ref, slots_ref, sweep):
     gram = gram_ref[0]
     for rank in range(1, RANKS):
         gram = gram + gram_ref[rank]
@@ -357,8 +361,7 @@
             return mul(inner[m, n], b)
         return conj_mul(inner[n, m], b)
 
-    angular = angular_rows(harmonic_ref)
-    counts = slot_rows(counts_ref, lambda ref, i: ref[sweep, i])
+    shift, angular, counts = slots_ref[0], slots_ref[1], slots_ref[2 + sweep]
     zero = jnp.zeros((8, LANES), jnp.float32)
     residual = [(jnp.ones((8, LANES), jnp.float32), zero)]
     correction = [(zero, zero) for _ in range(LMAX)]
@@ -384,7 +387,7 @@
                 with_image = add(with_image, gram_times(m, n, image[n]))
             lower = lower + image[m][0] * with_image[0] + image[m][1] * with_image[1]
         lower = lower + 1e-06
-        active = jnp.where(step < counts, 1.0, 0.0)
+        active = jnp.where(counts > float(step), 1.0, 0.0)
         alpha = (active * upper[0] / lower, active * upper[1] / lower)
         for m in range(step + 1):
             correction[m] = add(correction[m], mul(alpha, residual[m]))
@@ -404,8 +407,8 @@
     return straight + sign * pltpu.roll(turned, 4, 0)
 
 
-def update_kernel(sweep, gram_ref, fields_ref, basis_ref, friction_ref, shift_ref, harmonic_ref, counts_ref, *outs):
-    correction, residual = step_sizes(gram_ref, shift_ref[...], harmonic_ref, counts_ref, sweep)
+def update_kernel(sweep, gram_ref, fields_ref, basis_ref, friction_ref, slots_ref, *outs):
+    correction, residual = step_sizes(gram_ref, slots_ref, sweep)
     sign = jnp.where(iota((8, LANES), 0) < 4, -1.0, 1.0)
 
     def update(g, _):
@@ -462,7 +465,7 @@
     packed = call(
         pack_kernel,
         struct(RANKS, 7, 8, LANES),
-        [HBM] * 7 + [SMEM],
+        [HBM] * 8,
         (
             whole,
             whole,
@@ -471,9 +474,10 @@
             four,
             line,
             line,
+            pltpu.VMEM((4, RANKS), jnp.int32),
             pltpu.VMEM((RANKS, 1, 2048), jnp.float32),
             pltpu.VMEM((RANKS, 7, 8, LANES), jnp.float32),
-            pltpu.SemaphoreType.DMA((7,)),
+            pltpu.SemaphoreType.DMA((8,)),
             pltpu.SemaphoreType.DMA((3,)),
         ),
         58,
@@ -501,16 +505,16 @@
         terms = call(friction_kernel, struct(RANKS, 2, 8, LANES), [VMEM] * 4)(received, table, synthesis, analysis)
         return exchange(terms, "freq")
 
-    base, links, index, shift = call(
+    base, links, index, per_slot = call(
         start_kernel,
         [
             struct(RANKS, 3, 8, LANES),
             struct(RANKS, 16, 8, LANES),
             jax.ShapeDtypeStruct((RANKS, 2, 8, LANES), jnp.int32),
-            struct(8, LANES),
+            struct(2 + SWEEPS, 8, LANES),
         ],
-        [VMEM, VMEM, SMEM],
-    )(given, table, harmonic_of_slot)
+        [VMEM, VMEM, SMEM, SMEM],
+    )(given, table, harmonic_of_slot, counts)
     fields = given
     friction = friction_of(table)
     for sweep in range(SWEEPS):
@@ -525,8 +529,8 @@
             outs = [struct(RANKS, 3, 8, LANES), struct(RANKS, 3, 8, LANES)]
         else:
             outs = [struct(RANKS, 6, 8, LANES)]
-        results = call(functools.partial(update_kernel, sweep), outs, [VMEM] * 5 + [SMEM] * 2)(
-            gram, fields, basis, friction, shift, harmonic_of_slot, counts
+        results = call(functools.partial(update_kernel, sweep), outs, [VMEM] * 5)(
+            gram, fields, basis, friction, per_slot
         )
         if sweep < SWEEPS - 1:
             fields, base = results

time: 132 us -> 130 us (0.985)
  Pallas kernels: 18.5 us -> 16.7 us
where the time goes in v7:
time: 130 us
  blocking collectives  77.6 us (60%)
  waiting for transfers between devices  21.2 us (16%)
  Pallas kernels  16.7 us (13%)
  starting transfers between devices  13.5 us (10%)
    all_to_all x6, blocking collectives, exchange(): return lax.all_to_all(values, axis, split_axis=0, concat_axis=0, tiled=True)  77.6 us
    all_to_all x2, waiting for transfers between devices, exchange(): return lax.all_to_all(values, axis, split_axis=0, concat_axis=0, tiled=True)  21.2 us
    all_to_all x2, starting transfers between devices, exchange(): return lax.all_to_all(values, axis, split_axis=0, concat_axis=0, tiled=True)  13.5 us
    pallas_call x7, Pallas kernels, call(): result(*args)  11.9 us
    pallas_call x4, Pallas kernels, call(): result(*args)[0]  4.78 us
  transfers between devices with their start and end apart: 2, of which 2 were waited for; matrix products, arithmetic and copies ran while one was open for 0% of the time, Pallas kernels for 1%

profile of v7, /device:TPU:1, one launch (start us, length us, event | category | flops | bytes accessed | tf_op | source)
XLA Modules:
  0.0 129.9 jit_solution(6602434756733440738)
XLA Ops:
  0.6 0.0 copy-start.2
  0.6 0.0 copy-start
  0.7 2.9 %shard_map.122 = f32[16,7,8,128]{3,2,1,0:T(8,128)} custom-call(f32[384,128]{1,0:T(8,128)} %bitcast.27, f32[384,128]{1,0:T(8,128)} %bitcast.28, f32[4,2048]{1,0:T(4,128)} %weights_hbm.1, f32[4,2048]{1,0:T(4,128)} %east_hbm.1, f32[4,2048]{1,0:T(4,128)} %north_hbm.1, f32[1,2048]{1,0:T(1,128)} %bitcast.29, f32[1,2048]{1,0:T(1,128)} %bitcast.30, s32[4,16]{1,0:T(4,128)} %bitcast.31), custom_call_target="tpu_custom_call" | custom-call | tf_op jit(solution)/shard_map/pallas_call | solution.py:444
  3.5 10.0 %all-to-all-start = ((f32[16,7,8,128]{3,2,1,0:T(8,128)}), f32[16,7,8,128]{3,2,1,0:T(8,128)S(1)}, u32[]{:S(2)}, u32[]{:S(2)}) async-start(f32[16,7,8,128]{3,2,1,0:T(8,128)} %shard_map.122), calls=%async_computation | async-start | bytes 917504 | tf_op jit(solution)/shard_map/all_to_all | solution.py:448
  13.5 0.0 copy-done
  13.5 0.1 broadcast_in_dim.7
  13.6 0.1 reshape.45.harmonic_ref
  13.8 0.0 copy-done.2
  13.8 0.2 shard_map.123
  13.9 15.6 %all-to-all-done.given_ref.fields_ref = f32[16,7,8,128]{3,2,1,0:T(8,128)S(1)} async-done(((f32[16,7,8,128]{3,2,1,0:T(8,128)}), f32[16,7,8,128]{3,2,1,0:T(8,128)S(1)}, u32[]{:S(2)}, u32[]{:S(2)}) %all-to-all-start) | async-done | bytes 458784 | tf_op jit(solution)/shard_map/all_to_all | solution.py:448
  29.5 0.0 copy-start.1
  29.5 15.9 %all_to_all.40.table_ref.x_ref = f32[16,5,8,128]{3,2,1,0:T(8,128)S(1)} all-to-all(f32[16,5,8,128]{3,2,1,0:T(8,128)S(1)} %shard_map.124), channel_id=1, replica_groups=mesh['freq'=16,'node'=16] {'freq'}, dimensions={0} | all-to-all | bytes 655360 | tf_op jit(solution)/shard_map/all_to_all | solution.py:448
  45.5 1.3 shard_map.126
  46.7 3.5 %all-to-all-start.2 = ((f32[16,2,8,128]{3,2,1,0:T(8,128)}), f32[16,2,8,128]{3,2,1,0:T(8,128)S(1)}, u32[]{:S(2)}, u32[]{:S(2)}) async-start(f32[16,2,8,128]{3,2,1,0:T(8,128)} %shard_map.126), calls=%async_computation.2 | async-start | bytes 262144 | tf_op jit(solution)/shard_map/all_to_all | solution.py:448
  50.3 0.0 copy-done.1
  50.3 1.1 shard_map.125
  51.4 5.7 %all-to-all-done.2.friction_ref = f32[16,2,8,128]{3,2,1,0:T(8,128)S(1)} async-done(((f32[16,2,8,128]{3,2,1,0:T(8,128)}), f32[16,2,8,128]{3,2,1,0:T(8,128)S(1)}, u32[]{:S(2)}, u32[]{:S(2)}) %all-to-all-start.2) | async-done | bytes 131104 | tf_op jit(solution)/shard_map/all_to_all | solution.py:448
  57.1 3.8 %shard_map.127 = (f32[6,16,3,8,128]{4,3,2,1,0:T(8,128)S(1)}, f32[16,2,128]{2,1,0:T(2,128)S(1)}) custom-call(f32[16,3,8,128]{3,2,1,0:T(8,128)S(1)} %get-tuple-element.17.base_ref, f32[16,2,8,128]{3,2,1,0:T(8,128)S(1)} %all-to-all-done.2.friction_ref, f32[16,16,8,128]{3,2,1,0:T(8,128)S(1)} %get-tuple-element.19.links_ref, ...), custom_call_target="tpu_custom_call" | custom-call | tf_op jit(solution)/shard_map/pallas_call | solution.py:444
  60.9 11.7 %all_to_all.41.gram_ref = f32[16,2,128]{2,1,0:T(2,128)S(1)} all-to-all(f32[16,2,128]{2,1,0:T(2,128)S(1)} %get-tuple-element.21), channel_id=1, replica_groups=mesh['freq'=16,'node'=16] {'node'}, dimensions={0} | all-to-all | bytes 32768 | tf_op jit(solution)/shard_map/all_to_all | solution.py:448
  72.6 0.8 shard_map.128
  73.4 10.0 %all_to_all.42.x_ref = f32[16,3,8,128]{3,2,1,0:T(8,128)S(1)} all-to-all(f32[16,3,8,128]{3,2,1,0:T(8,128)S(1)} %get-tuple-element.25.fields_ref), channel_id=1, replica_groups=mesh['freq'=16,'node'=16] {'freq'}, dimensions={0} | all-to-all | bytes 393216 | tf_op jit(solution)/shard_map/all_to_all | solution.py:448
  83.4 0.6 shard_map.129
  84.0 9.8 %all_to_all.43.friction_ref = f32[16,2,8,128]{3,2,1,0:T(8,128)S(1)} all-to-all(f32[16,2,8,128]{3,2,1,0:T(8,128)S(1)} %shard_map.129), channel_id=1, replica_groups=mesh['freq'=16,'node'=16] {'freq'}, dimensions={0} | all-to-all | bytes 262144 | tf_op jit(solution)/shard_map/all_to_all | solution.py:448
  93.9 3.8 %shard_map.130 = (f32[6,16,3,8,128]{4,3,2,1,0:T(8,128)S(1)}, f32[16,2,128]{2,1,0:T(2,128)S(1)}) custom-call(f32[16,3,8,128]{3,2,1,0:T(8,128)S(1)} %get-tuple-element.24.base_ref, f32[16,2,8,128]{3,2,1,0:T(8,128)S(1)} %all_to_all.43.friction_ref, f32[16,16,8,128]{3,2,1,0:T(8,128)S(1)} %get-tuple-element.19.links_ref, ...), custom_call_target="tpu_custom_call" | custom-call | tf_op jit(solution)/shard_map/pallas_call | solution.py:444
  97.7 12.8 %all_to_all.44.gram_ref = f32[16,2,128]{2,1,0:T(2,128)S(1)} all-to-all(f32[16,2,128]{2,1,0:T(2,128)S(1)} %get-tuple-element.26), channel_id=1, replica_groups=mesh['freq'=16,'node'=16] {'node'}, dimensions={0} | all-to-all | bytes 32768 | tf_op jit(solution)/shard_map/all_to_all | solution.py:448
  110.5 0.8 shard_map.131
  111.3 17.4 %all_to_all.45.x_ref = f32[16,6,8,128]{3,2,1,0:T(8,128)S(1)} all-to-all(f32[16,6,8,128]{3,2,1,0:T(8,128)S(1)} %shard_map.131), channel_id=1, replica_groups=mesh['freq'=16,'node'=16] {'node'}, dimensions={0} | all-to-all | bytes 786432 | tf_op jit(solution)/shard_map/all_to_all | solution.py:448
  128.7 1.3 shard_map.132
  (2 shorter events, 0.0 us)
Async XLA Ops:
  0.6 13.1 %copy-start.2 = (f32[1,128]{1,0:T(1,128)S(1)}, f32[1,128]{1,0:T(1,128)}, u32[]{:S(2)}) copy-start(f32[1,128]{1,0:T(1,128)} %constant.2.clone.cosines_ref) | copy-start | bytes 1540
  0.6 12.9 %copy-start = (s32[64]{0:T(128)S(1)}, s32[64]{0:T(128)}, u32[]{:S(2)}) copy-start(s32[64]{0:T(128)} %harmonic_ref.1) | copy-start | bytes 772
  3.5 26.0 %all-to-all-start = ((f32[16,7,8,128]{3,2,1,0:T(8,128)}), f32[16,7,8,128]{3,2,1,0:T(8,128)S(1)}, u32[]{:S(2)}, u32[]{:S(2)}) async-start(f32[16,7,8,128]{3,2,1,0:T(8,128)} %shard_map.122), calls=%async_computation | async-start | bytes 917504 | tf_op jit(solution)/shard_map/all_to_all | solution.py:448
  29.5 20.7 %copy-start.1 = (s32[2,64]{1,0:T(2,128)S(1)}, s32[2,64]{1,0:T(2,128)}, u32[]{:S(2)}) copy-start(s32[2,64]{1,0:T(2,128)} %counts_ref.1) | copy-start | bytes 1540
  46.7 10.3 %all-to-all-start.2 = ((f32[16,2,8,128]{3,2,1,0:T(8,128)}), f32[16,2,8,128]{3,2,1,0:T(8,128)S(1)}, u32[]{:S(2)}, u32[]{:S(2)}) async-start(f32[16,2,8,128]{3,2,1,0:T(8,128)} %shard_map.126), calls=%async_computation.2 | async-start | bytes 262144 | tf_op jit(solution)/shard_map/all_to_all | solution.py:448

commit v8 on v7

--- a/solution.py
+++ b/solution.py
@@ -268,7 +268,7 @@
     return OMEGA_STEP * slot_rows(harmonic_ref, lambda ref, i: ref[i]).astype(jnp.float32)
 
 
-def start_kernel(given_ref, table_ref, harmonic_ref, counts_ref, base_ref, links_ref, index_ref, slots_ref):
+def start_kernel(given_ref, table_ref, harmonic_ref, counts_ref, _, base_ref, links_ref, index_ref, slots_ref):
     shift = given_ref[0, 6, 1:2]
     for g in range(1, RANKS):
         shift = shift + given_ref[g, 6, 1:2]
@@ -505,6 +505,7 @@
         terms = call(friction_kernel, struct(RANKS, 2, 8, LANES), [VMEM] * 4)(received, table, synthesis, analysis)
         return exchange(terms, "freq")
 
+    friction = friction_of(table)
     base, links, index, per_slot = call(
         start_kernel,
         [
@@ -513,10 +514,9 @@
             jax.ShapeDtypeStruct((RANKS, 2, 8, LANES), jnp.int32),
             struct(2 + SWEEPS, 8, LANES),
         ],
-        [VMEM, VMEM, SMEM, SMEM],
-    )(given, table, harmonic_of_slot, counts)
+        [VMEM, VMEM, SMEM, SMEM, VMEM],
+    )(given, table, harmonic_of_slot, counts, friction)
     fields = given
-    friction = friction_of(table)
     for sweep in range(SWEEPS):
         basis, gram = call(
             basis_kernel,

time: 130 us -> 130 us (level)
  blocking collectives: 77.6 us -> 87.3 us
  waiting for transfers between devices: 21.2 us -> 15.6 us
  starting transfers between devices: 13.5 us -> 9.99 us
    all_to_all x6 -> x7, blocking collectives: 77.6 us -> 87.3 us  [exchange(): return lax.all_to_all(values, axis, split_axis=0, concat_axis=0, tiled=True)]
    all_to_all x2 -> x1, waiting for transfers between devices: 21.2 us -> 15.6 us  [exchange(): return lax.all_to_all(values, axis, split_axis=0, concat_axis=0, tiled=True)]
    all_to_all x2 -> x1, starting transfers between devices: 13.5 us -> 9.99 us  [exchange(): return lax.all_to_all(values, axis, split_axis=0, concat_axis=0, tiled=True)]
  transfers between devices with their start and end apart: 2 -> 1, of which waited for: 2 -> 1; matrix products, arithmetic and copies ran while one was open for 0% -> 0% of each run, Pallas kernels for 1% -> 0%
where the time goes in v8:
time: 130 us
  blocking collectives  87.3 us (67%)
  Pallas kernels  15.9 us (12%)
  waiting for transfers between devices  15.6 us (12%)
  starting transfers between devices  9.99 us (8%)
    all_to_all x7, blocking collectives, exchange(): return lax.all_to_all(values, axis, split_axis=0, concat_axis=0, tiled=True)  87.3 us
    all_to_all x1, waiting for transfers between devices, exchange(): return lax.all_to_all(values, axis, split_axis=0, concat_axis=0, tiled=True)  15.6 us
    pallas_call x7, Pallas kernels, call(): result(*args)  11.8 us
    all_to_all x1, starting transfers between devices, exchange(): return lax.all_to_all(values, axis, split_axis=0, concat_axis=0, tiled=True)  9.99 us
    pallas_call x4, Pallas kernels, call(): result(*args)[0]  4.1 us
  transfers between devices with their start and end apart: 1, of which 1 were waited for; matrix products, arithmetic and copies ran while one was open for 0% of the time, Pallas kernels for 0%

profile of v8, /device:TPU:1, one launch (start us, length us, event | category | flops | bytes accessed | tf_op | source)
XLA Modules:
  0.0 129.7 jit_solution(8170109528058484170)
XLA Ops:
  0.6 0.0 copy-start.2
  0.6 0.0 copy-start
  0.7 2.9 %shard_map.122 = f32[16,7,8,128]{3,2,1,0:T(8,128)} custom-call(f32[384,128]{1,0:T(8,128)} %bitcast.27, f32[384,128]{1,0:T(8,128)} %bitcast.28, f32[4,2048]{1,0:T(4,128)} %weights_hbm.1, f32[4,2048]{1,0:T(4,128)} %east_hbm.1, f32[4,2048]{1,0:T(4,128)} %north_hbm.1, f32[1,2048]{1,0:T(1,128)} %bitcast.29, f32[1,2048]{1,0:T(1,128)} %bitcast.30, s32[4,16]{1,0:T(4,128)} %bitcast.31), custom_call_target="tpu_custom_call" | custom-call | tf_op jit(solution)/shard_map/pallas_call | solution.py:444
  3.5 10.0 %all-to-all-start = ((f32[16,7,8,128]{3,2,1,0:T(8,128)}), f32[16,7,8,128]{3,2,1,0:T(8,128)S(1)}, u32[]{:S(2)}, u32[]{:S(2)}) async-start(f32[16,7,8,128]{3,2,1,0:T(8,128)} %shard_map.122), calls=%async_computation | async-start | bytes 917504 | tf_op jit(solution)/shard_map/all_to_all | solution.py:448
  13.5 0.0 copy-done
  13.5 0.1 broadcast_in_dim.7
  13.6 0.1 reshape.45.harmonic_ref
  13.7 0.0 copy-done.2
  13.8 0.2 shard_map.123
  13.9 15.6 %all-to-all-done.given_ref.fields_ref = f32[16,7,8,128]{3,2,1,0:T(8,128)S(1)} async-done(((f32[16,7,8,128]{3,2,1,0:T(8,128)}), f32[16,7,8,128]{3,2,1,0:T(8,128)S(1)}, u32[]{:S(2)}, u32[]{:S(2)}) %all-to-all-start) | async-done | bytes 458784 | tf_op jit(solution)/shard_map/all_to_all | solution.py:448
  29.5 0.0 copy-start.1
  29.5 15.9 %all_to_all.40.x_ref.table_ref = f32[16,5,8,128]{3,2,1,0:T(8,128)S(1)} all-to-all(f32[16,5,8,128]{3,2,1,0:T(8,128)S(1)} %shard_map.124), channel_id=1, replica_groups=mesh['freq'=16,'node'=16] {'freq'}, dimensions={0} | all-to-all | bytes 655360 | tf_op jit(solution)/shard_map/all_to_all | solution.py:448
  45.5 0.6 shard_map.125
  46.1 9.5 %all_to_all.41._.friction_ref = f32[16,2,8,128]{3,2,1,0:T(8,128)S(1)} all-to-all(f32[16,2,8,128]{3,2,1,0:T(8,128)S(1)} %shard_map.125), channel_id=1, replica_groups=mesh['freq'=16,'node'=16] {'freq'}, dimensions={0} | all-to-all | bytes 262144 | tf_op jit(solution)/shard_map/all_to_all | solution.py:448
  55.6 0.0 copy-done.1
  55.6 1.1 shard_map.126
  56.7 3.8 %shard_map.127 = (f32[6,16,3,8,128]{4,3,2,1,0:T(8,128)S(1)}, f32[16,2,128]{2,1,0:T(2,128)S(1)}) custom-call(f32[16,3,8,128]{3,2,1,0:T(8,128)S(1)} %get-tuple-element.18.base_ref, f32[16,2,8,128]{3,2,1,0:T(8,128)S(1)} %all_to_all.41._.friction_ref, f32[16,16,8,128]{3,2,1,0:T(8,128)S(1)} %get-tuple-element.19.links_ref, ...), custom_call_target="tpu_custom_call" | custom-call | tf_op jit(solution)/shard_map/pallas_call | solution.py:444
  60.5 11.9 %all_to_all.42.gram_ref = f32[16,2,128]{2,1,0:T(2,128)S(1)} all-to-all(f32[16,2,128]{2,1,0:T(2,128)S(1)} %get-tuple-element.21), channel_id=1, replica_groups=mesh['freq'=16,'node'=16] {'node'}, dimensions={0} | all-to-all | bytes 32768 | tf_op jit(solution)/shard_map/all_to_all | solution.py:448
  72.4 0.8 shard_map.128
  73.2 10.0 %all_to_all.43.x_ref = f32[16,3,8,128]{3,2,1,0:T(8,128)S(1)} all-to-all(f32[16,3,8,128]{3,2,1,0:T(8,128)S(1)} %get-tuple-element.25.fields_ref), channel_id=1, replica_groups=mesh['freq'=16,'node'=16] {'freq'}, dimensions={0} | all-to-all | bytes 393216 | tf_op jit(solution)/shard_map/all_to_all | solution.py:448
  83.2 0.6 shard_map.129
  83.8 9.8 %all_to_all.44.friction_ref = f32[16,2,8,128]{3,2,1,0:T(8,128)S(1)} all-to-all(f32[16,2,8,128]{3,2,1,0:T(8,128)S(1)} %shard_map.129), channel_id=1, replica_groups=mesh['freq'=16,'node'=16] {'freq'}, dimensions={0} | all-to-all | bytes 262144 | tf_op jit(solution)/shard_map/all_to_all | solution.py:448
  93.7 3.8 %shard_map.130 = (f32[6,16,3,8,128]{4,3,2,1,0:T(8,128)S(1)}, f32[16,2,128]{2,1,0:T(2,128)S(1)}) custom-call(f32[16,3,8,128]{3,2,1,0:T(8,128)S(1)} %get-tuple-element.24.base_ref, f32[16,2,8,128]{3,2,1,0:T(8,128)S(1)} %all_to_all.44.friction_ref, f32[16,16,8,128]{3,2,1,0:T(8,128)S(1)} %get-tuple-element.19.links_ref, ...), custom_call_target="tpu_custom_call" | custom-call | tf_op jit(solution)/shard_map/pallas_call | solution.py:444
  97.5 12.8 %all_to_all.45.gram_ref = f32[16,2,128]{2,1,0:T(2,128)S(1)} all-to-all(f32[16,2,128]{2,1,0:T(2,128)S(1)} %get-tuple-element.26), channel_id=1, replica_groups=mesh['freq'=16,'node'=16] {'node'}, dimensions={0} | all-to-all | bytes 32768 | tf_op jit(solution)/shard_map/all_to_all | solution.py:448
  110.2 0.8 shard_map.131
  111.1 17.4 %all_to_all.46.x_ref = f32[16,6,8,128]{3,2,1,0:T(8,128)S(1)} all-to-all(f32[16,6,8,128]{3,2,1,0:T(8,128)S(1)} %shard_map.131), channel_id=1, replica_groups=mesh['freq'=16,'node'=16] {'node'}, dimensions={0} | all-to-all | bytes 786432 | tf_op jit(solution)/shard_map/all_to_all | solution.py:448
  128.5 1.3 shard_map.132
  (2 shorter events, 0.0 us)
Async XLA Ops:
  0.6 13.1 %copy-start.2 = (f32[1,128]{1,0:T(1,128)S(1)}, f32[1,128]{1,0:T(1,128)}, u32[]{:S(2)}) copy-start(f32[1,128]{1,0:T(1,128)} %constant.2.clone.cosines_ref) | copy-start | bytes 1540
  0.6 12.9 %copy-start = (s32[64]{0:T(128)S(1)}, s32[64]{0:T(128)}, u32[]{:S(2)}) copy-start(s32[64]{0:T(128)} %harmonic_ref.1) | copy-start | bytes 772
  3.5 26.0 %all-to-all-start = ((f32[16,7,8,128]{3,2,1,0:T(8,128)}), f32[16,7,8,128]{3,2,1,0:T(8,128)S(1)}, u32[]{:S(2)}, u32[]{:S(2)}) async-start(f32[16,7,8,128]{3,2,1,0:T(8,128)} %shard_map.122), calls=%async_computation | async-start | bytes 917504 | tf_op jit(solution)/shard_map/all_to_all | solution.py:448
  29.5 26.1 %copy-start.1 = (s32[2,64]{1,0:T(2,128)S(1)}, s32[2,64]{1,0:T(2,128)}, u32[]{:S(2)}) copy-start(s32[2,64]{1,0:T(2,128)} %counts_ref.1) | copy-start | bytes 1540
